TPU v7x, 128 devices: a whole 4x4x4 slice. The times are simulated.
128 devices in a mesh: dp: 8 (over x, core), expert: 16 (over z, y).
Axes of the slice: x: 4, y: 4, z: 4, core: 2. Of those that a mesh axis runs over, the one named last changes fastest.
Arguments:
- x_saved: bfloat16 [8, 32, 1280, 1024], P('dp', 'expert'), may hold values from -6 to 6
- d_out: bfloat16 [32768, 1024], P(('dp', 'expert')), may hold values from -6 to 6
- routes: int32 [32768, 8], P(('dp', 'expert')), may hold values from 0 to 31, all different within a row; in each aligned block of 256 rows (0 to 255, 256 to 511, ...) at most 80 rows name the same one
- probs: float32 [32768, 8], P(('dp', 'expert')), may hold values from 0.1 to 0.9
- w_gate: bfloat16 [32, 1024, 512], P('expert'), may hold values from -0.1875 to 0.1875
- w_up: bfloat16 [32, 1024, 512], P('expert'), may hold values from -0.1875 to 0.1875
- w_down: bfloat16 [32, 512, 1024], P('expert'), may hold values from -0.25 to 0.25
- res_gate: bfloat16 [8, 32, 1024, 512], P('dp', 'expert'), may hold values from -6 to 6
- res_up: bfloat16 [8, 32, 1024, 512], P('dp', 'expert'), may hold values from -6 to 6
- res_down: bfloat16 [8, 32, 512, 1024], P('dp', 'expert'), may hold values from -1.5 to 1.5
Outputs:
- d_tokens: bfloat16 [32768, 1024], P(('dp', 'expert'))
- grad_gate: float32 [32, 1024, 512], P('expert', 'dp')
- grad_up: float32 [32, 1024, 512], P('expert', 'dp')
- grad_down: float32 [32, 512, 1024], P('expert', None, 'dp')
- new_res_gate: bfloat16 [8, 32, 1024, 512], P('dp', 'expert')
- new_res_up: bfloat16 [8, 32, 1024, 512], P('dp', 'expert')
- new_res_down: bfloat16 [8, 32, 512, 1024], P('dp', 'expert')
Inputs may be any that keep to these rules, and one draw needn't show every extreme that they name: `routes`: the 8 entries of a row differ. In the rows of one device (aligned blocks of 256 rows) each expert is named by at most 80 rows, a bound that some block reaches.
All inputs are finite; a program needn't handle non-finite values. Where the computation divides by a largest or mean magnitude, that divisor is 1e-20 or more.
Results may differ from a plain program's by a relative error of at most 0.007.
Values may be sent and summed in bfloat16 or wider, within the bound.
No kernel may reach another device: no remote copies, remote signals or barrier semaphores. Data moves between devices by JAX's collectives and lax.ppermute only.
A program may use at most 192 MiB of HBM per device.

v0:
```python
import jax
import jax.numpy as jnp
from jax import lax
from jax.sharding import PartitionSpec as P

EXPERTS = 32


loss_unscale = 0.0625
epsilon = 1e-05


def gate_terms(gate_pre):
    logistic = jax.nn.sigmoid(gate_pre)
    return (gate_pre * logistic, logistic * (1.0 + gate_pre * (1.0 - logistic)))


def over_rows(left, right):
    return lax.dot_general(
        left, right, (((0,), (0,)), ((), ())), preferred_element_type=jnp.float32
    )


def over_columns(left, right):
    return lax.dot_general(
        left, right, (((1,), (1,)), ((), ())), preferred_element_type=jnp.float32
    )


def rows_backward(saved_rows, cotangent_in, gate_weight, up_weight, down_weight):
    gate_pre = jnp.dot(saved_rows, gate_weight, preferred_element_type=jnp.float32)
    up_pre = jnp.dot(saved_rows, up_weight, preferred_element_type=jnp.float32)
    gate_act, gate_slope = gate_terms(gate_pre)
    hidden = (gate_act * up_pre).astype(jnp.bfloat16)
    grad_hidden = over_columns(cotangent_in, down_weight)
    grad_a = (grad_hidden * up_pre * gate_slope).astype(jnp.bfloat16)
    grad_b = (grad_hidden * gate_act).astype(jnp.bfloat16)
    grad_gate = loss_unscale * over_rows(saved_rows, grad_a)
    grad_up = loss_unscale * over_rows(saved_rows, grad_b)
    grad_down = loss_unscale * over_rows(hidden, cotangent_in)
    return (grad_a, grad_b, grad_gate, grad_up, grad_down)


def project_rows(grad_a, grad_b, gate_weight, up_weight):
    return (over_columns(grad_a, gate_weight) + over_columns(grad_b, up_weight)).astype(
        jnp.bfloat16
    )


def compress(local_grad, residual):
    carried = local_grad + residual.astype(jnp.float32)
    magnitude = jnp.mean(jnp.abs(carried), axis=-1, keepdims=True) + epsilon
    compressed = (magnitude * jnp.tanh(carried / magnitude)).astype(jnp.bfloat16)
    kept = lax.optimization_barrier(compressed)
    leftover = (carried - kept.astype(jnp.float32)).astype(jnp.bfloat16)
    return (compressed, leftover)


def shard_backward(saved_rows, cotangent_in, gate_weight, up_weight, down_weight):
    grad_a, grad_b, grad_gate, grad_up, grad_down = rows_backward(
        saved_rows, cotangent_in, gate_weight, up_weight, down_weight
    )
    row_grads = project_rows(grad_a, grad_b, gate_weight, up_weight)
    return (grad_gate, grad_up, grad_down, row_grads)


def on_device(x_saved, d_out, routes, probs, w_gate, w_up, w_down, res_gate, res_up, res_down):
    expert_count = lax.axis_size("expert")
    replica_count = lax.axis_size("dp")
    group_size = max(1, expert_count // EXPERTS)
    per_dev = max(1, EXPERTS // expert_count)
    virtual = per_dev * expert_count
    slot_count = x_saved.shape[2]
    model_width = x_saved.shape[3]
    capacity = slot_count // expert_count
    route_top = routes.shape[1]
    route_flat = routes.reshape(-1)
    route_total = route_flat.shape[0]
    labels = jnp.arange(EXPERTS, dtype=jnp.int32)
    onehot = (route_flat[:, None] == labels[None, :]).astype(jnp.int32)
    before = jnp.cumsum(onehot, axis=0) - onehot
    route_rank = jnp.sum(before * onehot, axis=1)
    shard_ids = jnp.arange(group_size, dtype=jnp.int32)
    target = (
        (route_flat[:, None] * group_size + shard_ids[None, :]) * capacity + route_rank[:, None]
    ).reshape(-1)
    route_ids = jnp.arange(route_total, dtype=jnp.int32)[:, None].reshape(-1)
    slot_owner = jnp.full((virtual * capacity,), -1, jnp.int32).at[target].set(route_ids)
    filled = slot_owner >= 0
    owner_safe = jnp.maximum(slot_owner, 0)
    weights_sent = jnp.where(filled, probs.reshape(-1)[owner_safe], 0.0)
    rows_sent = (weights_sent[:, None] * d_out[owner_safe // route_top].astype(jnp.float32)).astype(
        jnp.bfloat16
    )
    expert_loads = jnp.sum(onehot, axis=0)
    counts_sent = (
        jnp.repeat(expert_loads, group_size).astype(jnp.bfloat16).reshape(expert_count, per_dev)
    )
    arrived, arrived_counts = (
        lax.all_to_all(
            rows_sent.reshape(expert_count, per_dev * capacity, model_width),
            "expert",
            split_axis=0,
            concat_axis=0,
            tiled=True,
        ),
        lax.all_to_all(counts_sent, "expert", split_axis=0, concat_axis=0, tiled=True),
    )
    arrived = arrived.reshape(expert_count, per_dev, capacity, model_width)
    results = []
    for local_index in range(per_dev):
        cotangent_in = arrived[:, local_index].reshape(slot_count, model_width)
        results.append(
            shard_backward(
                x_saved[0, local_index],
                cotangent_in,
                w_gate[local_index],
                w_up[local_index],
                w_down[local_index],
            )
        )
    grad_gate = jnp.stack([item[0] for item in results])
    grad_up = jnp.stack([item[1] for item in results])
    grad_down = jnp.stack([item[2] for item in results])
    row_grads = jnp.stack([item[3] for item in results])
    outgoing = row_grads.reshape(per_dev, expert_count, capacity, model_width).transpose(1, 0, 2, 3)
    returned = lax.all_to_all(
        outgoing.reshape(expert_count, per_dev * capacity, model_width),
        "expert",
        split_axis=0,
        concat_axis=0,
        tiled=True,
    )
    route_rows = returned.reshape(virtual * capacity, model_width)
    picked = (
        route_rows[target]
        .astype(jnp.float32)
        .reshape(route_total // route_top, route_top * group_size, model_width)
    )
    d_tokens = jnp.sum(picked, axis=1).astype(jnp.bfloat16)
    sent_gate, left_gate = compress(grad_gate, res_gate[0])
    sent_up, left_up = compress(grad_up, res_up[0])
    sent_down, left_down = compress(grad_down, res_down[0])
    width_block = model_width // replica_count
    hidden_units = w_gate.shape[2]
    gate_blocks = sent_gate.reshape(per_dev, replica_count, width_block, hidden_units)
    up_blocks = sent_up.reshape(per_dev, replica_count, width_block, hidden_units)
    down_blocks = sent_down.reshape(per_dev, hidden_units, replica_count, width_block).transpose(
        0, 2, 1, 3
    )
    received = (
        lax.all_to_all(gate_blocks, "dp", split_axis=1, concat_axis=1, tiled=True),
        lax.all_to_all(up_blocks, "dp", split_axis=1, concat_axis=1, tiled=True),
        lax.all_to_all(down_blocks, "dp", split_axis=1, concat_axis=1, tiled=True),
    )
    total_gate = jnp.sum(received[0].astype(jnp.float32), axis=1)
    total_up = jnp.sum(received[1].astype(jnp.float32), axis=1)
    total_down = jnp.sum(received[2].astype(jnp.float32), axis=1)
    return (
        d_tokens,
        total_gate / replica_count,
        total_up / replica_count,
        total_down / replica_count,
        left_gate[None],
        left_up[None],
        left_down[None],
    )


def solution(mesh):
    in_specs = (
        P("dp", "expert", None, None),
        P(("dp", "expert"), None),
        P(("dp", "expert"), None),
        P(("dp", "expert"), None),
        P("expert", None, None),
        P("expert", None, None),
        P("expert", None, None),
        P("dp", "expert", None, None),
        P("dp", "expert", None, None),
        P("dp", "expert", None, None),
    )
    out_specs = (
        P(("dp", "expert"), None),
        P("expert", "dp", None),
        P("expert", "dp", None),
        P("expert", None, "dp"),
        P("dp", "expert", None, None),
        P("dp", "expert", None, None),
        P("dp", "expert", None, None),
    )
    return jax.shard_map(
        on_device, mesh=mesh, in_specs=in_specs, out_specs=out_specs, check_vma=False
    )
```

profile of v0, /device:TPU:0, one launch (start us, length us, event | category | flops | bytes accessed | tf_op | source)
XLA Modules:
  0.0 357.5 jit_solution(13988325192744461253)
XLA Ops:
  2.5 9.1 %reduce-window.6 = s32[32,16,128]{2,1,0:T(8,128)S(1)} reduce-window(s32[32,16,128]{2,1,0:T(8,128)S(1)} %fusion.74, s32[]{:T(128)} %constant.45.clone.1), window={size=1x1x128 pad=0_0x0_0x127_0}, to_apply=%region_0.0 | reduce-window | flops 8323072 | bytes 524292 | tf_op jit(solution)/shard_map/reduce-window
  12.7 8.1 %scatter_custom_fusion = s32[2560]{0:T(1024)S(1)} fusion(s32[2048]{0:T(1024)S(1)} %bitcast.245, s32[2048]{0:T(1024)S(1)} %iota.11, s32[]{:T(128)} %constant.22.clone.1), kind=kCustom, calls=%fused_computation.139 | custom fusion | bytes 10244 | tf_op jit(solution)/shard_map/scatter | solution.py:88
  21.1 13.6 %gather_fusion = f32[2560]{0:T(1024)S(1)} fusion(f32[2048]{0:T(1024)S(1)} %reshape.162, s32[3072]{0:T(1024)S(1)} %get-tuple-element.53), kind=kCustom, calls=%fused_computation | custom fusion | bytes 30720 | tf_op jit(solution)/shard_map/gather | solution.py:91
  34.8 8.9 %gather_fusion.1 = bf16[2560,1024]{1,0:T(8,128)(2,1)} fusion(bf16[256,1024]{1,0:T(8,128)(2,1)S(1)} %copy-done, s32[3072]{0:T(1024)S(1)} %get-tuple-element.52), kind=kCustom, calls=%fused_computation.1 | custom fusion | bytes 10496000 | tf_op jit(solution)/shard_map/gather | solution.py:92
  43.7 5.7 %fusion = bf16[16,160,1024]{2,1,0:T(8,128)(2,1)} fusion(bf16[16,160,1024]{2,1,0:T(8,128)(2,1)} %bitcast.216, f32[16,160]{1,0:T(8,128)S(1)} %mul.148), kind=kLoop, calls=%fused_computation.5 | loop fusion | flops 7864320 | bytes 10496000 | tf_op jit(solution)/shard_map/convert_element_type | solution.py:92
  49.4 8.3 %all-to-all-start = ((bf16[16,160,1024]{2,1,0:T(8,128)(2,1)}), bf16[16,160,1024]{2,1,0:T(8,128)(2,1)}, u32[]{:S(2)}, u32[]{:S(2)}) async-start(bf16[16,160,1024]{2,1,0:T(8,128)(2,1)} %fusion), calls=%async_computation | async-start | bytes 10485760 | tf_op jit(solution)/shard_map/all_to_all | solution.py:100
  60.1 3.2 copy.41
  63.3 4.4 %copy.72 = f32[128,8,8,128]{3,2,1,0:T(8,128)} copy(bf16[128,8,8,128]{3,1,2,0:T(8,128)(2,1)} %bitcast.215) | data formatting | bytes 6291456
  71.6 3.2 copy.66
  78.9 3.1 fusion.17
  88.0 47.9 %all-to-all-done = bf16[16,160,1024]{2,1,0:T(8,128)(2,1)} async-done(((bf16[16,160,1024]{2,1,0:T(8,128)(2,1)}), bf16[16,160,1024]{2,1,0:T(8,128)(2,1)}, u32[]{:S(2)}, u32[]{:S(2)}) %all-to-all-start) | async-done | bytes 5242912 | tf_op jit(solution)/shard_map/all_to_all | solution.py:100
  135.9 3.3 fusion.82
  141.7 4.0 %multiply_convert_fusion.7 = (bf16[1280,512]{1,0:T(8,128)(2,1)}, bf16[1280,512]{1,0:T(8,128)(2,1)}) fusion(f32[1280,512]{1,0:T(8,128)S(1)} %copy-done.34, f32[1280,512]{1,0:T(8,128)S(1)} %copy-done.35, bf16[1280,1024]{1,0:T(8,128)(2,1)S(1)} %bitcast.240, bf16[2,512,1024]{2,1,0:T(8,128)(2,1)S(1)} %copy-done.29), kind=kOutput, calls=%fused_computation.62 | convolution fusion | flops 1350696960 | bytes 11534336 | tf_op jit(solution)/shard_map/dot_general | solution.py:25
  147.6 4.0 %multiply_convert_fusion.5 = (bf16[1280,512]{1,0:T(8,128)(2,1)}, bf16[1280,512]{1,0:T(8,128)(2,1)}) fusion(f32[1280,512]{1,0:T(8,128)S(1)} %copy-done.32, f32[1280,512]{1,0:T(8,128)S(1)} %copy-done.33, bf16[1280,1024]{1,0:T(8,128)(2,1)S(1)} %bitcast.238, bf16[2,512,1024]{2,1,0:T(8,128)(2,1)S(1)} %copy-done.29), kind=kOutput, calls=%fused_computation.58 | convolution fusion | flops 1350696960 | bytes 11534336 | tf_op jit(solution)/shard_map/dot_general | solution.py:25
  157.9 4.8 %all-to-all-start.4 = ((bf16[2,8,512,128]{3,2,0,1:T(8,128)(2,1)}), bf16[2,8,512,128]{3,2,0,1:T(8,128)(2,1)}, u32[]{:S(2)}, u32[]{:S(2)}) async-start(bf16[2,8,512,128]{3,2,0,1:T(8,128)(2,1)} %fusion.34), calls=%async_computation.4 | async-start | bytes 4194304 | tf_op jit(solution)/shard_map/all_to_all | solution.py:154
  162.7 3.8 %multiply_bitcast_fusion.6 = (f32[1,1024,512]{1,2,0:T(8,128)S(1)}, f32[64,8,8,128]{3,1,2,0:T(8,128)S(1)}) fusion(bf16[1280,512]{1,0:T(8,128)(2,1)} %get-tuple-element.28, bf16[1,2,1280,1024]{3,2,1,0:T(8,128)(2,1)} %param.10), kind=kOutput, calls=%fused_computation.76 | convolution fusion | flops 1342701568 | bytes 8126464 | tf_op jit(solution)/shard_map/dot_general | solution.py:19
  177.4 12.6 %all-to-all-done.4 = bf16[2,8,512,128]{3,2,0,1:T(8,128)(2,1)} async-done(((bf16[2,8,512,128]{3,2,0,1:T(8,128)(2,1)}), bf16[2,8,512,128]{3,2,0,1:T(8,128)(2,1)}, u32[]{:S(2)}, u32[]{:S(2)}) %all-to-all-start.4) | async-done | bytes 2097184 | tf_op jit(solution)/shard_map/all_to_all | solution.py:154
  189.9 4.4 %all-to-all-start.3 = ((bf16[2,8,128,512]{2,3,0,1:T(8,128)(2,1)}), bf16[2,8,128,512]{2,3,0,1:T(8,128)(2,1)}, u32[]{:S(2)}, u32[]{:S(2)}) async-start(bf16[2,8,128,512]{2,3,0,1:T(8,128)(2,1)} %fusion.11), calls=%async_computation.3 | async-start | bytes 4194304 | tf_op jit(solution)/shard_map/all_to_all | solution.py:153
  194.3 3.8 %multiply_bitcast_fusion.10 = (f32[1,1024,512]{1,2,0:T(8,128)S(1)}, f32[64,8,8,128]{3,1,2,0:T(8,128)S(1)}) fusion(bf16[1280,512]{1,0:T(8,128)(2,1)} %get-tuple-element.29, bf16[1,2,1280,1024]{3,2,1,0:T(8,128)(2,1)} %param.10), kind=kOutput, calls=%fused_computation.80 | convolution fusion | flops 1342701568 | bytes 8126464 | tf_op jit(solution)/shard_map/dot_general | solution.py:19
  208.0 13.5 %all-to-all-done.3 = bf16[2,8,128,512]{2,3,0,1:T(8,128)(2,1)} async-done(((bf16[2,8,128,512]{2,3,0,1:T(8,128)(2,1)}), bf16[2,8,128,512]{2,3,0,1:T(8,128)(2,1)}, u32[]{:S(2)}, u32[]{:S(2)}) %all-to-all-start.3) | async-done | bytes 2097184 | tf_op jit(solution)/shard_map/all_to_all | solution.py:153
  221.5 4.5 %all-to-all-start.2 = ((bf16[2,8,128,512]{2,3,0,1:T(8,128)(2,1)}), bf16[2,8,128,512]{2,3,0,1:T(8,128)(2,1)}, u32[]{:S(2)}, u32[]{:S(2)}) async-start(bf16[2,8,128,512]{2,3,0,1:T(8,128)(2,1)} %fusion.12), calls=%async_computation.2 | async-start | bytes 4194304 | tf_op jit(solution)/shard_map/all_to_all | solution.py:152
  226.1 3.3 fusion.52
  237.4 15.8 %all-to-all-done.2 = bf16[2,8,128,512]{2,3,0,1:T(8,128)(2,1)} async-done(((bf16[2,8,128,512]{2,3,0,1:T(8,128)(2,1)}), bf16[2,8,128,512]{2,3,0,1:T(8,128)(2,1)}, u32[]{:S(2)}, u32[]{:S(2)}) %all-to-all-start.2) | async-done | bytes 2097184 | tf_op jit(solution)/shard_map/all_to_all | solution.py:152
  253.3 5.3 %all-to-all-start.1 = ((bf16[16,160,1024]{2,1,0:T(8,128)(2,1)}), bf16[16,160,1024]{2,1,0:T(8,128)(2,1)}, u32[]{:S(2)}, u32[]{:S(2)}) async-start(bf16[16,160,1024]{2,1,0:T(8,128)(2,1)} %bitcast.223), calls=%async_computation.1 | async-start | bytes 10485760 | tf_op jit(solution)/shard_map/all_to_all | solution.py:127
  258.7 4.4 %multiply_convert_fusion = bf16[2,512,1024]{2,1,0:T(8,128)(2,1)} fusion(f32[2,512]{1,0:T(2,128)S(1)} %multiply_add_fusion.2, bf16[1,2,512,1024]{3,2,1,0:T(8,128)(2,1)} %param.19, f32[1,512,1024]{2,1,0:T(8,128)} %copy-done.16, f32[1,512,1024]{2,1,0:T(8,128)} %copy-done.15), kind=kLoop, calls=%fused_computation.26 | loop fusion | flops 6291456 | bytes 8392704 | tf_op jit(solution)/shard_map/convert_element_type | solution.py:53
  267.6 3.9 %copy.59 = bf16[1,2,1024,512]{3,2,1,0:T(8,128)(2,1)} copy(bf16[1,2,1024,512]{2,3,1,0:T(8,128)(2,1)} %fusion.32) | data formatting | bytes 4194304
  271.6 3.2 multiply_convert_fusion.2
  277.6 4.1 %copy.58 = bf16[1,2,1024,512]{3,2,1,0:T(8,128)(2,1)} copy(bf16[1,2,1024,512]{2,3,1,0:T(8,128)(2,1)} %fusion.31) | data formatting | bytes 4194304
  281.7 5.3 %fusion.33 = bf16[1,2,512,1024]{3,2,1,0:T(8,128)(2,1)} fusion(bf16[2,512,1024]{2,1,0:T(8,128)(2,1)} %multiply_convert_fusion, bf16[1,2,512,1024]{3,2,1,0:T(8,128)(2,1)S(1)} %copy-done.14, f32[1,512,1024]{2,1,0:T(8,128)} %copy-done.16, f32[1,512,1024]{2,1,0:T(8,128)} %copy-done.15), kind=kLoop, calls=%fused_computation.68 | loop fusion | flops 6291456 | bytes 10485760 | tf_op jit(solution)/shard_map/broadcast_in_dim | solution.py:166
  295.7 40.9 %all-to-all-done.1 = bf16[16,160,1024]{2,1,0:T(8,128)(2,1)} async-done(((bf16[16,160,1024]{2,1,0:T(8,128)(2,1)}), bf16[16,160,1024]{2,1,0:T(8,128)(2,1)}, u32[]{:S(2)}, u32[]{:S(2)}) %all-to-all-start.1) | async-done | bytes 5242912 | tf_op jit(solution)/shard_map/all_to_all | solution.py:127
  336.6 14.4 %gather_fusion.2 = bf16[2048,1024]{1,0:T(8,128)(2,1)} fusion(bf16[2560,1024]{1,0:T(8,128)(2,1)} %bitcast.23, s32[2048]{0:T(1024)S(1)} %broadcast_clamp_fusion), kind=kCustom, calls=%fused_computation.2 | custom fusion | bytes 8396800 | tf_op jit(solution)/shard_map/gather | solution.py:136
  351.0 6.3 %bitcast_reduce_fusion = bf16[256,1024]{1,0:T(8,128)(2,1)} fusion(bf16[2048,1024]{1,0:T(8,128)(2,1)} %gather_fusion.2), kind=kLoop, calls=%fused_computation.24 | loop fusion | flops 1835008 | bytes 4718592 | tf_op jit(solution)/shard_map/reduce_sum | solution.py:140
  (155 shorter events, 74.4 us)
Async XLA Ops:
  0.6 34.1 %copy-start = (bf16[256,1024]{1,0:T(8,128)(2,1)S(1)}, bf16[256,1024]{1,0:T(8,128)(2,1)}, u32[]{:S(2)}) copy-start(bf16[256,1024]{1,0:T(8,128)(2,1)} %param.11) | copy-start | bytes 1572868
  0.6 20.1 %copy-start.28 = (f32[256,8]{0,1:T(8,128)S(1)}, f32[256,8]{0,1:T(8,128)}, u32[]{:S(2)}) copy-start(f32[256,8]{0,1:T(8,128)} %param.13) | copy-start | bytes 24580
  49.4 8.3 %copy-start.25 = (bf16[1,2,1024,512]{3,2,1,0:T(8,128)(2,1)S(1)}, bf16[1,2,1024,512]{3,2,1,0:T(8,128)(2,1)}, u32[]{:S(2)}) copy-start(bf16[1,2,1024,512]{3,2,1,0:T(8,128)(2,1)} %param.18) | copy-start | bytes 6291460
  49.4 86.5 %all-to-all-start = ((bf16[16,160,1024]{2,1,0:T(8,128)(2,1)}), bf16[16,160,1024]{2,1,0:T(8,128)(2,1)}, u32[]{:S(2)}, u32[]{:S(2)}) async-start(bf16[16,160,1024]{2,1,0:T(8,128)(2,1)} %fusion), calls=%async_computation | async-start | bytes 10485760 | tf_op jit(solution)/shard_map/all_to_all | solution.py:100
  63.2 4.4 %copy-start.2 = (bf16[1,2,1024,512]{2,3,1,0:T(8,128)(2,1)S(1)}, bf16[1,2,1024,512]{2,3,1,0:T(8,128)(2,1)}, u32[]{:S(2)}) copy-start(bf16[1,2,1024,512]{2,3,1,0:T(8,128)(2,1)} %copy.47) | copy-start | bytes 6291460
  71.1 3.7 %slice-start = ((s8[5242880]{0:T(1024)(128)(4,1)}), s8[4194304]{0:T(1024)(128)(4,1)S(1)}, s32[]{:S(2)}) async-start(s8[5242880]{0:T(1024)(128)(4,1)} %bitcast.217), calls=%async_computation.5 | async-start | bytes 8388608
  71.5 3.2 slice-start.1
  71.5 4.3 %copy-start.30 = (bf16[2,1024,512]{2,1,0:T(8,128)(2,1)S(1)}, bf16[2,1024,512]{2,1,0:T(8,128)(2,1)}, u32[]{:S(2)}) copy-start(bf16[2,1024,512]{2,1,0:T(8,128)(2,1)} %param.14) | copy-start | bytes 6291460
  135.9 3.4 copy-start.34
  135.9 4.1 %copy-start.35 = (f32[1280,512]{1,0:T(8,128)S(1)}, f32[1280,512]{1,0:T(8,128)}, u32[]{:S(2)}) copy-start(f32[1280,512]{1,0:T(8,128)} %fusion.27) | copy-start | bytes 7864324
  141.7 10.0 %copy-start.15 = (f32[1,512,1024]{2,1,0:T(8,128)}, f32[1,512,1024]{2,1,0:T(8,128)S(1)}, u32[]{:S(2)}) copy-start(f32[1,512,1024]{2,1,0:T(8,128)S(1)} %get-tuple-element.34) | copy-start | bytes 6291460
  141.7 4.2 %copy-start.32 = (f32[1280,512]{1,0:T(8,128)S(1)}, f32[1280,512]{1,0:T(8,128)}, u32[]{:S(2)}) copy-start(f32[1280,512]{1,0:T(8,128)} %fusion.17) | copy-start | bytes 7864324
  141.7 4.2 %copy-start.33 = (f32[1280,512]{1,0:T(8,128)S(1)}, f32[1280,512]{1,0:T(8,128)}, u32[]{:S(2)}) copy-start(f32[1280,512]{1,0:T(8,128)} %fusion.19) | copy-start | bytes 7864324
  147.6 4.1 %copy-start.16 = (f32[1,512,1024]{2,1,0:T(8,128)}, f32[1,512,1024]{2,1,0:T(8,128)S(1)}, u32[]{:S(2)}) copy-start(f32[1,512,1024]{2,1,0:T(8,128)S(1)} %get-tuple-element.36) | copy-start | bytes 6291460
  147.6 4.1 %copy-start.13 = (bf16[1,2,512,1024]{3,2,1,0:T(8,128)(2,1)S(1)}, bf16[1,2,512,1024]{3,2,1,0:T(8,128)(2,1)}, u32[]{:S(2)}) copy-start(bf16[1,2,512,1024]{3,2,1,0:T(8,128)(2,1)} %param.19) | copy-start | bytes 6291460
  157.9 32.0 %all-to-all-start.4 = ((bf16[2,8,512,128]{3,2,0,1:T(8,128)(2,1)}), bf16[2,8,512,128]{3,2,0,1:T(8,128)(2,1)}, u32[]{:S(2)}, u32[]{:S(2)}) async-start(bf16[2,8,512,128]{3,2,0,1:T(8,128)(2,1)} %fusion.34), calls=%async_computation.4 | async-start | bytes 4194304 | tf_op jit(solution)/shard_map/all_to_all | solution.py:154
  162.7 4.8 %slice-start.2 = ((s8[5242880]{0:T(1024)(128)(4,1)}), s8[4194304]{0:T(1024)(128)(4,1)S(1)}, s32[]{:S(2)}) async-start(s8[5242880]{0:T(1024)(128)(4,1)} %bitcast.219), calls=%async_computation.7 | async-start | bytes 8388608
  166.5 4.9 %copy-start.5 = (f32[1,1024,512]{1,2,0:T(8,128)}, f32[1,1024,512]{1,2,0:T(8,128)S(1)}, u32[]{:S(2)}) copy-start(f32[1,1024,512]{1,2,0:T(8,128)S(1)} %get-tuple-element.38) | copy-start | bytes 6291460
  189.9 31.6 %all-to-all-start.3 = ((bf16[2,8,128,512]{2,3,0,1:T(8,128)(2,1)}), bf16[2,8,128,512]{2,3,0,1:T(8,128)(2,1)}, u32[]{:S(2)}, u32[]{:S(2)}) async-start(bf16[2,8,128,512]{2,3,0,1:T(8,128)(2,1)} %fusion.11), calls=%async_computation.3 | async-start | bytes 4194304 | tf_op jit(solution)/shard_map/all_to_all | solution.py:153
  194.3 4.8 %slice-start.4 = ((s8[5242880]{0:T(1024)(128)(4,1)}), s8[4194304]{0:T(1024)(128)(4,1)S(1)}, s32[]{:S(2)}) async-start(s8[5242880]{0:T(1024)(128)(4,1)} %bitcast.221), calls=%async_computation.9 | async-start | bytes 8388608
  198.2 4.9 %copy-start.9 = (f32[1,1024,512]{1,2,0:T(8,128)}, f32[1,1024,512]{1,2,0:T(8,128)S(1)}, u32[]{:S(2)}) copy-start(f32[1,1024,512]{1,2,0:T(8,128)S(1)} %get-tuple-element.42) | copy-start | bytes 6291460
  221.5 31.7 %all-to-all-start.2 = ((bf16[2,8,128,512]{2,3,0,1:T(8,128)(2,1)}), bf16[2,8,128,512]{2,3,0,1:T(8,128)(2,1)}, u32[]{:S(2)}, u32[]{:S(2)}) async-start(bf16[2,8,128,512]{2,3,0,1:T(8,128)(2,1)} %fusion.12), calls=%async_computation.2 | async-start | bytes 4194304 | tf_op jit(solution)/shard_map/all_to_all | solution.py:152
  226.1 3.4 copy-start.27
  226.1 3.4 copy-start.31
  253.3 83.3 %all-to-all-start.1 = ((bf16[16,160,1024]{2,1,0:T(8,128)(2,1)}), bf16[16,160,1024]{2,1,0:T(8,128)(2,1)}, u32[]{:S(2)}, u32[]{:S(2)}) async-start(bf16[16,160,1024]{2,1,0:T(8,128)(2,1)} %bitcast.223), calls=%async_computation.1 | async-start | bytes 10485760 | tf_op jit(solution)/shard_map/all_to_all | solution.py:127
  258.6 4.4 %copy-start.4 = (bf16[1,2,1024,512]{2,3,1,0:T(8,128)(2,1)S(1)}, bf16[1,2,1024,512]{2,3,1,0:T(8,128)(2,1)}, u32[]{:S(2)}) copy-start(bf16[1,2,1024,512]{2,3,1,0:T(8,128)(2,1)} %copy.47) | copy-start | bytes 6291460
  258.6 4.6 %copy-start.6 = (f32[1,1024,512]{1,2,0:T(8,128)S(1)}, f32[1,1024,512]{1,2,0:T(8,128)}, u32[]{:S(2)}) copy-start(f32[1,1024,512]{1,2,0:T(8,128)} %copy-done.5) | copy-start | bytes 6291460
  258.7 5.5 %copy-start.8 = (f32[1,1024,512]{1,2,0:T(8,128)S(1)}, f32[1,1024,512]{1,2,0:T(8,128)}, u32[]{:S(2)}) copy-start(f32[1,1024,512]{1,2,0:T(8,128)} %copy-done.7) | copy-start | bytes 6291460
  271.6 3.3 copy-start.10
  271.6 3.5 copy-start.12
  277.6 4.1 %copy-start.14 = (bf16[1,2,512,1024]{3,2,1,0:T(8,128)(2,1)S(1)}, bf16[1,2,512,1024]{3,2,1,0:T(8,128)(2,1)}, u32[]{:S(2)}) copy-start(bf16[1,2,512,1024]{3,2,1,0:T(8,128)(2,1)} %param.19) | copy-start | bytes 6291460
  336.6 20.7 %copy-start.1 = (bf16[256,1024]{1,0:T(8,128)(2,1)S(1)}, bf16[256,1024]{1,0:T(8,128)(2,1)}, u32[]{:S(2)}) copy-start(bf16[256,1024]{1,0:T(8,128)(2,1)} %param.11) | copy-start | bytes 1572868
  (15 other events, 28.6 us)
where the time goes:
time: 363 us; the launch traced here: 358 us
  waiting for transfers between devices  131 us (36%)
  local copies, waits for them, and re-layouts  94.8 us (26%)
  other arithmetic  60.6 us (17%)
  matrix products  42.1 us (12%)
  starting transfers between devices  27.3 us (8%)
    all_to_all x1, waiting for transfers between devices, on_device(): lax.all_to_all(rows_sent.reshape(expert_count, per_dev * capacity, model_...  47.9 us
    unnamed x101, local copies, waits for them, and re-layouts  43.1 us
    all_to_all x1, waiting for transfers between devices, on_device(): lax.all_to_all(outgoing.reshape(expert_count, per_dev * capacity, model_w...  40.9 us
    dot_general x6, matrix products, over_columns(): lax.dot_general(left, right, (((1,), (1,)), ((), ())), preferred_element_...  16 us
    all_to_all x1, waiting for transfers between devices, on_device(): lax.all_to_all(gate_blocks, 'dp', split_axis=1, concat_axis=1, tiled=True)  15.8 us
    gather x1, local copies, waits for them, and re-layouts, on_device(): route_rows[target].astype(jnp.float32)  14.4 us
    dot_general x6, matrix products, over_rows(): lax.dot_general(left, right, (((0,), (0,)), ((), ())), preferred_element_...  14 us
    gather x1, local copies, waits for them, and re-layouts, on_device(): weights_sent = jnp.where(filled, probs.reshape(-1)[owner_safe], 0.0)  13.6 us
  transfers between devices with their start and end apart: 5, of which 5 were waited for; matrix products, arithmetic and copies ran while one was open for 27% of the time, Pallas kernels for 0%

commit v1 on v0

v1 whole, which is shorter than its diff:
```python
import functools

import jax
import jax.numpy as jnp
from jax import lax
from jax.experimental import pallas as pl
from jax.experimental.pallas import tpu as pltpu
from jax.sharding import PartitionSpec as P

loss_unscale = 0.0625
epsilon = 1e-05

SIDE = 4
OFFSETS = (0, -1, 1, 2)
CAP = 80
TOK = 256
D = 1024
HID = 512
BF = jnp.bfloat16
F32 = jnp.float32
VMEM_LIMIT = 56 * 2**20


def expert_index(core, first, second):
    return jnp.where(core == 0, first * SIDE + second, second * SIDE + first)


def pairs(axis, step):
    out = []
    for dp in range(8):
        core = dp % 2
        for z in range(SIDE):
            for y in range(SIDE):
                along_z = (axis == 0) == (core == 0)
                z2, y2 = ((z + step) % SIDE, y) if along_z else (z, (y + step) % SIDE)
                out.append((dp * 16 + z * SIDE + y, dp * 16 + z2 * SIDE + y2))
    return out


def hop(value, axis, step):
    return lax.ppermute(value, ("dp", "expert"), pairs(axis, step))


def nt(left, right):
    return lax.dot_general(left, right, (((1,), (1,)), ((), ())), preferred_element_type=F32)


def forward_kernel(perm, *refs):
    xs, (wg, wu, xt, ht, m12, rows) = refs[:8], refs[8:]
    for i in range(8):
        rows[i * CAP : (i + 1) * CAP, :] = xs[i][0, 0]
    saved = rows[...]
    gate = jnp.dot(saved, wg[0], preferred_element_type=F32)
    up = jnp.dot(saved, wu[0], preferred_element_type=F32)
    logistic = jax.nn.sigmoid(gate)
    act = gate * logistic
    m12[0, :, :HID] = up * (logistic * (1.0 + gate * (1.0 - logistic)))
    m12[0, :, HID:] = act
    ht[0] = (act * up).astype(BF).T
    xt[0] = saved.T


def forward_terms(perm, x, wg, wu):
    blocks = x.reshape(2, 16, CAP, D)

    def block_at(i):
        return pl.BlockSpec((1, 1, CAP, D), lambda e, h, p: (e, p[8 * h + i], 0, 0))

    half = 8 * CAP
    return pl.pallas_call(
        forward_kernel,
        grid_spec=pltpu.PrefetchScalarGridSpec(
            num_scalar_prefetch=1,
            grid=(2, 2),
            in_specs=[block_at(i) for i in range(8)]
            + [pl.BlockSpec((1, D, HID), lambda e, h, p: (e, 0, 0))] * 2,
            out_specs=[
                pl.BlockSpec((1, D, half), lambda e, h, p: (e, 0, h)),
                pl.BlockSpec((1, HID, half), lambda e, h, p: (e, 0, h)),
                pl.BlockSpec((1, half, 2 * HID), lambda e, h, p: (e, h, 0)),
            ],
            scratch_shapes=[pltpu.VMEM((half, D), BF)],
        ),
        out_shape=[
            jax.ShapeDtypeStruct((2, D, 16 * CAP), BF),
            jax.ShapeDtypeStruct((2, HID, 16 * CAP), BF),
            jax.ShapeDtypeStruct((2, 16 * CAP, 2 * HID), F32),
        ],
        compiler_params=pltpu.CompilerParams(vmem_limit_bytes=VMEM_LIMIT),
        cost_estimate=pl.CostEstimate(flops=5_400_000_000, bytes_accessed=30_000_000, transcendentals=1_310_720),
        name="forward_terms",
    )(perm, *([blocks] * 8), wg, wu)


def slots_kernel(perm, first, meta, info):
    eid = first[0]
    before = (
        lax.broadcasted_iota(jnp.int32, (TOK, TOK), 0) < lax.broadcasted_iota(jnp.int32, (TOK, TOK), 1)
    ).astype(BF)
    for b in range(16):
        block = meta[perm[b]]
        routes, probs = block[:8], block[8:]
        named, weight = [], []
        for e in range(2):
            hit = routes == (eid + e).astype(F32)
            named.append(jnp.sum(jnp.where(hit, 1.0, 0.0), axis=0, keepdims=True))
            weight.append(jnp.sum(jnp.where(hit, probs, 0.0), axis=0, keepdims=True))
        mask = jnp.concatenate(named + [jnp.zeros((6, TOK), F32)], axis=0)
        rank = jnp.dot(mask.astype(BF), before, preferred_element_type=F32)
        key = jnp.where(mask > 0.5, rank, -1.0)
        info[b] = jnp.concatenate([key[:2], weight[0], weight[1], jnp.zeros((4, TOK), F32)], axis=0)


def slot_info(perm, first, meta):
    return pl.pallas_call(
        slots_kernel,
        in_specs=[
            pl.BlockSpec(memory_space=pltpu.SMEM),
            pl.BlockSpec(memory_space=pltpu.SMEM),
            pl.BlockSpec(memory_space=pltpu.VMEM),
        ],
        out_specs=pl.BlockSpec(memory_space=pltpu.VMEM),
        out_shape=jax.ShapeDtypeStruct((16, 8, TOK), F32),
        cost_estimate=pl.CostEstimate(flops=20_000_000, bytes_accessed=400_000, transcendentals=0),
        name="slot_info",
    )(perm, first, meta)


def group_kernel(parts, chained, *refs):
    tokens, refs = refs[:parts], refs[parts:]
    info, m12, wd, wg, wu = refs[:5]
    refs = refs[5 + (2 if chained else 0) :]
    cot, gab, partial, onehot, rows = refs
    e = pl.program_id(0)
    per = 4 // parts

    @pl.when(e == 0)
    def _():
        slot = lax.broadcasted_iota(jnp.int32, (CAP, TOK), 0).astype(F32)
        for i in range(4):
            halves, scales = [], []
            for k in range(2):
                hit = slot == info[i, k : k + 1, :]
                halves.append(jnp.where(hit, 1.0, 0.0).astype(BF))
                scales.append(jnp.sum(jnp.where(hit, info[i, 2 + k : 3 + k, :], 0.0), axis=1, keepdims=True))
            chosen = jnp.concatenate(halves, axis=0)
            onehot[i] = chosen
            source = tokens[i // per][(i % per) * TOK : (i % per + 1) * TOK, :]
            taken = jnp.dot(chosen, source, preferred_element_type=F32)
            scaled = (taken * jnp.concatenate(scales, axis=0)).astype(BF)
            cot[0, i * CAP : (i + 1) * CAP, :] = scaled[:CAP]
            cot[1, i * CAP : (i + 1) * CAP, :] = scaled[CAP:]

    grad_hidden = nt(cot[e], wd[0])
    grad_a = (grad_hidden * m12[0, :, :HID]).astype(BF)
    grad_b = (grad_hidden * m12[0, :, HID:]).astype(BF)
    gab[0, :, :HID] = grad_a
    gab[0, :, HID:] = grad_b
    row_grads = (nt(grad_a, wg[0]) + nt(grad_b, wu[0])).astype(BF)
    for i in range(4):
        rows[e, i] = row_grads[i * CAP : (i + 1) * CAP]

    @pl.when(e == 1)
    def _():
        for i in range(4):
            both = jnp.concatenate([rows[0, i], rows[1, i]], axis=0)
            partial[i * TOK : (i + 1) * TOK, :] = lax.dot_general(
                onehot[i], both, (((0,), (0,)), ((), ())), preferred_element_type=F32
            ).astype(BF)


def group_pass(group, tokens, info, m12, wd, wg, wu, carried):
    parts = len(tokens)
    group_rows = 4 * CAP
    any_spec = pl.BlockSpec(memory_space=pl.ANY)
    chained = carried is not None
    args = [*tokens, info, m12, wd, wg, wu] + (list(carried) if chained else [])
    slots = jax.ShapeDtypeStruct((2, 16 * CAP, D), BF)
    return pl.pallas_call(
        functools.partial(group_kernel, parts, chained),
        grid=(2,),
        in_specs=[pl.BlockSpec((4 * TOK // parts, D), lambda e: (0, 0))] * parts
        + [
            pl.BlockSpec((4, 8, TOK), lambda e: (group, 0, 0)),
            pl.BlockSpec((1, group_rows, 2 * HID), lambda e: (e, group, 0)),
            pl.BlockSpec((1, HID, D), lambda e: (e, 0, 0)),
            pl.BlockSpec((1, D, HID), lambda e: (e, 0, 0)),
            pl.BlockSpec((1, D, HID), lambda e: (e, 0, 0)),
        ]
        + ([any_spec, any_spec] if chained else []),
        out_specs=[
            pl.BlockSpec((2, group_rows, D), lambda e: (0, group, 0)),
            pl.BlockSpec((1, group_rows, D), lambda e: (e, group, 0)),
            pl.BlockSpec((4 * TOK, D), lambda e: (0, 0)),
        ],
        out_shape=[slots, slots, jax.ShapeDtypeStruct((4 * TOK, D), BF)],
        scratch_shapes=[pltpu.VMEM((4, 2 * CAP, TOK), BF), pltpu.VMEM((2, 4, CAP, D), BF)],
        input_output_aliases={parts + 5: 0, parts + 6: 1} if chained else {},
        compiler_params=pltpu.CompilerParams(vmem_limit_bytes=VMEM_LIMIT),
        cost_estimate=pl.CostEstimate(flops=2_700_000_000, bytes_accessed=18_000_000, transcendentals=0),
        name=f"group_{group}",
    )(*args)


def compress(local_grad, residual):
    carried = local_grad * loss_unscale + residual.astype(F32)
    magnitude = jnp.mean(jnp.abs(carried), axis=-1, keepdims=True) + epsilon
    compressed = (magnitude * jnp.tanh(carried * (1.0 / magnitude))).astype(BF)
    return compressed, (carried - compressed.astype(F32)).astype(BF)


def gate_up_kernel(xt, gab, res_gate, res_up, sent, left_gate, left_up):
    grads = jnp.dot(xt[0], gab[0], preferred_element_type=F32)
    for m, (res, left) in enumerate(((res_gate, left_gate), (res_up, left_up))):
        compressed, left[0] = compress(grads[:, m * HID : (m + 1) * HID], res[0])
        sent[0, m, 0] = compressed[:128]
        sent[1, m, 0] = compressed[128:]


def gate_up_grads(xt, gab, res_gate, res_up):
    tile = pl.BlockSpec((1, 256, HID), lambda e, t: (e, t, 0))
    res_shape = jax.ShapeDtypeStruct((2, D, HID), BF)
    return pl.pallas_call(
        gate_up_kernel,
        grid=(2, 4),
        in_specs=[
            pl.BlockSpec((1, 256, 16 * CAP), lambda e, t: (e, t, 0)),
            pl.BlockSpec((1, 16 * CAP, 2 * HID), lambda e, t: (e, 0, 0)),
            tile,
            tile,
        ],
        out_specs=[pl.BlockSpec((2, 2, 1, 128, HID), lambda e, t: (t, 0, e, 0, 0)), tile, tile],
        out_shape=[jax.ShapeDtypeStruct((8, 3, 2, 128, HID), BF), res_shape, res_shape],
        compiler_params=pltpu.CompilerParams(vmem_limit_bytes=VMEM_LIMIT),
        cost_estimate=pl.CostEstimate(flops=5_400_000_000, bytes_accessed=22_000_000, transcendentals=2_000_000),
        name="gate_up_grads",
    )(xt, gab, res_gate, res_up)


def down_kernel(ht, cot, res, _, sent, left):
    compressed, left[0] = compress(jnp.dot(ht[0], cot[0], preferred_element_type=F32), res[0])
    for owner in range(8):
        for q in range(2):
            sent[owner, 0, 0, :, q * 128 : (q + 1) * 128] = compressed[
                q * 128 : (q + 1) * 128, owner * 128 : (owner + 1) * 128
            ]


def down_grads(ht, cot, res, sent):
    tile = pl.BlockSpec((1, 256, D), lambda e, t: (e, t, 0))
    return pl.pallas_call(
        down_kernel,
        grid=(2, 2),
        in_specs=[
            pl.BlockSpec((1, 256, 16 * CAP), lambda e, t: (e, t, 0)),
            pl.BlockSpec((1, 16 * CAP, D), lambda e, t: (e, 0, 0)),
            tile,
            pl.BlockSpec(memory_space=pl.ANY),
        ],
        out_specs=[pl.BlockSpec((8, 1, 1, 128, 256), lambda e, t: (0, 2, e, 0, t)), tile],
        out_shape=[jax.ShapeDtypeStruct((8, 3, 2, 128, HID), BF), jax.ShapeDtypeStruct((2, HID, D), BF)],
        input_output_aliases={3: 0},
        compiler_params=pltpu.CompilerParams(vmem_limit_bytes=VMEM_LIMIT),
        cost_estimate=pl.CostEstimate(flops=2_700_000_000, bytes_accessed=14_000_000, transcendentals=1_000_000),
        name="down_grads",
    )(ht, cot, res, sent)


def add(*terms):
    total = terms[0].astype(F32)
    for term in terms[1:]:
        total = total + term.astype(F32)
    return total.astype(BF)


def on_device(x_saved, d_out, routes, probs, w_gate, w_up, w_down, res_gate, res_up, res_down):
    place = lax.axis_index("expert")
    core = lax.axis_index("dp") % 2
    first = jnp.where(core == 0, place // SIDE, place % SIDE)
    second = jnp.where(core == 0, place % SIDE, place // SIDE)
    offsets = jnp.array(OFFSETS, jnp.int32)
    perm = expert_index(
        core, ((first + offsets) % SIDE)[None, :], ((second + offsets) % SIDE)[:, None]
    ).reshape(-1).astype(jnp.int32)

    near_plus, near_minus = hop(d_out, 0, 1), hop(d_out, 0, -1)
    far_plus, far_minus = hop(near_plus[:128], 0, 1), hop(near_minus[128:], 0, -1)
    group0 = jnp.concatenate([d_out, near_plus, near_minus, far_plus, far_minus], axis=0)
    group1, group2 = hop(group0, 1, 1), hop(group0, 1, -1)
    group3 = (hop(group1[:512], 1, 1), hop(group2[512:], 1, -1))

    meta = lax.all_gather(
        jnp.concatenate([routes.astype(F32).T, probs.T], axis=0), "expert", axis=0, tiled=False
    )
    info = slot_info(perm, (place * 2).astype(jnp.int32).reshape(1), meta)
    xt, ht, m12 = forward_terms(perm, x_saved[0], w_gate, w_up)

    run = functools.partial(group_pass, info=info, m12=m12, wd=w_down, wg=w_gate, wu=w_up)
    cot, gab, part0 = run(0, (group0,), carried=None)
    cot, gab, part1 = run(1, (group1,), carried=(cot, gab))
    cot, gab, part2 = run(2, (group2,), carried=(cot, gab))
    cot, gab, part3 = run(3, group3, carried=(cot, gab))

    over_plus, over_minus = hop(part3[:512], 1, 1), hop(part3[512:], 1, -1)
    to_plus = jnp.concatenate([add(part2[:512], over_plus), part2[512:]], axis=0)
    to_minus = jnp.concatenate([part1[:512], add(part1[512:], over_minus)], axis=0)
    column = add(part0, hop(to_plus, 1, 1), hop(to_minus, 1, -1))
    over_plus, over_minus = hop(column[768:896], 0, 1), hop(column[896:], 0, -1)
    to_plus = jnp.concatenate([add(column[512:640], over_plus), column[640:768]], axis=0)
    to_minus = jnp.concatenate([column[256:384], add(column[384:512], over_minus)], axis=0)
    d_tokens = add(column[:256], hop(to_plus, 0, 1), hop(to_minus, 0, -1))

    sent, left_gate, left_up = gate_up_grads(xt, gab, res_gate[0], res_up[0])
    sent, left_down = down_grads(ht, cot, res_down[0], sent)
    total = lax.psum_scatter(sent.reshape(8 * 3 * 2 * 128, HID), "dp", scatter_dimension=0, tiled=True)
    mean = total.reshape(3, 2, 128, HID).astype(F32) / 8.0
    mean_down = mean[2].reshape(2, 128, 4, 128).transpose(0, 2, 1, 3).reshape(2, HID, 128)
    return (d_tokens, mean[0], mean[1], mean_down, left_gate[None], left_up[None], left_down[None])


def solution(mesh):
    in_specs = (
        P("dp", "expert", None, None),
        P(("dp", "expert"), None),
        P(("dp", "expert"), None),
        P(("dp", "expert"), None),
        P("expert", None, None),
        P("expert", None, None),
        P("expert", None, None),
        P("dp", "expert", None, None),
        P("dp", "expert", None, None),
        P("dp", "expert", None, None),
    )
    out_specs = (
        P(("dp", "expert"), None),
        P("expert", "dp", None),
        P("expert", "dp", None),
        P("expert", None, "dp"),
        P("dp", "expert", None, None),
        P("dp", "expert", None, None),
        P("dp", "expert", None, None),
    )
    return jax.shard_map(
        on_device, mesh=mesh, in_specs=in_specs, out_specs=out_specs, check_vma=False
    )
```

time: 363 us -> 247 us (0.68); the launches traced: 358 us -> 246 us
  local copies, waits for them, and re-layouts: 94.8 us -> 12.3 us
  Pallas kernels: 0 us -> 78 us
  waiting for transfers between devices: 131 us -> 66.2 us
  other arithmetic: 60.6 us -> 5.43 us
  blocking collectives: 0 us -> 44.3 us
  matrix products: 42.1 us -> 0 us
  between operations: 1.87 us -> 14.3 us
    all_to_all x5 -> x0, waiting for transfers between devices: 131 us -> none  [the longest x1 47.9 us: on_device(): lax.all_to_all(rows_sent.reshape(expert_count, per_dev * capacity, model_...]
    pallas_call x0 -> x8, Pallas kernels: none -> 78 us  [the longest x4 36.9 us: group_pass(): pl.pallas_call(functools.partial(group_kernel, parts, chained), grid=(2,)...]
    ppermute x0 -> x16, waiting for transfers between devices: none -> 66.2 us  [hop(): return lax.ppermute(value, ('dp', 'expert'), pairs(axis, step))]
    all_gather x0 -> x1, blocking collectives: none -> 44.3 us  [on_device(): lax.all_gather(jnp.concatenate([routes.astype(F32).T, probs.T], axis=0),...]
    dot_general x16 -> x0, matrix products: 42.1 us -> none  [the longest x6 16 us: over_columns(): lax.dot_general(left, right, (((1,), (1,)), ((), ())), preferred_element_...]
    gather x3 -> x0, local copies, waits for them, and re-layouts: 36.9 us -> none  [the longest x1 14.4 us: on_device(): route_rows[target].astype(jnp.float32)]
    unnamed x101 -> x24, local copies, waits for them, and re-layouts: 43.1 us -> 7.13 us
    all_to_all x5 -> x0, starting transfers between devices: 27.3 us -> none  [the longest x1 8.31 us: on_device(): lax.all_to_all(rows_sent.reshape(expert_count, per_dev * capacity, model_...]
  transfers between devices with their start and end apart: 5 -> 17, of which waited for: 5 -> 9; matrix products, arithmetic and copies ran while one was open for 27% -> 4% of each run, Pallas kernels for 0% -> 18%
where the time goes in v1:
time: 247 us; the launch traced here: 246 us
  Pallas kernels  78 us (32%)
  waiting for transfers between devices  66.2 us (27%)
  blocking collectives  44.3 us (18%)
  starting transfers between devices  26 us (11%)
  between operations  14.3 us (6%)
  local copies, waits for them, and re-layouts  12.3 us (5%)
  other arithmetic  5.43 us (2%)
    ppermute x16, waiting for transfers between devices, hop(): return lax.ppermute(value, ('dp', 'expert'), pairs(axis, step))  66.2 us
    all_gather x1, blocking collectives, on_device(): lax.all_gather(jnp.concatenate([routes.astype(F32).T, probs.T], axis=0),...  44.3 us
    pallas_call x4, Pallas kernels, group_pass(): pl.pallas_call(functools.partial(group_kernel, parts, chained), grid=(2,)...  36.9 us
    ppermute x16, starting transfers between devices, hop(): return lax.ppermute(value, ('dp', 'expert'), pairs(axis, step))  26 us
    pallas_call x1, Pallas kernels, forward_terms(): pl.pallas_call(forward_kernel, grid_spec=pltpu.PrefetchScalarGridSpec(num...  15.2 us
    pallas_call x1, Pallas kernels, gate_up_grads(): pl.pallas_call(gate_up_kernel, grid=(2, 4), in_specs=[pl.BlockSpec((1, 25...  14.6 us
    pallas_call x1, Pallas kernels, down_grads(): pl.pallas_call(down_kernel, grid=(2, 2), in_specs=[pl.BlockSpec((1, 256,...  9.32 us
    unnamed x24, local copies, waits for them, and re-layouts  7.13 us
  transfers between devices with their start and end apart: 17, of which 9 were waited for; matrix products, arithmetic and copies ran while one was open for 4% of the time, Pallas kernels for 18%

profile of v1, /device:TPU:0, one launch (start us, length us, event | category | flops | bytes accessed | tf_op | source)
XLA Modules:
  0.0 246.5 jit_solution(15500769107011793952)
XLA Ops:
  7.2 2.1 collective-permute-start
  9.3 2.2 collective-permute-start.1
  11.5 7.3 %collective-permute-done = bf16[256,1024]{1,0:T(8,128)(2,1)S(1)} collective-permute-done((bf16[256,1024]{1,0:T(8,128)(2,1)}, bf16[256,1024]{1,0:T(8,128)(2,1)S(1)}, u32[]{:S(2)}, u32[]{:S(2)}) %collective-permute-start) | collective-permute-done | bytes 524320 | tf_op jit(solution)/shard_map/ppermute | solution.py:41
  18.9 1.9 constant_dynamic-update-slice_fusion.4
  20.8 3.3 %collective-permute-start.3 = (bf16[128,1024]{1,0:T(8,128)(2,1)S(1)}, bf16[128,1024]{1,0:T(8,128)(2,1)S(1)}, u32[]{:S(2)}, u32[]{:S(2)}) collective-permute-start(bf16[128,1024]{1,0:T(8,128)(2,1)S(1)} %slice.84), channel_id=1, source_target_pairs={{0,12},{1,13},{2,14},{3,15},{4,0},{5,1},{6,2},{7,3},{8,4},{9,5},{1... | collective-permute-start | bytes 786440 | tf_op jit(solution)/shard_map/ppermute | solution.py:41
  28.7 1.6 collective-permute-start.5
  30.3 1.7 collective-permute-start.4
  32.6 44.3 %all-gather = f32[256,256]{1,0:T(8,128)} all-gather(f32[16,256]{1,0:T(8,128)S(1)} %pad_maximum_fusion.4), channel_id=2, replica_groups=mesh['dp'=8,'expert'=16] {'expert'}, dimensions={0}, use_global_device_ids=true | all-gather | bytes 278528 | tf_op jit(solution)/shard_map/all_gather | solution.py:292
  76.9 2.0 slot_info.1.refs_1_.refs_2_
  78.9 1.3 slice.85
  80.2 1.5 collective-permute-start.6
  81.8 2.1 collective-permute-start.7
  83.9 15.2 %forward_terms.1 = (bf16[2,1024,1280]{2,1,0:T(8,128)(2,1)}, bf16[2,512,1280]{2,1,0:T(8,128)(2,1)}, f32[2,1280,1024]{2,1,0:T(8,128)}) custom-call(s32[16]{0:T(128)} %select_n.55.perm, bf16[2,16,80,1024]{3,2,1,0:T(8,128)(2,1)} %bitcast.18, bf16[2,16,80,1024]{3,2,1,0:T(8,128)(2,1)} %bitcast.19, bf16[2,16,80,1024]{3,2,1,0:T(8,128)(2,1)} %bitcast.20, ...), custom_call_target="tpu_custom_call" | custom-call | flops 5400000000 | bytes 30000000 | tf_op jit(solution)/shard_map/forward_terms/pallas_call | solution.py:70
  99.0 9.2 %group_0.1 = (bf16[2,1280,1024]{2,1,0:T(8,128)(2,1)}, bf16[2,1280,1024]{2,1,0:T(8,128)(2,1)}, bf16[1024,1024]{1,0:T(8,128)(2,1)}) custom-call(bf16[1024,1024]{1,0:T(8,128)(2,1)} %constant_dynamic-update-slice_fusion.refs_0_, f32[16,8,256]{2,1,0:T(8,128)} %slot_info.1.refs_1_.refs_2_, f32[2,1280,1024]{2,1,0:T(8,128)} %get-tuple-element.27.refs_2_.refs_3_, ...), custom_call_target="tpu_custom_call" | custom-call | flops 2700000000 | bytes 18000000 | tf_op jit(solution)/shard_map/group_0/pallas_call | solution.py:179
  108.3 9.2 %group_1.1 = (bf16[2,1280,1024]{2,1,0:T(8,128)(2,1)}, bf16[2,1280,1024]{2,1,0:T(8,128)(2,1)}, bf16[1024,1024]{1,0:T(8,128)(2,1)}) custom-call(bf16[1024,1024]{1,0:T(8,128)(2,1)} %collective-permute-done.5.refs_0_, f32[16,8,256]{2,1,0:T(8,128)} %slot_info.1.refs_1_.refs_2_, ...), custom_call_target="tpu_custom_call", output_to_operand_aliasing={{0}: (6, {}), {1}: (7, {})} | custom-call | flops 2700000000 | bytes 18000000 | tf_op jit(solution)/shard_map/group_1/pallas_call | solution.py:179
  117.5 9.3 %group_2.1 = (bf16[2,1280,1024]{2,1,0:T(8,128)(2,1)}, bf16[2,1280,1024]{2,1,0:T(8,128)(2,1)}, bf16[1024,1024]{1,0:T(8,128)(2,1)}) custom-call(bf16[1024,1024]{1,0:T(8,128)(2,1)} %copy-done, f32[16,8,256]{2,1,0:T(8,128)} %slot_info.1.refs_1_.refs_2_, ...), custom_call_target="tpu_custom_call", output_to_operand_aliasing={{0}: (6, {}), {1}: (7, {})} | custom-call | flops 2700000000 | bytes 18000000 | tf_op jit(solution)/shard_map/group_2/pallas_call | solution.py:179
  128.2 9.1 %group_3.1 = (bf16[2,1280,1024]{2,1,0:T(8,128)(2,1)}, bf16[2,1280,1024]{2,1,0:T(8,128)(2,1)}, bf16[1024,1024]{1,0:T(8,128)(2,1)}) custom-call(bf16[512,1024]{1,0:T(8,128)(2,1)} %copy-done.5, bf16[512,1024]{1,0:T(8,128)(2,1)} %copy-done.6, f32[16,8,256]{2,1,0:T(8,128)} %slot_info.1.refs_1_.refs_2_, ...), custom_call_target="tpu_custom_call", output_to_operand_aliasing={{0}: (7, {}), {1}: (8, {})} | custom-call | flops 2700000000 | bytes 18000000 | tf_op jit(solution)/shard_map/group_3/pallas_call | solution.py:179
  137.2 14.6 %gate_up_grads.1 = (bf16[8,3,2,128,512]{4,3,2,1,0:T(8,128)(2,1)}, bf16[2,1024,512]{2,1,0:T(8,128)(2,1)}, bf16[2,1024,512]{2,1,0:T(8,128)(2,1)}) custom-call(bf16[2,1024,1280]{2,1,0:T(8,128)(2,1)} %get-tuple-element.40.xt, bf16[2,1280,1024]{2,1,0:T(8,128)(2,1)} %get-tuple-element.41.gab, bf16[2,1024,512]{2,1,0:T(8,128)(2,1)} %bitcast.33, ...), custom_call_target="tpu_custom_call" | custom-call | flops 5400000000 | bytes 22000000 | tf_op jit(solution)/shard_map/gate_up_grads/pallas_call | solution.py:223
  151.8 9.3 %down_grads.1 = (bf16[8,3,2,128,512]{4,3,2,1,0:T(8,128)(2,1)}, bf16[2,512,1024]{2,1,0:T(8,128)(2,1)}) custom-call(bf16[2,512,1280]{2,1,0:T(8,128)(2,1)} %get-tuple-element.38.ht, bf16[2,1280,1024]{2,1,0:T(8,128)(2,1)} %get-tuple-element.39.cot, bf16[2,512,1024]{2,1,0:T(8,128)(2,1)} %bitcast.27, ...), custom_call_target="tpu_custom_call", output_to_operand_aliasing={{0}: (3, {})} | custom-call | flops 2700000000 | bytes 14000000 | tf_op jit(solution)/shard_map/down_grads/pallas_call | solution.py:251
  161.2 1.6 copy-done.3
  162.9 1.5 collective-permute-start.10
  165.2 12.6 %collective-permute-done.10 = bf16[512,1024]{1,0:T(8,128)(2,1)S(1)} collective-permute-done((bf16[512,1024]{1,0:T(8,128)(2,1)S(1)}, bf16[512,1024]{1,0:T(8,128)(2,1)S(1)}, u32[]{:S(2)}, u32[]{:S(2)}) %collective-permute-start.10) | collective-permute-done | bytes 1048608 | tf_op jit(solution)/shard_map/ppermute | solution.py:41
  178.4 2.7 %collective-permute-start.11 = (bf16[1024,1024]{1,0:T(8,128)(2,1)S(1)}, bf16[1024,1024]{1,0:T(8,128)(2,1)S(1)}, u32[]{:S(2)}, u32[]{:S(2)}) collective-permute-start(bf16[1024,1024]{1,0:T(8,128)(2,1)S(1)} %pad_maximum_fusion.1), channel_id=1, source_target_pairs={{0,3},{1,0},{2,1},{3,2},{4,7},{5,4},{6,5},{7,6},{8,11},{9,8},{10,9... | collective-permute-start | bytes 6291464 | tf_op jit(solution)/shard_map/ppermute | solution.py:41
  181.8 23.3 %collective-permute-done.11 = bf16[1024,1024]{1,0:T(8,128)(2,1)S(1)} collective-permute-done((bf16[1024,1024]{1,0:T(8,128)(2,1)S(1)}, bf16[1024,1024]{1,0:T(8,128)(2,1)S(1)}, u32[]{:S(2)}, u32[]{:S(2)}) %collective-permute-start.11) | collective-permute-done | bytes 2097184 | tf_op jit(solution)/shard_map/ppermute | solution.py:41
  205.0 6.8 %collective-permute-done.9 = bf16[1024,1024]{1,0:T(8,128)(2,1)S(1)} collective-permute-done((bf16[1024,1024]{1,0:T(8,128)(2,1)S(1)}, bf16[1024,1024]{1,0:T(8,128)(2,1)S(1)}, u32[]{:S(2)}, u32[]{:S(2)}) %collective-permute-start.9) | collective-permute-done | bytes 2097184 | tf_op jit(solution)/shard_map/ppermute | solution.py:41
  211.8 1.5 add_convert_fusion
  213.6 3.1 %collective-permute-start.14 = (bf16[128,1024]{1,0:T(8,128)(2,1)S(1)}, bf16[128,1024]{1,0:T(8,128)(2,1)S(1)}, u32[]{:S(2)}, u32[]{:S(2)}) collective-permute-start(bf16[128,1024]{1,0:T(8,128)(2,1)S(1)} %get-tuple-element.54), channel_id=1, source_target_pairs={{0,12},{1,13},{2,14},{3,15},{4,0},{5,1},{6,2},{7,3},{8,4},{9,5},{1... | collective-permute-start | bytes 786440 | tf_op jit(solution)/shard_map/ppermute | solution.py:41
  216.7 4.3 %collective-permute-done.12 = bf16[128,1024]{1,0:T(8,128)(2,1)S(1)} collective-permute-done((bf16[128,1024]{1,0:T(8,128)(2,1)S(1)}, bf16[128,1024]{1,0:T(8,128)(2,1)S(1)}, u32[]{:S(2)}, u32[]{:S(2)}) %collective-permute-start.12) | collective-permute-done | bytes 262176 | tf_op jit(solution)/shard_map/ppermute | solution.py:41
  221.3 3.3 %collective-permute-start.15 = (bf16[256,1024]{1,0:T(8,128)(2,1)S(1)}, bf16[256,1024]{1,0:T(8,128)(2,1)S(1)}, u32[]{:S(2)}, u32[]{:S(2)}) collective-permute-start(bf16[256,1024]{1,0:T(8,128)(2,1)S(1)} %pad_maximum_fusion.3), channel_id=1, source_target_pairs={{0,12},{1,13},{2,14},{3,15},{4,0},{5,1},{6,2},{7,3},{8,4},{9,5},{1... | collective-permute-start | bytes 1572872 | tf_op jit(solution)/shard_map/ppermute | solution.py:41
  224.7 6.6 %collective-permute-done.15 = bf16[256,1024]{1,0:T(8,128)(2,1)S(1)} collective-permute-done((bf16[256,1024]{1,0:T(8,128)(2,1)S(1)}, bf16[256,1024]{1,0:T(8,128)(2,1)S(1)}, u32[]{:S(2)}, u32[]{:S(2)}) %collective-permute-start.15) | collective-permute-done | bytes 524320 | tf_op jit(solution)/shard_map/ppermute | solution.py:41
  231.3 3.8 %collective-permute-done.13 = bf16[256,1024]{1,0:T(8,128)(2,1)S(1)} collective-permute-done((bf16[256,1024]{1,0:T(8,128)(2,1)S(1)}, bf16[256,1024]{1,0:T(8,128)(2,1)S(1)}, u32[]{:S(2)}, u32[]{:S(2)}) %collective-permute-start.13) | collective-permute-done | bytes 524320 | tf_op jit(solution)/shard_map/ppermute | solution.py:41
  236.2 1.3 convert_multiply_fusion
  (63 shorter events, 12.8 us)
Async XLA Ops:
  7.2 229.0 %reduce-scatter.2.cloned.1.call-start = ((), (), s32[]{:S(2)}) async-start(), calls=%async_computation.1 | async-start | bytes 7077888 | tf_op jit(solution)/shard_map/reduce_scatter | solution.py:315
  7.2 11.6 %collective-permute-start = (bf16[256,1024]{1,0:T(8,128)(2,1)}, bf16[256,1024]{1,0:T(8,128)(2,1)S(1)}, u32[]{:S(2)}, u32[]{:S(2)}) collective-permute-start(bf16[256,1024]{1,0:T(8,128)(2,1)} %param.12), channel_id=1, source_target_pairs={{0,4},{1,5},{2,6},{3,7},{4,8},{5,9},{6,10},{7,11},{8,12},{9,13},{1... | collective-permute-start | bytes 1572872 | tf_op jit(solution)/shard_map/ppermute | solution.py:41
  9.3 11.5 %collective-permute-start.1 = (bf16[256,1024]{1,0:T(8,128)(2,1)}, bf16[256,1024]{1,0:T(8,128)(2,1)S(1)}, u32[]{:S(2)}, u32[]{:S(2)}) collective-permute-start(bf16[256,1024]{1,0:T(8,128)(2,1)} %param.12), channel_id=1, source_target_pairs={{0,12},{1,13},{2,14},{3,15},{4,0},{5,1},{6,2},{7,3},{8,4},{9,5},{1... | collective-permute-start | bytes 1572872 | tf_op jit(solution)/shard_map/ppermute | solution.py:41
  18.8 7.7 %collective-permute-start.2 = (bf16[128,1024]{1,0:T(8,128)(2,1)S(1)}, bf16[128,1024]{1,0:T(8,128)(2,1)S(1)}, u32[]{:S(2)}, u32[]{:S(2)}) collective-permute-start(bf16[128,1024]{1,0:T(8,128)(2,1)S(1)} %slice.83), channel_id=1, source_target_pairs={{0,4},{1,5},{2,6},{3,7},{4,8},{5,9},{6,10},{7,11},{8,12},{9,13},{1... | collective-permute-start | bytes 786440 | tf_op jit(solution)/shard_map/ppermute | solution.py:41
  20.7 11.2 %copy-start.9 = (s32[4]{0:T(128)S(1)}, s32[4]{0:T(128)}, u32[]{:S(2)}) copy-start(s32[4]{0:T(128)} %constant.68.clone) | copy-start | bytes 52
  20.8 11.9 %copy-start.7 = (s32[256,8]{0,1:T(8,128)S(1)}, s32[256,8]{0,1:T(8,128)}, u32[]{:S(2)}) copy-start(s32[256,8]{0,1:T(8,128)} %param.13) | copy-start | bytes 24580
  20.8 11.9 %copy-start.8 = (f32[256,8]{0,1:T(8,128)S(1)}, f32[256,8]{0,1:T(8,128)}, u32[]{:S(2)}) copy-start(f32[256,8]{0,1:T(8,128)} %param.14) | copy-start | bytes 24580
  20.8 7.2 %collective-permute-start.3 = (bf16[128,1024]{1,0:T(8,128)(2,1)S(1)}, bf16[128,1024]{1,0:T(8,128)(2,1)S(1)}, u32[]{:S(2)}, u32[]{:S(2)}) collective-permute-start(bf16[128,1024]{1,0:T(8,128)(2,1)S(1)} %slice.84), channel_id=1, source_target_pairs={{0,12},{1,13},{2,14},{3,15},{4,0},{5,1},{6,2},{7,3},{8,4},{9,5},{1... | collective-permute-start | bytes 786440 | tf_op jit(solution)/shard_map/ppermute | solution.py:41
  28.7 50.2 %collective-permute-start.5 = (bf16[1024,1024]{1,0:T(8,128)(2,1)}, bf16[1024,1024]{1,0:T(8,128)(2,1)}, u32[]{:S(2)}, u32[]{:S(2)}) collective-permute-start(bf16[1024,1024]{1,0:T(8,128)(2,1)} %constant_dynamic-update-slice_fusion.refs_0_), channel_id=1, source_target_pairs={{0,1},{1,2},{2,3},{3,0},{4,5},{5,6},{6,7},{7,4},{8,9},{9,10},{10,1... | collective-permute-start | bytes 6291464 | tf_op jit(solution)/shard_map/ppermute | solution.py:41
  30.3 51.4 %collective-permute-start.4 = (bf16[1024,1024]{1,0:T(8,128)(2,1)}, bf16[1024,1024]{1,0:T(8,128)(2,1)S(1)}, u32[]{:S(2)}, u32[]{:S(2)}) collective-permute-start(bf16[1024,1024]{1,0:T(8,128)(2,1)} %constant_dynamic-update-slice_fusion.refs_0_), channel_id=1, source_target_pairs={{0,3},{1,0},{2,1},{3,2},{4,7},{5,4},{6,5},{7,6},{8,11},{9,8},{10,9... | collective-permute-start | bytes 6291464 | tf_op jit(solution)/shard_map/ppermute | solution.py:41
  80.2 46.6 %collective-permute-start.6 = (bf16[512,1024]{1,0:T(8,128)(2,1)S(1)}, bf16[512,1024]{1,0:T(8,128)(2,1)S(1)}, u32[]{:S(2)}, u32[]{:S(2)}) collective-permute-start(bf16[512,1024]{1,0:T(8,128)(2,1)S(1)} %slice.85), channel_id=1, source_target_pairs={{0,1},{1,2},{2,3},{3,0},{4,5},{5,6},{6,7},{7,4},{8,9},{9,10},{10,1... | collective-permute-start | bytes 3145736 | tf_op jit(solution)/shard_map/ppermute | solution.py:41
  81.7 17.3 %copy-start = (bf16[1024,1024]{1,0:T(8,128)(2,1)}, bf16[1024,1024]{1,0:T(8,128)(2,1)S(1)}, u32[]{:S(2)}) copy-start(bf16[1024,1024]{1,0:T(8,128)(2,1)S(1)} %collective-permute-done.4.refs_0_) | copy-start | bytes 6291460
  81.8 45.1 %collective-permute-start.7 = (bf16[512,1024]{1,0:T(8,128)(2,1)S(1)}, bf16[512,1024]{1,0:T(8,128)(2,1)S(1)}, u32[]{:S(2)}, u32[]{:S(2)}) collective-permute-start(bf16[512,1024]{1,0:T(8,128)(2,1)S(1)} %slice.86), channel_id=1, source_target_pairs={{0,3},{1,0},{2,1},{3,2},{4,7},{5,4},{6,5},{7,6},{8,11},{9,8},{10,9... | collective-permute-start | bytes 3145736 | tf_op jit(solution)/shard_map/ppermute | solution.py:41
  126.8 1.0 copy-start.5
  126.9 1.3 copy-start.6
  161.1 1.6 copy-start.3
  162.7 2.3 copy-start.1
  162.9 2.2 copy-start.2
  162.9 14.9 %collective-permute-start.10 = (bf16[512,1024]{1,0:T(8,128)(2,1)S(1)}, bf16[512,1024]{1,0:T(8,128)(2,1)S(1)}, u32[]{:S(2)}, u32[]{:S(2)}) collective-permute-start(bf16[512,1024]{1,0:T(8,128)(2,1)S(1)} %get-tuple-element.58), channel_id=1, source_target_pairs={{0,3},{1,0},{2,1},{3,2},{4,7},{5,4},{6,5},{7,6},{8,11},{9,8},{10,9... | collective-permute-start | bytes 3145736 | tf_op jit(solution)/shard_map/ppermute | solution.py:41
  164.4 16.7 %collective-permute-start.8 = (bf16[512,1024]{1,0:T(8,128)(2,1)S(1)}, bf16[512,1024]{1,0:T(8,128)(2,1)S(1)}, u32[]{:S(2)}, u32[]{:S(2)}) collective-permute-start(bf16[512,1024]{1,0:T(8,128)(2,1)S(1)} %get-tuple-element.57), channel_id=1, source_target_pairs={{0,1},{1,2},{2,3},{3,0},{4,5},{5,6},{6,7},{7,4},{8,9},{9,10},{10,1... | collective-permute-start | bytes 3145736 | tf_op jit(solution)/shard_map/ppermute | solution.py:41
  178.4 26.7 %collective-permute-start.11 = (bf16[1024,1024]{1,0:T(8,128)(2,1)S(1)}, bf16[1024,1024]{1,0:T(8,128)(2,1)S(1)}, u32[]{:S(2)}, u32[]{:S(2)}) collective-permute-start(bf16[1024,1024]{1,0:T(8,128)(2,1)S(1)} %pad_maximum_fusion.1), channel_id=1, source_target_pairs={{0,3},{1,0},{2,1},{3,2},{4,7},{5,4},{6,5},{7,6},{8,11},{9,8},{10,9... | collective-permute-start | bytes 6291464 | tf_op jit(solution)/shard_map/ppermute | solution.py:41
  181.5 30.3 %copy-start.4 = (bf16[1024,1024]{1,0:T(8,128)(2,1)S(1)}, bf16[1024,1024]{1,0:T(8,128)(2,1)}, u32[]{:S(2)}) copy-start(bf16[1024,1024]{1,0:T(8,128)(2,1)} %get-tuple-element.28) | copy-start | bytes 6291460
  181.7 30.1 %collective-permute-start.9 = (bf16[1024,1024]{1,0:T(8,128)(2,1)S(1)}, bf16[1024,1024]{1,0:T(8,128)(2,1)S(1)}, u32[]{:S(2)}, u32[]{:S(2)}) collective-permute-start(bf16[1024,1024]{1,0:T(8,128)(2,1)S(1)} %pad_maximum_fusion), channel_id=1, source_target_pairs={{0,1},{1,2},{2,3},{3,0},{4,5},{5,6},{6,7},{7,4},{8,9},{9,10},{10,1... | collective-permute-start | bytes 6291464 | tf_op jit(solution)/shard_map/ppermute | solution.py:41
  213.4 7.7 %collective-permute-start.12 = (bf16[128,1024]{1,0:T(8,128)(2,1)S(1)}, bf16[128,1024]{1,0:T(8,128)(2,1)S(1)}, u32[]{:S(2)}, u32[]{:S(2)}) collective-permute-start(bf16[128,1024]{1,0:T(8,128)(2,1)S(1)} %get-tuple-element.53), channel_id=1, source_target_pairs={{0,4},{1,5},{2,6},{3,7},{4,8},{5,9},{6,10},{7,11},{8,12},{9,13},{1... | collective-permute-start | bytes 786440 | tf_op jit(solution)/shard_map/ppermute | solution.py:41
  213.6 7.5 %collective-permute-start.14 = (bf16[128,1024]{1,0:T(8,128)(2,1)S(1)}, bf16[128,1024]{1,0:T(8,128)(2,1)S(1)}, u32[]{:S(2)}, u32[]{:S(2)}) collective-permute-start(bf16[128,1024]{1,0:T(8,128)(2,1)S(1)} %get-tuple-element.54), channel_id=1, source_target_pairs={{0,12},{1,13},{2,14},{3,15},{4,0},{5,1},{6,2},{7,3},{8,4},{9,5},{1... | collective-permute-start | bytes 786440 | tf_op jit(solution)/shard_map/ppermute | solution.py:41
  221.3 10.0 %collective-permute-start.15 = (bf16[256,1024]{1,0:T(8,128)(2,1)S(1)}, bf16[256,1024]{1,0:T(8,128)(2,1)S(1)}, u32[]{:S(2)}, u32[]{:S(2)}) collective-permute-start(bf16[256,1024]{1,0:T(8,128)(2,1)S(1)} %pad_maximum_fusion.3), channel_id=1, source_target_pairs={{0,12},{1,13},{2,14},{3,15},{4,0},{5,1},{6,2},{7,3},{8,4},{9,5},{1... | collective-permute-start | bytes 1572872 | tf_op jit(solution)/shard_map/ppermute | solution.py:41
  224.7 10.5 %collective-permute-start.13 = (bf16[256,1024]{1,0:T(8,128)(2,1)S(1)}, bf16[256,1024]{1,0:T(8,128)(2,1)S(1)}, u32[]{:S(2)}, u32[]{:S(2)}) collective-permute-start(bf16[256,1024]{1,0:T(8,128)(2,1)S(1)} %pad_maximum_fusion.2), channel_id=1, source_target_pairs={{0,4},{1,5},{2,6},{3,7},{4,8},{5,9},{6,10},{7,11},{8,12},{9,13},{1... | collective-permute-start | bytes 1572872 | tf_op jit(solution)/shard_map/ppermute | solution.py:41
Sparse Core Ops, SparseCore 0:
  161.3 40.8 reduce-scatter.1

commit v2 on v1

v2 whole, which is shorter than its diff:
```python
import functools

import jax
import jax.numpy as jnp
from jax import lax
from jax.experimental import pallas as pl
from jax.experimental.pallas import tpu as pltpu
from jax.sharding import PartitionSpec as P

loss_unscale = 0.0625
epsilon = 1e-05

SIDE = 4
OFFSETS = (0, -1, 1, 2)
CAP = 80
TOK = 256
PACK = TOK + 16
D = 1024
HID = 512
BF = jnp.bfloat16
F32 = jnp.float32
VMEM_LIMIT = 56 * 2**20


def expert_index(core, first, second):
    return jnp.where(core == 0, first * SIDE + second, second * SIDE + first)


def pairs(axis, step):
    out = []
    for dp in range(8):
        core = dp % 2
        for z in range(SIDE):
            for y in range(SIDE):
                along_z = (axis == 0) == (core == 0)
                z2, y2 = ((z + step) % SIDE, y) if along_z else (z, (y + step) % SIDE)
                out.append((dp * 16 + z * SIDE + y, dp * 16 + z2 * SIDE + y2))
    return out


def hop(value, axis, step):
    return lax.ppermute(value, ("dp", "expert"), pairs(axis, step))


def dp_hop(value, move):
    return lax.ppermute(
        value, "dp", [(x * 2 + c, move(x, c)[0] % SIDE * 2 + move(x, c)[1]) for x in range(SIDE) for c in range(2)]
    )


def nt(left, right):
    return lax.dot_general(left, right, (((1,), (1,)), ((), ())), preferred_element_type=F32)


def pack_kernel(tokens, routes, probs, out):
    out[:TOK, :] = tokens[...]
    weights = probs[...].T
    high = weights.astype(BF)
    left = weights - high.astype(F32)
    middle = left.astype(BF)
    low = (left - middle.astype(F32)).astype(BF)
    out[TOK : TOK + 8, :] = jnp.concatenate(
        [routes[...].astype(F32).T.astype(BF), high, middle, low], axis=1
    )
    out[TOK + 8 :, :] = jnp.zeros((8, D), BF)


def pack(tokens, routes, probs):
    return pl.pallas_call(
        pack_kernel,
        out_shape=jax.ShapeDtypeStruct((PACK, D), BF),
        cost_estimate=pl.CostEstimate(flops=0, bytes_accessed=1_100_000, transcendentals=0),
        name="pack",
    )(tokens, routes, probs)


def forward_kernel(chained, perm, *refs):
    xs, (wg, wu), refs = refs[:8], refs[8:10], refs[10 + (3 if chained else 0) :]
    xt, ht, m12, rows = refs
    for i in range(8):
        rows[i * CAP : (i + 1) * CAP, :] = xs[i][0, 0]
    half = 4 * CAP
    pre = []
    for h in range(2):
        saved = rows[h * half : (h + 1) * half, :]
        pre.append(
            (
                jnp.dot(saved, wg[0], preferred_element_type=F32),
                jnp.dot(saved, wu[0], preferred_element_type=F32),
            )
        )
    xt[0] = rows[...].T
    hidden = []
    for h, (gate, up) in enumerate(pre):
        logistic = jax.nn.sigmoid(gate)
        act = gate * logistic
        m12[0, h * half : (h + 1) * half, :HID] = up * (logistic * (1.0 + gate * (1.0 - logistic)))
        m12[0, h * half : (h + 1) * half, HID:] = act
        hidden.append((act * up).astype(BF))
    ht[0] = jnp.concatenate(hidden, axis=0).T


def forward_terms(e, perm, x, wg, wu, carried):
    blocks = x.reshape(2, 16, CAP, D)
    chained = carried is not None

    def block_at(i):
        return pl.BlockSpec((1, 1, CAP, D), lambda h, p: (e, p[8 * h + i], 0, 0))

    half = 8 * CAP
    return pl.pallas_call(
        functools.partial(forward_kernel, chained),
        grid_spec=pltpu.PrefetchScalarGridSpec(
            num_scalar_prefetch=1,
            grid=(2,),
            in_specs=[block_at(i) for i in range(8)]
            + [pl.BlockSpec((1, D, HID), lambda h, p: (e, 0, 0))] * 2
            + [pl.BlockSpec(memory_space=pl.ANY)] * (3 if chained else 0),
            out_specs=[
                pl.BlockSpec((1, D, half), lambda h, p: (e, 0, h)),
                pl.BlockSpec((1, HID, half), lambda h, p: (e, 0, h)),
                pl.BlockSpec((1, half, 2 * HID), lambda h, p: (e, h, 0)),
            ],
            scratch_shapes=[pltpu.VMEM((half, D), BF)],
        ),
        out_shape=[
            jax.ShapeDtypeStruct((2, D, 16 * CAP), BF),
            jax.ShapeDtypeStruct((2, HID, 16 * CAP), BF),
            jax.ShapeDtypeStruct((2, 16 * CAP, 2 * HID), F32),
        ],
        input_output_aliases={11 + i: i for i in range(3)} if chained else {},
        compiler_params=pltpu.CompilerParams(vmem_limit_bytes=VMEM_LIMIT),
        cost_estimate=pl.CostEstimate(flops=2_700_000_000, bytes_accessed=15_000_000, transcendentals=655_360),
        name="forward_terms",
    )(perm, *([blocks] * 8), wg, wu, *(carried or ()))


def groups_kernel(groups, pieces, chained, eid, *refs):
    count, lent = len(groups), sum(len(p) for p in pieces)
    tokens, refs = refs[:lent], refs[lent:]
    m12, wd, wg, wu = refs[:4]
    refs = refs[4 + (2 if chained else 0) :]
    cot, gab, partials, refs = refs[0], refs[1], refs[2 : 2 + 2 * count], refs[2 + 2 * count :]
    tok_v, m12_v, wd_v, wg_v, wu_v, cot_v, gab_v, part_v, onehot, rows, sem_in, sem_out = refs

    loads, token_loads, factor_loads, at = [], [], [], 0

    def load(source, target):
        loads.append(pltpu.make_async_copy(source, target, sem_in.at[len(loads)]))
        loads[-1].start()
        return loads[-1]

    weight_loads = None
    for n, group in enumerate(groups):
        offset, mine = 0, []
        for height in pieces[n]:
            mine.append(load(tokens[at], tok_v.at[n, pl.ds(offset, height)]))
            at, offset = at + 1, offset + height
        token_loads.append(mine)
        if n == 0:
            down_load = load(wd, wd_v)
        factor_loads.append(load(m12.at[:, pl.ds(group * 4 * CAP, 4 * CAP)], m12_v.at[n]))
        if n == 0:
            weight_loads = [load(wg, wg_v), load(wu, wu_v)]

    stores = []

    def store(source, target):
        stores.append(pltpu.make_async_copy(source, target, sem_out.at[len(stores)]))
        stores[-1].start()

    before = (
        lax.broadcasted_iota(jnp.int32, (TOK, TOK), 0) < lax.broadcasted_iota(jnp.int32, (TOK, TOK), 1)
    ).astype(BF)
    slot = lax.broadcasted_iota(jnp.int32, (CAP, TOK), 0).astype(F32)
    for n, group in enumerate(groups):
        for item in token_loads[n]:
            item.wait()
        named, weights = [], []
        for i in range(4):
            meta = tok_v[n, i * PACK + TOK : (i + 1) * PACK, :].astype(F32)[:8]
            routes = meta[:, :TOK]
            probs = meta[:, TOK : 2 * TOK] + meta[:, 2 * TOK : 3 * TOK] + meta[:, 3 * TOK :]
            for k in range(2):
                hit = routes == (eid[0] + k).astype(F32)
                named.append(jnp.sum(jnp.where(hit, 1.0, 0.0), axis=0, keepdims=True))
                weights.append(jnp.sum(jnp.where(hit, probs, 0.0), axis=0, keepdims=True))
        mask = jnp.concatenate(named, axis=0)
        rank = jnp.dot(mask.astype(BF), before, preferred_element_type=F32)
        key = jnp.where(mask > 0.5, rank, -1.0)
        for i in range(4):
            halves, scales = [], []
            for k in range(2):
                hit = slot == key[2 * i + k : 2 * i + k + 1, :]
                halves.append(jnp.where(hit, 1.0, 0.0).astype(BF))
                scales.append(jnp.sum(jnp.where(hit, weights[2 * i + k], 0.0), axis=1, keepdims=True))
            chosen = jnp.concatenate(halves, axis=0)
            onehot[i] = chosen
            taken = jnp.dot(chosen, tok_v[n, i * PACK : i * PACK + TOK, :], preferred_element_type=F32)
            scaled = (taken * jnp.concatenate(scales, axis=0)).astype(BF)
            cot_v[n, 0, i * CAP : (i + 1) * CAP, :] = scaled[:CAP]
            cot_v[n, 1, i * CAP : (i + 1) * CAP, :] = scaled[CAP:]
        place = pl.ds(group * 4 * CAP, 4 * CAP)
        store(cot_v.at[n], cot.at[:, place])
        if n == 0:
            down_load.wait()
        factor_loads[n].wait()
        for e in range(2):
            grad_hidden = nt(cot_v[n, e], wd_v[e])
            gab_v[n, e, :, :HID] = (grad_hidden * m12_v[n, e, :, :HID]).astype(BF)
            gab_v[n, e, :, HID:] = (grad_hidden * m12_v[n, e, :, HID:]).astype(BF)
        store(gab_v.at[n], gab.at[:, place])
        if n == 0:
            for item in weight_loads:
                item.wait()
        for e in range(2):
            row_grads = (nt(gab_v[n, e, :, :HID], wg_v[e]) + nt(gab_v[n, e, :, HID:], wu_v[e])).astype(BF)
            for i in range(4):
                rows[i, e * CAP : (e + 1) * CAP, :] = row_grads[i * CAP : (i + 1) * CAP]
        for i in range(4):
            part_v[n, i * TOK : (i + 1) * TOK, :] = lax.dot_general(
                onehot[i], rows[i], (((0,), (0,)), ((), ())), preferred_element_type=F32
            ).astype(BF)
            if i % 2 == 1:
                store(part_v.at[n, pl.ds((i - 1) * TOK, 2 * TOK)], partials[2 * n + i // 2])
    for item in stores:
        item.wait()


def groups_pass(groups, tokens, eid, m12, wd, wg, wu, carried):
    chained = carried is not None
    count = len(groups)
    pieces = [[t.shape[0] for t in mine] for mine in tokens]
    lent = sum(len(p) for p in pieces)
    anywhere = pl.BlockSpec(memory_space=pl.ANY)
    slots = jax.ShapeDtypeStruct((2, 16 * CAP, D), BF)
    args = [t for mine in tokens for t in mine] + [m12, wd, wg, wu] + (list(carried) if chained else [])
    out = pl.pallas_call(
        functools.partial(groups_kernel, groups, pieces, chained),
        in_specs=[pl.BlockSpec(memory_space=pltpu.SMEM)] + [anywhere] * len(args),
        out_specs=[anywhere] * (2 + 2 * count),
        out_shape=[slots, slots] + [jax.ShapeDtypeStruct((2 * TOK, D), BF)] * (2 * count),
        scratch_shapes=[
            pltpu.VMEM((count, 4 * PACK, D), BF),
            pltpu.VMEM((count, 2, 4 * CAP, 2 * HID), F32),
            pltpu.VMEM((2, HID, D), BF),
            pltpu.VMEM((2, D, HID), BF),
            pltpu.VMEM((2, D, HID), BF),
            pltpu.VMEM((count, 2, 4 * CAP, D), BF),
            pltpu.VMEM((count, 2, 4 * CAP, 2 * HID), BF),
            pltpu.VMEM((count, 4 * TOK, D), BF),
            pltpu.VMEM((4, 2 * CAP, TOK), BF),
            pltpu.VMEM((4, 2 * CAP, D), BF),
            pltpu.SemaphoreType.DMA((lent + 3 + count,)),
            pltpu.SemaphoreType.DMA((4 * count,)),
        ],
        input_output_aliases={lent + 5: 0, lent + 6: 1} if chained else {},
        compiler_params=pltpu.CompilerParams(vmem_limit_bytes=VMEM_LIMIT),
        cost_estimate=pl.CostEstimate(
            flops=2_900_000_000 * count, bytes_accessed=6_000_000 + 9_000_000 * count, transcendentals=0
        ),
        name="groups_" + "".join(str(g) for g in groups),
    )(eid, *args)
    return out[0], out[1], out[2:]


def compress(local_grad, residual):
    carried = local_grad * loss_unscale + residual.astype(F32)
    magnitude = jnp.mean(jnp.abs(carried), axis=-1, keepdims=True) + epsilon
    compressed = (magnitude * jnp.tanh(carried * (1.0 / magnitude))).astype(BF)
    return compressed, (carried - compressed.astype(F32)).astype(BF)


def gate_up_kernel(spot, xt, gab, res_gate, res_up, keep, give, left_gate, left_up, held):
    core = spot[4]
    half = pl.program_id(1)
    grads = [jnp.dot(xt[0, u * 256 : (u + 1) * 256], gab[0], preferred_element_type=F32) for u in range(2)]
    for u in range(2):
        rows = slice(u * 256, (u + 1) * 256)
        at = spot[2 * half + u]
        for m, (res, left) in enumerate(((res_gate, left_gate), (res_up, left_up))):
            held[u, m], left[0, rows] = compress(grads[u][:, m * HID : (m + 1) * HID], res[0, rows])
            keep[at, m, 0] = held[u, m, pl.ds(pl.multiple_of(core * 128, 128), 128)]
            give[at, m, 0] = held[u, m, pl.ds(pl.multiple_of((1 - core) * 128, 128), 128)]


def gate_up_grads(spot, xt, gab, res_gate, res_up):
    tile = pl.BlockSpec((1, HID, HID), lambda e, t, s: (e, t, 0))
    res_shape = jax.ShapeDtypeStruct((2, D, HID), BF)
    blocks = jax.ShapeDtypeStruct((SIDE, 2, 2, 128, HID), BF)
    return pl.pallas_call(
        gate_up_kernel,
        grid_spec=pltpu.PrefetchScalarGridSpec(
            num_scalar_prefetch=1,
            grid=(2, 2),
            in_specs=[
                pl.BlockSpec((1, 512, 16 * CAP), lambda e, t, s: (e, t, 0)),
                pl.BlockSpec((1, 16 * CAP, 2 * HID), lambda e, t, s: (e, 0, 0)),
                tile,
                tile,
            ],
            out_specs=[pl.BlockSpec((SIDE, 2, 1, 128, HID), lambda e, t, s: (0, 0, e, 0, 0))] * 2 + [tile, tile],
            scratch_shapes=[pltpu.VMEM((2, 2, 256, HID), BF)],
        ),
        out_shape=[blocks, blocks, res_shape, res_shape],
        compiler_params=pltpu.CompilerParams(vmem_limit_bytes=VMEM_LIMIT),
        cost_estimate=pl.CostEstimate(flops=5_400_000_000, bytes_accessed=22_000_000, transcendentals=2_000_000),
        name="gate_up_grads",
    )(spot, xt, gab, res_gate, res_up)


def down_kernel(spot, ht, cot, res, keep, give, left):
    core = spot[4]
    grads = [jnp.dot(ht[0, u * 256 : (u + 1) * 256], cot[0], preferred_element_type=F32) for u in range(2)]
    for u in range(2):
        rows = slice(u * 256, (u + 1) * 256)
        compressed, left[0, rows] = compress(grads[u], res[0, rows])
        for own in range(2):

            @pl.when(core == own)
            def _():
                for x in range(SIDE):
                    keep[spot[x], 0, rows] = compressed[:, (2 * x + own) * 128 : (2 * x + own + 1) * 128]
                    give[spot[x], 0, rows] = compressed[:, (2 * x + 1 - own) * 128 : (2 * x + 2 - own) * 128]


def down_grads(spot, ht, cot, res):
    tile = pl.BlockSpec((1, HID, D), lambda e, s: (e, 0, 0))
    blocks = jax.ShapeDtypeStruct((SIDE, 2, HID, 128), BF)
    return pl.pallas_call(
        down_kernel,
        grid_spec=pltpu.PrefetchScalarGridSpec(
            num_scalar_prefetch=1,
            grid=(2,),
            in_specs=[
                pl.BlockSpec((1, HID, 16 * CAP), lambda e, s: (e, 0, 0)),
                pl.BlockSpec((1, 16 * CAP, D), lambda e, s: (e, 0, 0)),
                tile,
            ],
            out_specs=[pl.BlockSpec((SIDE, 1, HID, 128), lambda e, s: (0, e, 0, 0))] * 2 + [tile],
        ),
        out_shape=[blocks, blocks, jax.ShapeDtypeStruct((2, HID, D), BF)],
        compiler_params=pltpu.CompilerParams(vmem_limit_bytes=VMEM_LIMIT),
        cost_estimate=pl.CostEstimate(flops=2_700_000_000, bytes_accessed=14_000_000, transcendentals=1_000_000),
        name="down_grads",
    )(spot, ht, cot, res)


def total(*terms):
    out = terms[0].astype(F32)
    for term in terms[1:]:
        out = out + term.astype(F32)
    return out


def add(*terms):
    return total(*terms).astype(BF)


def mean_over_dp(keep, give):
    got = dp_hop(give, lambda x, c: (x, 1 - c))
    to_minus = dp_hop(add(keep[1], got[1]), lambda x, c: (x - 1, c))
    to_plus = dp_hop(add(keep[2], got[2]), lambda x, c: (x + 1, c))
    to_far = dp_hop(add(keep[3], got[3]), lambda x, c: (x + 2, c))
    return total(keep[0], got[0], to_minus, to_plus, to_far) / 8.0


def on_device(x_saved, d_out, routes, probs, w_gate, w_up, w_down, res_gate, res_up, res_down):
    place = lax.axis_index("expert")
    replica = lax.axis_index("dp")
    x, core = replica // 2, replica % 2
    first = jnp.where(core == 0, place // SIDE, place % SIDE)
    second = jnp.where(core == 0, place % SIDE, place // SIDE)
    offsets = jnp.array(OFFSETS, jnp.int32)
    perm = expert_index(
        core, ((first + offsets) % SIDE)[None, :], ((second + offsets) % SIDE)[:, None]
    ).reshape(-1).astype(jnp.int32)
    where_held = jnp.array([OFFSETS.index(o) for o in (0, 1, 2, -1)], jnp.int32)
    spot = jnp.concatenate([where_held[(jnp.arange(SIDE) - x) % SIDE], core[None]]).astype(jnp.int32)
    eid = (place * 2).astype(jnp.int32).reshape(1)

    own = pack(d_out, routes, probs)
    rest = jnp.concatenate([hop(own, 0, 1), hop(own, 0, -1), hop(own, 0, 2)], axis=0)
    own1, own2 = hop(own, 1, 1), hop(own, 1, -1)
    rest1, rest2 = hop(rest, 1, 1), hop(rest, 1, -1)
    group3 = (
        hop(jnp.concatenate([own1, rest1[:PACK]], axis=0), 1, 1),
        hop(rest2[PACK:], 1, -1),
    )

    terms = forward_terms(0, perm, x_saved[0], w_gate, w_up, None)
    xt, ht, m12 = forward_terms(1, perm, x_saved[0], w_gate, w_up, terms)

    run = functools.partial(groups_pass, eid=eid, m12=m12, wd=w_down, wg=w_gate, wu=w_up)
    cot, gab, (part0a, part0b) = run((0,), [(own, rest)], carried=None)
    cot, gab, (part1a, part1b, part2a, part2b) = run(
        (1, 2), [(own1, rest1), (own2, rest2)], carried=(cot, gab)
    )
    cot, gab, (part3a, part3b) = run((3,), [group3], carried=(cot, gab))

    direct_plus, direct_minus = hop(part2b, 1, 1), hop(part1a, 1, -1)
    over_plus, over_minus = hop(part3a, 1, 1), hop(part3b, 1, -1)
    late_plus, late_minus = hop(add(part2a, over_plus), 1, 1), hop(add(part1b, over_minus), 1, -1)

    def column(i):
        part = slice(i % 2 * TOK, (i % 2 + 1) * TOK)
        terms = (part0a, late_plus, direct_minus) if i < 2 else (part0b, direct_plus, late_minus)
        return total(*(t[part] for t in terms))

    d_tokens = add(
        column(0),
        hop(column(2).astype(BF), 0, 1),
        hop(column(1).astype(BF), 0, -1),
        hop(column(3).astype(BF), 0, 2),
    )

    keep, give, left_gate, left_up = gate_up_grads(spot, xt, gab, res_gate[0], res_up[0])
    mean = mean_over_dp(keep, give)
    keep, give, left_down = down_grads(spot, ht, cot, res_down[0])
    mean_down = mean_over_dp(keep, give)
    return (d_tokens, mean[0], mean[1], mean_down, left_gate[None], left_up[None], left_down[None])


def solution(mesh):
    in_specs = (
        P("dp", "expert", None, None),
        P(("dp", "expert"), None),
        P(("dp", "expert"), None),
        P(("dp", "expert"), None),
        P("expert", None, None),
        P("expert", None, None),
        P("expert", None, None),
        P("dp", "expert", None, None),
        P("dp", "expert", None, None),
        P("dp", "expert", None, None),
    )
    out_specs = (
        P(("dp", "expert"), None),
        P("expert", "dp", None),
        P("expert", "dp", None),
        P("expert", None, "dp"),
        P("dp", "expert", None, None),
        P("dp", "expert", None, None),
        P("dp", "expert", None, None),
    )
    return jax.shard_map(
        on_device, mesh=mesh, in_specs=in_specs, out_specs=out_specs, check_vma=False
    )
```

time: 247 us -> 188 us (0.76)
  blocking collectives: 44.3 us -> 0 us
  between operations: 14.3 us -> 0.9 us
  Pallas kernels: 78 us -> 69.2 us
  starting transfers between devices: 26 us -> 34.3 us
  local copies, waits for them, and re-layouts: 12.3 us -> 9.08 us
  other arithmetic: 5.43 us -> 7.99 us
    all_gather x1 -> x0, blocking collectives: 44.3 us -> none  [on_device(): lax.all_gather(jnp.concatenate([routes.astype(F32).T, probs.T], axis=0),...]
    ppermute x0 -> x8, waiting for transfers between devices: none -> 11.9 us  [dp_hop(): lax.ppermute(value, 'dp', [(x * 2 + c, move(x, c)[0] % SIDE * 2 + move(x,...]
    ppermute x16 -> x18, waiting for transfers between devices: 66.2 us -> 54.7 us  [hop(): return lax.ppermute(value, ('dp', 'expert'), pairs(axis, step))]
    ppermute x0 -> x8, starting transfers between devices: none -> 10.8 us  [dp_hop(): lax.ppermute(value, 'dp', [(x * 2 + c, move(x, c)[0] % SIDE * 2 + move(x,...]
    pallas_call x8, Pallas kernels: 78 us -> 69.2 us  [the longest x3 27.6 us: groups_pass(): pl.pallas_call(functools.partial(groups_kernel, groups, pieces, chained),...]
    ppermute x16 -> x18, starting transfers between devices: 26 us -> 23.5 us  [hop(): return lax.ppermute(value, ('dp', 'expert'), pairs(axis, step))]
    unnamed x24 -> x32, local copies, waits for them, and re-layouts: 7.13 us -> 4.71 us
  transfers between devices with their start and end apart: 17 -> 26, of which waited for: 9 -> 12; matrix products, arithmetic and copies ran while one was open for 4% -> 6% of each run, Pallas kernels for 18% -> 27%
where the time goes in v2:
time: 188 us
  Pallas kernels  69.2 us (37%)
  waiting for transfers between devices  66.6 us (35%)
  starting transfers between devices  34.3 us (18%)
  local copies, waits for them, and re-layouts  9.08 us (5%)
  other arithmetic  7.99 us (4%)
    ppermute x18, waiting for transfers between devices, hop(): return lax.ppermute(value, ('dp', 'expert'), pairs(axis, step))  54.7 us
    pallas_call x3, Pallas kernels, groups_pass(): pl.pallas_call(functools.partial(groups_kernel, groups, pieces, chained),...  27.6 us
    ppermute x18, starting transfers between devices, hop(): return lax.ppermute(value, ('dp', 'expert'), pairs(axis, step))  23.5 us
    pallas_call x2, Pallas kernels, forward_terms(): pl.pallas_call(functools.partial(forward_kernel, chained), grid_spec=pltp...  16.9 us
    pallas_call x1, Pallas kernels, gate_up_grads(): pl.pallas_call(gate_up_kernel, grid_spec=pltpu.PrefetchScalarGridSpec(num...  13.6 us
    ppermute x8, waiting for transfers between devices, dp_hop(): lax.ppermute(value, 'dp', [(x * 2 + c, move(x, c)[0] % SIDE * 2 + move(x,...  11.9 us
    ppermute x8, starting transfers between devices, dp_hop(): lax.ppermute(value, 'dp', [(x * 2 + c, move(x, c)[0] % SIDE * 2 + move(x,...  10.8 us
    pallas_call x1, Pallas kernels, down_grads(): pl.pallas_call(down_kernel, grid_spec=pltpu.PrefetchScalarGridSpec(num_sc...  9.04 us
  transfers between devices with their start and end apart: 26, of which 12 were waited for; matrix products, arithmetic and copies ran while one was open for 6% of the time, Pallas kernels for 27%

profile of v2, /device:TPU:0, one launch (start us, length us, event | category | flops | bytes accessed | tf_op | source)
XLA Modules:
  0.0 188.0 jit_solution(12391020869158745431)
XLA Ops:
  3.6 2.1 %pack.1.refs_0_ = bf16[272,1024]{1,0:T(8,128)(2,1)} custom-call(bf16[256,1024]{1,0:T(8,128)(2,1)} %tokens.1, s32[256,8]{1,0:T(8,128)} %copy.28.routes, f32[256,8]{1,0:T(8,128)} %copy.29.probs), custom_call_target="tpu_custom_call" | custom-call | bytes 1100000 | tf_op jit(solution)/shard_map/pack/pallas_call | solution.py:69
  5.7 2.0 %collective-permute-start = (bf16[272,1024]{1,0:T(8,128)(2,1)}, bf16[272,1024]{1,0:T(8,128)(2,1)S(1)}, u32[]{:S(2)}, u32[]{:S(2)}) collective-permute-start(bf16[272,1024]{1,0:T(8,128)(2,1)} %pack.1.refs_0_), channel_id=1, source_target_pairs={{0,4},{1,5},{2,6},{3,7},{4,8},{5,9},{6,10},{7,11},{8,12},{9,13},{1... | collective-permute-start | bytes 1671176 | tf_op jit(solution)/shard_map/ppermute | solution.py:42
  7.7 2.1 %collective-permute-start.1 = (bf16[272,1024]{1,0:T(8,128)(2,1)}, bf16[272,1024]{1,0:T(8,128)(2,1)S(1)}, u32[]{:S(2)}, u32[]{:S(2)}) collective-permute-start(bf16[272,1024]{1,0:T(8,128)(2,1)} %pack.1.refs_0_), channel_id=1, source_target_pairs={{0,12},{1,13},{2,14},{3,15},{4,0},{5,1},{6,2},{7,3},{8,4},{9,5},{1... | collective-permute-start | bytes 1671176 | tf_op jit(solution)/shard_map/ppermute | solution.py:42
  9.8 1.9 collective-permute-start.2
  11.7 5.9 %collective-permute-done = bf16[272,1024]{1,0:T(8,128)(2,1)S(1)} collective-permute-done((bf16[272,1024]{1,0:T(8,128)(2,1)}, bf16[272,1024]{1,0:T(8,128)(2,1)S(1)}, u32[]{:S(2)}, u32[]{:S(2)}) %collective-permute-start) | collective-permute-done | bytes 557088 | tf_op jit(solution)/shard_map/ppermute | solution.py:42
  18.3 4.8 %collective-permute-done.1 = bf16[272,1024]{1,0:T(8,128)(2,1)S(1)} collective-permute-done((bf16[272,1024]{1,0:T(8,128)(2,1)}, bf16[272,1024]{1,0:T(8,128)(2,1)S(1)}, u32[]{:S(2)}, u32[]{:S(2)}) %collective-permute-start.1) | collective-permute-done | bytes 557088 | tf_op jit(solution)/shard_map/ppermute | solution.py:42
  27.4 1.7 collective-permute-start.6
  29.4 2.9 %collective-permute-start.5 = (bf16[272,1024]{1,0:T(8,128)(2,1)}, bf16[272,1024]{1,0:T(8,128)(2,1)}, u32[]{:S(2)}, u32[]{:S(2)}) collective-permute-start(bf16[272,1024]{1,0:T(8,128)(2,1)} %pack.1.refs_0_), channel_id=1, source_target_pairs={{0,3},{1,0},{2,1},{3,2},{4,7},{5,4},{6,5},{7,6},{8,11},{9,8},{10,9... | collective-permute-start | bytes 1671176 | tf_op jit(solution)/shard_map/ppermute | solution.py:42
  33.6 8.5 %forward_terms.2 = (bf16[2,1024,1280]{2,1,0:T(8,128)(2,1)}, bf16[2,512,1280]{2,1,0:T(8,128)(2,1)}, f32[2,1280,1024]{2,1,0:T(8,128)}) custom-call(s32[16]{0:T(128)} %select_n.79.perm, bf16[2,16,80,1024]{3,2,1,0:T(8,128)(2,1)} %bitcast.43, bf16[2,16,80,1024]{3,2,1,0:T(8,128)(2,1)} %bitcast.44, bf16[2,16,80,1024]{3,2,1,0:T(8,128)(2,1)} %bitcast.45, ...), custom_call_target="tpu_custom_call" | custom-call | flops 2700000000 | bytes 15000000 | tf_op jit(solution)/shard_map/forward_terms/pallas_call | solution.py:111
  42.1 6.6 %collective-permute-done.4.refs_1_ = bf16[816,1024]{1,0:T(8,128)(2,1)S(1)} collective-permute-done((bf16[816,1024]{1,0:T(8,128)(2,1)}, bf16[816,1024]{1,0:T(8,128)(2,1)S(1)}, u32[]{:S(2)}, u32[]{:S(2)}) %collective-permute-start.4) | collective-permute-done | bytes 1671200 | tf_op jit(solution)/shard_map/ppermute | solution.py:42
  48.7 6.0 %collective-permute-done.3.refs_0_ = bf16[272,1024]{1,0:T(8,128)(2,1)} collective-permute-done((bf16[272,1024]{1,0:T(8,128)(2,1)}, bf16[272,1024]{1,0:T(8,128)(2,1)}, u32[]{:S(2)}, u32[]{:S(2)}) %collective-permute-start.3) | collective-permute-done | bytes 557088 | tf_op jit(solution)/shard_map/ppermute | solution.py:42
  54.7 2.2 %pad_maximum_fusion = bf16[544,1024]{1,0:T(8,128)(2,1)} fusion(bf16[272,1024]{1,0:T(8,128)(2,1)S(1)} %slice.130, bf16[272,1024]{1,0:T(8,128)(2,1)} %collective-permute-done.3.refs_0_), kind=kLoop, calls=%fused_computation.3 | loop fusion | flops 2228224 | bytes 2228224 | tf_op jit(solution)/shard_map/concatenate | solution.py:387
  58.5 2.9 %collective-permute-start.8 = (bf16[544,1024]{1,0:T(8,128)(2,1)}, bf16[544,1024]{1,0:T(8,128)(2,1)}, u32[]{:S(2)}, u32[]{:S(2)}) collective-permute-start(bf16[544,1024]{1,0:T(8,128)(2,1)} %slice.131), channel_id=1, source_target_pairs={{0,3},{1,0},{2,1},{3,2},{4,7},{5,4},{6,5},{7,6},{8,11},{9,8},{10,9... | collective-permute-start | bytes 3342344 | tf_op jit(solution)/shard_map/ppermute | solution.py:42
  61.9 8.4 %forward_terms.3 = (bf16[2,1024,1280]{2,1,0:T(8,128)(2,1)}, bf16[2,512,1280]{2,1,0:T(8,128)(2,1)}, f32[2,1280,1024]{2,1,0:T(8,128)}) custom-call(s32[16]{0:T(128)} %select_n.79.perm, bf16[2,16,80,1024]{3,2,1,0:T(8,128)(2,1)} %bitcast.51, bf16[2,16,80,1024]{3,2,1,0:T(8,128)(2,1)} %bitcast.52, ...), custom_call_target="tpu_custom_call", output_to_operand_aliasing={{0}: (11, {}), {1}: (12, {}), {2}: (13, {})} | custom-call | flops 2700000000 | bytes 15000000 | tf_op jit(solution)/shard_map/forward_terms/pallas_call | solution.py:111
  70.4 8.0 %groups_0.1 = (bf16[2,1280,1024]{2,1,0:T(8,128)(2,1)}, bf16[2,1280,1024]{2,1,0:T(8,128)(2,1)}, bf16[512,1024]{1,0:T(8,128)(2,1)}, bf16[512,1024]{1,0:T(8,128)(2,1)}) custom-call(s32[1]{0:T(128)} %bitcast.eid, bf16[272,1024]{1,0:T(8,128)(2,1)} %pack.1.refs_0_, bf16[816,1024]{1,0:T(8,128)(2,1)} %constant_dynamic-update-slice_fusion.refs_1_, ...), custom_call_target="tpu_custom_call" | custom-call | flops 2900000000 | bytes 15000000 | tf_op jit(solution)/shard_map/groups_0/pallas_call | solution.py:238
  78.4 11.5 %groups_12.1 = (bf16[2,1280,1024]{2,1,0:T(8,128)(2,1)}, bf16[2,1280,1024]{2,1,0:T(8,128)(2,1)}, bf16[512,1024]{1,0:T(8,128)(2,1)}, bf16[512,1024]{1,0:T(8,128)(2...) custom-call(s32[1]{0:T(128)} %bitcast.eid, ...), custom_call_target="tpu_custom_call", output_to_operand_aliasing={{0}: (9, {}), {1}: (10, {})} | custom-call | flops 5800000000 | bytes 24000000 | tf_op jit(solution)/shard_map/groups_12/pallas_call | solution.py:238
  89.9 8.2 %groups_3.1 = (bf16[2,1280,1024]{2,1,0:T(8,128)(2,1)}, bf16[2,1280,1024]{2,1,0:T(8,128)(2,1)}, bf16[512,1024]{1,0:T(8,128)(2,1)}, bf16[512,1024]{1,0:T(8,128)(2,1)}) custom-call(s32[1]{0:T(128)} %bitcast.eid, bf16[544,1024]{1,0:T(8,128)(2,1)} %collective-permute-done.7.refs_0_, ...), custom_call_target="tpu_custom_call", output_to_operand_aliasing={{0}: (7, {}), {1}: (8, {})} | custom-call | flops 2900000000 | bytes 15000000 | tf_op jit(solution)/shard_map/groups_3/pallas_call | solution.py:238
  98.1 9.0 %down_grads.1 = (bf16[4,2,512,128]{3,2,1,0:T(8,128)(2,1)}, bf16[4,2,512,128]{3,2,1,0:T(8,128)(2,1)}, bf16[2,512,1024]{2,1,0:T(8,128)(2,1)}) custom-call(s32[5]{0:T(128)} %pad_add_fusion.spot, bf16[2,512,1280]{2,1,0:T(8,128)(2,1)} %get-tuple-element.54.ht, bf16[2,1280,1024]{2,1,0:T(8,128)(2,1)} %get-tuple-element.55.cot, bf16[2,512,1024]{2,1,0:T(8,128)(2,1)} %bitcast.59), custom_call_target="tpu_custom_call" | custom-call | flops 2700000000 | bytes 14000000 | tf_op jit(solution)/shard_map/down_grads/pallas_call | solution.py:330
  107.2 13.6 %gate_up_grads.1 = (bf16[4,2,2,128,512]{4,3,2,1,0:T(8,128)(2,1)}, bf16[4,2,2,128,512]{4,3,2,1,0:T(8,128)(2,1)}, bf16[2,1024,512]{2,1,0:T(8,128)(2,1)}, bf16[2,1024,512]{2,1,0:T(8,128)(2,1)}) custom-call(s32[5]{0:T(128)} %pad_add_fusion.spot, bf16[2,1024,1280]{2,1,0:T(8,128)(2,1)} %get-tuple-element.50.xt, bf16[2,1280,1024]{2,1,0:T(8,128)(2,1)} %get-tuple-element.51.gab, ...), custom_call_target="tpu_custom_call" | custom-call | flops 5400000000 | bytes 22000000 | tf_op jit(solution)/shard_map/gate_up_grads/pallas_call | solution.py:291
  122.5 1.7 collective-permute-start.13
  124.5 2.8 %collective-permute-start.23 = (bf16[2,512,128]{2,1,0:T(8,128)(2,1)S(1)}, bf16[2,512,128]{2,1,0:T(8,128)(2,1)S(1)}, u32[]{:S(2)}, u32[]{:S(2)}) collective-permute-start(bf16[2,512,128]{2,1,0:T(8,128)(2,1)S(1)} %get-tuple-element.70), channel_id=1, source_target_pairs={{0,96},{16,112},{32,0},{48,16},{64,32},{80,48},{96,64},{112,80},{1... | collective-permute-start | bytes 786440 | tf_op jit(solution)/shard_map/ppermute | solution.py:46
  127.8 9.5 %collective-permute-done.13 = bf16[512,1024]{1,0:T(8,128)(2,1)S(1)} collective-permute-done((bf16[512,1024]{1,0:T(8,128)(2,1)S(1)}, bf16[512,1024]{1,0:T(8,128)(2,1)S(1)}, u32[]{:S(2)}, u32[]{:S(2)}) %collective-permute-start.13) | collective-permute-done | bytes 1048608 | tf_op jit(solution)/shard_map/ppermute | solution.py:42
  137.3 3.0 %collective-permute-start.25 = (bf16[2,512,128]{2,1,0:T(8,128)(2,1)S(1)}, bf16[2,512,128]{2,1,0:T(8,128)(2,1)S(1)}, u32[]{:S(2)}, u32[]{:S(2)}) collective-permute-start(bf16[2,512,128]{2,1,0:T(8,128)(2,1)S(1)} %get-tuple-element.71), channel_id=1, source_target_pairs={{0,64},{16,80},{32,96},{48,112},{64,0},{80,16},{96,32},{112,48},{1... | collective-permute-start | bytes 786440 | tf_op jit(solution)/shard_map/ppermute | solution.py:46
  142.0 4.3 %collective-permute-done.25 = bf16[2,512,128]{2,1,0:T(8,128)(2,1)S(1)} collective-permute-done((bf16[2,512,128]{2,1,0:T(8,128)(2,1)S(1)}, bf16[2,512,128]{2,1,0:T(8,128)(2,1)S(1)}, u32[]{:S(2)}, u32[]{:S(2)}) %collective-permute-start.25) | collective-permute-done | bytes 262176 | tf_op jit(solution)/shard_map/ppermute | solution.py:46
  146.2 2.2 %collective-permute-start.14 = (bf16[512,1024]{1,0:T(8,128)(2,1)S(1)}, bf16[512,1024]{1,0:T(8,128)(2,1)S(1)}, u32[]{:S(2)}, u32[]{:S(2)}) collective-permute-start(bf16[512,1024]{1,0:T(8,128)(2,1)S(1)} %add_convert_fusion), channel_id=1, source_target_pairs={{0,3},{1,0},{2,1},{3,2},{4,7},{5,4},{6,5},{7,6},{8,11},{9,8},{10,9... | collective-permute-start | bytes 3145736 | tf_op jit(solution)/shard_map/ppermute | solution.py:42
  149.9 2.8 %collective-permute-start.19 = (bf16[2,2,128,512]{3,2,1,0:T(8,128)(2,1)S(1)}, bf16[2,2,128,512]{3,2,1,0:T(8,128)(2,1)S(1)}, u32[]{:S(2)}, u32[]{:S(2)}) collective-permute-start(bf16[2,2,128,512]{3,2,1,0:T(8,128)(2,1)S(1)} %get-tuple-element.65), channel_id=1, source_target_pairs={{0,96},{16,112},{32,0},{48,16},{64,32},{80,48},{96,64},{112,80},{1... | collective-permute-start | bytes 1572872 | tf_op jit(solution)/shard_map/ppermute | solution.py:46
  152.8 3.6 %collective-permute-done.10 = bf16[512,1024]{1,0:T(8,128)(2,1)S(1)} collective-permute-done((bf16[512,1024]{1,0:T(8,128)(2,1)S(1)}, bf16[512,1024]{1,0:T(8,128)(2,1)S(1)}, u32[]{:S(2)}, u32[]{:S(2)}) %collective-permute-start.10) | collective-permute-done | bytes 1048608 | tf_op jit(solution)/shard_map/ppermute | solution.py:42
  157.1 10.4 %collective-permute-done.12 = bf16[512,1024]{1,0:T(8,128)(2,1)S(1)} collective-permute-done((bf16[512,1024]{1,0:T(8,128)(2,1)S(1)}, bf16[512,1024]{1,0:T(8,128)(2,1)S(1)}, u32[]{:S(2)}, u32[]{:S(2)}) %collective-permute-start.12) | collective-permute-done | bytes 1048608 | tf_op jit(solution)/shard_map/ppermute | solution.py:42
  167.5 2.3 %collective-permute-start.16 = (bf16[256,1024]{1,0:T(8,128)(2,1)S(1)}, bf16[256,1024]{1,0:T(8,128)(2,1)S(1)}, u32[]{:S(2)}, u32[]{:S(2)}) collective-permute-start(bf16[256,1024]{1,0:T(8,128)(2,1)S(1)} %add_convert_fusion.7), channel_id=1, source_target_pairs={{0,12},{1,13},{2,14},{3,15},{4,0},{5,1},{6,2},{7,3},{8,4},{9,5},{1... | collective-permute-start | bytes 1572872 | tf_op jit(solution)/shard_map/ppermute | solution.py:42
  170.6 4.2 %collective-permute-done.19 = bf16[2,2,128,512]{3,2,1,0:T(8,128)(2,1)S(1)} collective-permute-done((bf16[2,2,128,512]{3,2,1,0:T(8,128)(2,1)S(1)}, bf16[2,2,128,512]{3,2,1,0:T(8,128)(2,1)S(1)}, u32[]{:S(2)}, u32[]{:S(2)}) %collective-permute-start.19) | collective-permute-done | bytes 524320 | tf_op jit(solution)/shard_map/ppermute | solution.py:46
  174.8 3.4 %collective-permute-done.20 = bf16[2,2,128,512]{3,2,1,0:T(8,128)(2,1)S(1)} collective-permute-done((bf16[2,2,128,512]{3,2,1,0:T(8,128)(2,1)S(1)}, bf16[2,2,128,512]{3,2,1,0:T(8,128)(2,1)S(1)}, u32[]{:S(2)}, u32[]{:S(2)}) %collective-permute-start.20) | collective-permute-done | bytes 524320 | tf_op jit(solution)/shard_map/ppermute | solution.py:46
  179.6 7.0 %collective-permute-done.15 = bf16[256,1024]{1,0:T(8,128)(2,1)S(1)} collective-permute-done((bf16[256,1024]{1,0:T(8,128)(2,1)S(1)}, bf16[256,1024]{1,0:T(8,128)(2,1)S(1)}, u32[]{:S(2)}, u32[]{:S(2)}) %collective-permute-start.15) | collective-permute-done | bytes 524320 | tf_op jit(solution)/shard_map/ppermute | solution.py:42
  (81 shorter events, 21.8 us)
Async XLA Ops:
  3.6 28.7 %copy-start.9 = (s32[4]{0:T(128)S(1)}, s32[4]{0:T(128)}, u32[]{:S(2)}) copy-start(s32[4]{0:T(128)} %constant.87.clone) | copy-start | bytes 52
  3.6 29.4 %copy-start = (s32[4]{0:T(128)S(1)}, s32[4]{0:T(128)}, u32[]{:S(2)}) copy-start(s32[4]{0:T(128)} %constant.88.clone) | copy-start | bytes 52
  5.7 11.8 %collective-permute-start = (bf16[272,1024]{1,0:T(8,128)(2,1)}, bf16[272,1024]{1,0:T(8,128)(2,1)S(1)}, u32[]{:S(2)}, u32[]{:S(2)}) collective-permute-start(bf16[272,1024]{1,0:T(8,128)(2,1)} %pack.1.refs_0_), channel_id=1, source_target_pairs={{0,4},{1,5},{2,6},{3,7},{4,8},{5,9},{6,10},{7,11},{8,12},{9,13},{1... | collective-permute-start | bytes 1671176 | tf_op jit(solution)/shard_map/ppermute | solution.py:42
  7.7 15.5 %collective-permute-start.1 = (bf16[272,1024]{1,0:T(8,128)(2,1)}, bf16[272,1024]{1,0:T(8,128)(2,1)S(1)}, u32[]{:S(2)}, u32[]{:S(2)}) collective-permute-start(bf16[272,1024]{1,0:T(8,128)(2,1)} %pack.1.refs_0_), channel_id=1, source_target_pairs={{0,12},{1,13},{2,14},{3,15},{4,0},{5,1},{6,2},{7,3},{8,4},{9,5},{1... | collective-permute-start | bytes 1671176 | tf_op jit(solution)/shard_map/ppermute | solution.py:42
  9.8 15.1 %collective-permute-start.2 = (bf16[272,1024]{1,0:T(8,128)(2,1)}, bf16[272,1024]{1,0:T(8,128)(2,1)S(1)}, u32[]{:S(2)}, u32[]{:S(2)}) collective-permute-start(bf16[272,1024]{1,0:T(8,128)(2,1)} %pack.1.refs_0_), channel_id=1, source_target_pairs={{0,8},{1,9},{2,10},{3,11},{4,12},{5,13},{6,14},{7,15},{8,0},{9,1},... | collective-permute-start | bytes 1671176 | tf_op jit(solution)/shard_map/ppermute | solution.py:42
  25.8 22.9 %collective-permute-start.4 = (bf16[816,1024]{1,0:T(8,128)(2,1)}, bf16[816,1024]{1,0:T(8,128)(2,1)S(1)}, u32[]{:S(2)}, u32[]{:S(2)}) collective-permute-start(bf16[816,1024]{1,0:T(8,128)(2,1)} %constant_dynamic-update-slice_fusion.refs_1_), channel_id=1, source_target_pairs={{0,1},{1,2},{2,3},{3,0},{4,5},{5,6},{6,7},{7,4},{8,9},{9,10},{10,1... | collective-permute-start | bytes 5013512 | tf_op jit(solution)/shard_map/ppermute | solution.py:42
  27.4 29.9 %collective-permute-start.6 = (bf16[816,1024]{1,0:T(8,128)(2,1)}, bf16[816,1024]{1,0:T(8,128)(2,1)S(1)}, u32[]{:S(2)}, u32[]{:S(2)}) collective-permute-start(bf16[816,1024]{1,0:T(8,128)(2,1)} %constant_dynamic-update-slice_fusion.refs_1_), channel_id=1, source_target_pairs={{0,3},{1,0},{2,1},{3,2},{4,7},{5,4},{6,5},{7,6},{8,11},{9,8},{10,9... | collective-permute-start | bytes 5013512 | tf_op jit(solution)/shard_map/ppermute | solution.py:42
  29.0 25.7 %collective-permute-start.3 = (bf16[272,1024]{1,0:T(8,128)(2,1)}, bf16[272,1024]{1,0:T(8,128)(2,1)}, u32[]{:S(2)}, u32[]{:S(2)}) collective-permute-start(bf16[272,1024]{1,0:T(8,128)(2,1)} %pack.1.refs_0_), channel_id=1, source_target_pairs={{0,1},{1,2},{2,3},{3,0},{4,5},{5,6},{6,7},{7,4},{8,9},{9,10},{10,1... | collective-permute-start | bytes 1671176 | tf_op jit(solution)/shard_map/ppermute | solution.py:42
  29.4 49.0 %collective-permute-start.5 = (bf16[272,1024]{1,0:T(8,128)(2,1)}, bf16[272,1024]{1,0:T(8,128)(2,1)}, u32[]{:S(2)}, u32[]{:S(2)}) collective-permute-start(bf16[272,1024]{1,0:T(8,128)(2,1)} %pack.1.refs_0_), channel_id=1, source_target_pairs={{0,3},{1,0},{2,1},{3,2},{4,7},{5,4},{6,5},{7,6},{8,11},{9,8},{10,9... | collective-permute-start | bytes 1671176 | tf_op jit(solution)/shard_map/ppermute | solution.py:42
  56.9 33.0 %collective-permute-start.7 = (bf16[544,1024]{1,0:T(8,128)(2,1)}, bf16[544,1024]{1,0:T(8,128)(2,1)}, u32[]{:S(2)}, u32[]{:S(2)}) collective-permute-start(bf16[544,1024]{1,0:T(8,128)(2,1)} %pad_maximum_fusion), channel_id=1, source_target_pairs={{0,1},{1,2},{2,3},{3,0},{4,5},{5,6},{6,7},{7,4},{8,9},{9,10},{10,1... | collective-permute-start | bytes 3342344 | tf_op jit(solution)/shard_map/ppermute | solution.py:42
  58.5 31.4 %collective-permute-start.8 = (bf16[544,1024]{1,0:T(8,128)(2,1)}, bf16[544,1024]{1,0:T(8,128)(2,1)}, u32[]{:S(2)}, u32[]{:S(2)}) collective-permute-start(bf16[544,1024]{1,0:T(8,128)(2,1)} %slice.131), channel_id=1, source_target_pairs={{0,3},{1,0},{2,1},{3,2},{4,7},{5,4},{6,5},{7,6},{8,11},{9,8},{10,9... | collective-permute-start | bytes 3342344 | tf_op jit(solution)/shard_map/ppermute | solution.py:42
  107.1 17.2 %collective-permute-start.22 = (bf16[4,2,512,128]{3,2,1,0:T(8,128)(2,1)}, bf16[4,2,512,128]{3,2,1,0:T(8,128)(2,1)S(1)}, u32[]{:S(2)}, u32[]{:S(2)}) collective-permute-start(bf16[4,2,512,128]{3,2,1,0:T(8,128)(2,1)} %get-tuple-element.57), channel_id=1, source_target_pairs={{0,16},{16,0},{32,48},{48,32},{64,80},{80,64},{96,112},{112,96},{1... | collective-permute-start | bytes 3145736 | tf_op jit(solution)/shard_map/ppermute | solution.py:46
  107.1 20.3 %collective-permute-start.9 = (bf16[512,1024]{1,0:T(8,128)(2,1)S(1)}, bf16[512,1024]{1,0:T(8,128)(2,1)S(1)}, u32[]{:S(2)}, u32[]{:S(2)}) collective-permute-start(bf16[512,1024]{1,0:T(8,128)(2,1)S(1)} %copy-done.13), channel_id=1, source_target_pairs={{0,1},{1,2},{2,3},{3,0},{4,5},{5,6},{6,7},{7,4},{8,9},{9,10},{10,1... | collective-permute-start | bytes 3145736 | tf_op jit(solution)/shard_map/ppermute | solution.py:42
  107.2 17.0 %copy-start.11 = (bf16[512,1024]{1,0:T(8,128)(2,1)S(1)}, bf16[512,1024]{1,0:T(8,128)(2,1)}, u32[]{:S(2)}) copy-start(bf16[512,1024]{1,0:T(8,128)(2,1)} %get-tuple-element.45) | copy-start | bytes 3145732
  107.2 17.1 %copy-start.7 = (bf16[4,2,512,128]{3,2,1,0:T(8,128)(2,1)S(1)}, bf16[4,2,512,128]{3,2,1,0:T(8,128)(2,1)}, u32[]{:S(2)}) copy-start(bf16[4,2,512,128]{3,2,1,0:T(8,128)(2,1)} %get-tuple-element.56) | copy-start | bytes 3145732
  120.8 28.6 %collective-permute-start.18 = (bf16[4,2,2,128,512]{4,3,2,1,0:T(8,128)(2,1)}, bf16[4,2,2,128,512]{4,3,2,1,0:T(8,128)(2,1)S(1)}, u32[]{:S(2)}, u32[]{:S(2)}) collective-permute-start(bf16[4,2,2,128,512]{4,3,2,1,0:T(8,128)(2,1)} %get-tuple-element.53), channel_id=1, source_target_pairs={{0,16},{16,0},{32,48},{48,32},{64,80},{80,64},{96,112},{112,96},{1... | collective-permute-start | bytes 6291464 | tf_op jit(solution)/shard_map/ppermute | solution.py:46
  122.5 14.8 %collective-permute-start.13 = (bf16[512,1024]{1,0:T(8,128)(2,1)S(1)}, bf16[512,1024]{1,0:T(8,128)(2,1)S(1)}, u32[]{:S(2)}, u32[]{:S(2)}) collective-permute-start(bf16[512,1024]{1,0:T(8,128)(2,1)S(1)} %copy-done.12), channel_id=1, source_target_pairs={{0,3},{1,0},{2,1},{3,2},{4,7},{5,4},{6,5},{7,6},{8,11},{9,8},{10,9... | collective-permute-start | bytes 3145736 | tf_op jit(solution)/shard_map/ppermute | solution.py:42
  124.2 28.5 %collective-permute-start.11 = (bf16[512,1024]{1,0:T(8,128)(2,1)S(1)}, bf16[512,1024]{1,0:T(8,128)(2,1)S(1)}, u32[]{:S(2)}, u32[]{:S(2)}) collective-permute-start(bf16[512,1024]{1,0:T(8,128)(2,1)S(1)} %copy-done.11), channel_id=1, source_target_pairs={{0,3},{1,0},{2,1},{3,2},{4,7},{5,4},{6,5},{7,6},{8,11},{9,8},{10,9... | collective-permute-start | bytes 3145736 | tf_op jit(solution)/shard_map/ppermute | solution.py:42
  124.5 15.8 %copy-start.4 = (bf16[512,1024]{1,0:T(8,128)(2,1)S(1)}, bf16[512,1024]{1,0:T(8,128)(2,1)}, u32[]{:S(2)}) copy-start(bf16[512,1024]{1,0:T(8,128)(2,1)} %get-tuple-element.48) | copy-start | bytes 3145732
  124.5 15.8 %collective-permute-start.23 = (bf16[2,512,128]{2,1,0:T(8,128)(2,1)S(1)}, bf16[2,512,128]{2,1,0:T(8,128)(2,1)S(1)}, u32[]{:S(2)}, u32[]{:S(2)}) collective-permute-start(bf16[2,512,128]{2,1,0:T(8,128)(2,1)S(1)} %get-tuple-element.70), channel_id=1, source_target_pairs={{0,96},{16,112},{32,0},{48,16},{64,32},{80,48},{96,64},{112,80},{1... | collective-permute-start | bytes 786440 | tf_op jit(solution)/shard_map/ppermute | solution.py:46
  127.4 13.4 %collective-permute-start.24 = (bf16[2,512,128]{2,1,0:T(8,128)(2,1)S(1)}, bf16[2,512,128]{2,1,0:T(8,128)(2,1)S(1)}, u32[]{:S(2)}, u32[]{:S(2)}) collective-permute-start(bf16[2,512,128]{2,1,0:T(8,128)(2,1)S(1)} %get-tuple-element.72), channel_id=1, source_target_pairs={{0,32},{16,48},{32,64},{48,80},{64,96},{80,112},{96,0},{112,16},{1... | collective-permute-start | bytes 786440 | tf_op jit(solution)/shard_map/ppermute | solution.py:46
  137.3 8.9 %collective-permute-start.25 = (bf16[2,512,128]{2,1,0:T(8,128)(2,1)S(1)}, bf16[2,512,128]{2,1,0:T(8,128)(2,1)S(1)}, u32[]{:S(2)}, u32[]{:S(2)}) collective-permute-start(bf16[2,512,128]{2,1,0:T(8,128)(2,1)S(1)} %get-tuple-element.71), channel_id=1, source_target_pairs={{0,64},{16,80},{32,96},{48,112},{64,0},{80,16},{96,32},{112,48},{1... | collective-permute-start | bytes 786440 | tf_op jit(solution)/shard_map/ppermute | solution.py:46
  140.3 16.0 %collective-permute-start.10 = (bf16[512,1024]{1,0:T(8,128)(2,1)S(1)}, bf16[512,1024]{1,0:T(8,128)(2,1)S(1)}, u32[]{:S(2)}, u32[]{:S(2)}) collective-permute-start(bf16[512,1024]{1,0:T(8,128)(2,1)S(1)} %add_convert_fusion.1), channel_id=1, source_target_pairs={{0,1},{1,2},{2,3},{3,0},{4,5},{5,6},{6,7},{7,4},{8,9},{9,10},{10,1... | collective-permute-start | bytes 3145736 | tf_op jit(solution)/shard_map/ppermute | solution.py:42
  140.8 26.8 %collective-permute-start.12 = (bf16[512,1024]{1,0:T(8,128)(2,1)S(1)}, bf16[512,1024]{1,0:T(8,128)(2,1)S(1)}, u32[]{:S(2)}, u32[]{:S(2)}) collective-permute-start(bf16[512,1024]{1,0:T(8,128)(2,1)S(1)} %copy-done.10), channel_id=1, source_target_pairs={{0,1},{1,2},{2,3},{3,0},{4,5},{5,6},{6,7},{7,4},{8,9},{9,10},{10,1... | collective-permute-start | bytes 3145736 | tf_op jit(solution)/shard_map/ppermute | solution.py:42
  146.2 23.7 %collective-permute-start.14 = (bf16[512,1024]{1,0:T(8,128)(2,1)S(1)}, bf16[512,1024]{1,0:T(8,128)(2,1)S(1)}, u32[]{:S(2)}, u32[]{:S(2)}) collective-permute-start(bf16[512,1024]{1,0:T(8,128)(2,1)S(1)} %add_convert_fusion), channel_id=1, source_target_pairs={{0,3},{1,0},{2,1},{3,2},{4,7},{5,4},{6,5},{7,6},{8,11},{9,8},{10,9... | collective-permute-start | bytes 3145736 | tf_op jit(solution)/shard_map/ppermute | solution.py:42
  149.9 20.0 %copy-start.8 = (bf16[512,1024]{1,0:T(8,128)(2,1)S(1)}, bf16[512,1024]{1,0:T(8,128)(2,1)}, u32[]{:S(2)}) copy-start(bf16[512,1024]{1,0:T(8,128)(2,1)} %get-tuple-element.46) | copy-start | bytes 3145732
  149.9 24.9 %collective-permute-start.19 = (bf16[2,2,128,512]{3,2,1,0:T(8,128)(2,1)S(1)}, bf16[2,2,128,512]{3,2,1,0:T(8,128)(2,1)S(1)}, u32[]{:S(2)}, u32[]{:S(2)}) collective-permute-start(bf16[2,2,128,512]{3,2,1,0:T(8,128)(2,1)S(1)} %get-tuple-element.65), channel_id=1, source_target_pairs={{0,96},{16,112},{32,0},{48,16},{64,32},{80,48},{96,64},{112,80},{1... | collective-permute-start | bytes 1572872 | tf_op jit(solution)/shard_map/ppermute | solution.py:46
  152.8 25.5 %collective-permute-start.20 = (bf16[2,2,128,512]{3,2,1,0:T(8,128)(2,1)S(1)}, bf16[2,2,128,512]{3,2,1,0:T(8,128)(2,1)S(1)}, u32[]{:S(2)}, u32[]{:S(2)}) collective-permute-start(bf16[2,2,128,512]{3,2,1,0:T(8,128)(2,1)S(1)} %get-tuple-element.67), channel_id=1, source_target_pairs={{0,32},{16,48},{32,64},{48,80},{64,96},{80,112},{96,0},{112,16},{1... | collective-permute-start | bytes 1572872 | tf_op jit(solution)/shard_map/ppermute | solution.py:46
  156.3 21.9 %collective-permute-start.21 = (bf16[2,2,128,512]{3,2,1,0:T(8,128)(2,1)S(1)}, bf16[2,2,128,512]{3,2,1,0:T(8,128)(2,1)S(1)}, u32[]{:S(2)}, u32[]{:S(2)}) collective-permute-start(bf16[2,2,128,512]{3,2,1,0:T(8,128)(2,1)S(1)} %get-tuple-element.66), channel_id=1, source_target_pairs={{0,64},{16,80},{32,96},{48,112},{64,0},{80,16},{96,32},{112,48},{1... | collective-permute-start | bytes 1572872 | tf_op jit(solution)/shard_map/ppermute | solution.py:46
  167.5 12.1 %collective-permute-start.16 = (bf16[256,1024]{1,0:T(8,128)(2,1)S(1)}, bf16[256,1024]{1,0:T(8,128)(2,1)S(1)}, u32[]{:S(2)}, u32[]{:S(2)}) collective-permute-start(bf16[256,1024]{1,0:T(8,128)(2,1)S(1)} %add_convert_fusion.7), channel_id=1, source_target_pairs={{0,12},{1,13},{2,14},{3,15},{4,0},{5,1},{6,2},{7,3},{8,4},{9,5},{1... | collective-permute-start | bytes 1572872 | tf_op jit(solution)/shard_map/ppermute | solution.py:42
  170.5 16.1 %collective-permute-start.15 = (bf16[256,1024]{1,0:T(8,128)(2,1)S(1)}, bf16[256,1024]{1,0:T(8,128)(2,1)S(1)}, u32[]{:S(2)}, u32[]{:S(2)}) collective-permute-start(bf16[256,1024]{1,0:T(8,128)(2,1)S(1)} %get-tuple-element.68), channel_id=1, source_target_pairs={{0,4},{1,5},{2,6},{3,7},{4,8},{5,9},{6,10},{7,11},{8,12},{9,13},{1... | collective-permute-start | bytes 1572872 | tf_op jit(solution)/shard_map/ppermute | solution.py:42
  174.8 11.8 %collective-permute-start.17 = (bf16[256,1024]{1,0:T(8,128)(2,1)S(1)}, bf16[256,1024]{1,0:T(8,128)(2,1)S(1)}, u32[]{:S(2)}, u32[]{:S(2)}) collective-permute-start(bf16[256,1024]{1,0:T(8,128)(2,1)S(1)} %get-tuple-element.69), channel_id=1, source_target_pairs={{0,8},{1,9},{2,10},{3,11},{4,12},{5,13},{6,14},{7,15},{8,0},{9,1},... | collective-permute-start | bytes 1572872 | tf_op jit(solution)/shard_map/ppermute | solution.py:42
  (8 other events, 83.3 us)

commit v3 on v2

--- a/solution.py
+++ b/solution.py
@@ -54,13 +54,13 @@
 
 def pack_kernel(tokens, routes, probs, out):
     out[:TOK, :] = tokens[...]
-    weights = probs[...].T
+    weights = probs[...]
     high = weights.astype(BF)
     left = weights - high.astype(F32)
     middle = left.astype(BF)
     low = (left - middle.astype(F32)).astype(BF)
     out[TOK : TOK + 8, :] = jnp.concatenate(
-        [routes[...].astype(F32).T.astype(BF), high, middle, low], axis=1
+        [routes[...].astype(F32).astype(BF), high, middle, low], axis=1
     )
     out[TOK + 8 :, :] = jnp.zeros((8, D), BF)
 
@@ -71,7 +71,7 @@
         out_shape=jax.ShapeDtypeStruct((PACK, D), BF),
         cost_estimate=pl.CostEstimate(flops=0, bytes_accessed=1_100_000, transcendentals=0),
         name="pack",
-    )(tokens, routes, probs)
+    )(tokens, routes.T, probs.T)
 
 
 def forward_kernel(chained, perm, *refs):
@@ -380,27 +380,33 @@
     eid = (place * 2).astype(jnp.int32).reshape(1)
 
     own = pack(d_out, routes, probs)
-    rest = jnp.concatenate([hop(own, 0, 1), hop(own, 0, -1), hop(own, 0, 2)], axis=0)
-    own1, own2 = hop(own, 1, 1), hop(own, 1, -1)
-    rest1, rest2 = hop(rest, 1, 1), hop(rest, 1, -1)
-    group3 = (
-        hop(jnp.concatenate([own1, rest1[:PACK]], axis=0), 1, 1),
-        hop(rest2[PACK:], 1, -1),
-    )
-
+    near = (hop(own, 0, 1), hop(own, 0, -1), hop(own, 0, 2))
     terms = forward_terms(0, perm, x_saved[0], w_gate, w_up, None)
+    near, terms = lax.optimization_barrier((near, terms))
+    group0 = jnp.concatenate([own, *near], axis=0)
+    group1, group2 = hop(group0, 1, 1), hop(group0, 1, -1)
     xt, ht, m12 = forward_terms(1, perm, x_saved[0], w_gate, w_up, terms)
 
     run = functools.partial(groups_pass, eid=eid, m12=m12, wd=w_down, wg=w_gate, wu=w_up)
-    cot, gab, (part0a, part0b) = run((0,), [(own, rest)], carried=None)
+    cot, gab, (part0a, part0b) = run((0,), [(group0,)], carried=None)
+    group1, group2, cot = lax.optimization_barrier((group1, group2, cot))
+    group3 = (hop(group1[: 2 * PACK], 1, 1), hop(group2[2 * PACK :], 1, -1))
     cot, gab, (part1a, part1b, part2a, part2b) = run(
-        (1, 2), [(own1, rest1), (own2, rest2)], carried=(cot, gab)
+        (1, 2), [(group1,), (group2,)], carried=(cot, gab)
     )
     cot, gab, (part3a, part3b) = run((3,), [group3], carried=(cot, gab))
 
     direct_plus, direct_minus = hop(part2b, 1, 1), hop(part1a, 1, -1)
     over_plus, over_minus = hop(part3a, 1, 1), hop(part3b, 1, -1)
+    keep, give, left_gate, left_up = gate_up_grads(spot, xt, gab, res_gate[0], res_up[0])
+    over_plus, over_minus, direct_plus, direct_minus, give = lax.optimization_barrier(
+        (over_plus, over_minus, direct_plus, direct_minus, give)
+    )
+    mean = mean_over_dp(keep, give)
     late_plus, late_minus = hop(add(part2a, over_plus), 1, 1), hop(add(part1b, over_minus), 1, -1)
+    keep, give, left_down = down_grads(spot, ht, cot, res_down[0])
+    late_plus, late_minus, give = lax.optimization_barrier((late_plus, late_minus, give))
+    mean_down = mean_over_dp(keep, give)
 
     def column(i):
         part = slice(i % 2 * TOK, (i % 2 + 1) * TOK)
@@ -413,11 +419,6 @@
         hop(column(1).astype(BF), 0, -1),
         hop(column(3).astype(BF), 0, 2),
     )
-
-    keep, give, left_gate, left_up = gate_up_grads(spot, xt, gab, res_gate[0], res_up[0])
-    mean = mean_over_dp(keep, give)
-    keep, give, left_down = down_grads(spot, ht, cot, res_down[0])
-    mean_down = mean_over_dp(keep, give)
     return (d_tokens, mean[0], mean[1], mean_down, left_gate[None], left_up[None], left_down[None])
 
 

time: 188 us -> 168 us (0.89)
  waiting for transfers between devices: 66.6 us -> 45.9 us
    ppermute x18 -> x16, waiting for transfers between devices: 54.7 us -> 27.5 us  [hop(): return lax.ppermute(value, ('dp', 'expert'), pairs(axis, step))]
    ppermute x8, waiting for transfers between devices: 11.9 us -> 18.3 us  [dp_hop(): lax.ppermute(value, 'dp', [(x * 2 + c, move(x, c)[0] % SIDE * 2 + move(x,...]
    unnamed x32 -> x28, local copies, waits for them, and re-layouts: 4.71 us -> 2.91 us
    ppermute x18 -> x16, starting transfers between devices: 23.5 us -> 24.1 us  [hop(): return lax.ppermute(value, ('dp', 'expert'), pairs(axis, step))]
  transfers between devices with their start and end apart: 26 -> 24, of which waited for: 12 -> 10; matrix products, arithmetic and copies ran while one was open for 6% -> 6% of each run, Pallas kernels for 27% -> 40%
where the time goes in v3:
time: 168 us; the launch traced here: 167 us
  Pallas kernels  68.8 us (41%)
  waiting for transfers between devices  45.9 us (27%)
  starting transfers between devices  34.9 us (21%)
  other arithmetic  9.2 us (5%)
  local copies, waits for them, and re-layouts  7.82 us (5%)
    ppermute x16, waiting for transfers between devices, hop(): return lax.ppermute(value, ('dp', 'expert'), pairs(axis, step))  27.5 us
    pallas_call x3, Pallas kernels, groups_pass(): pl.pallas_call(functools.partial(groups_kernel, groups, pieces, chained),...  27.4 us
    ppermute x16, starting transfers between devices, hop(): return lax.ppermute(value, ('dp', 'expert'), pairs(axis, step))  24.1 us
    ppermute x8, waiting for transfers between devices, dp_hop(): lax.ppermute(value, 'dp', [(x * 2 + c, move(x, c)[0] % SIDE * 2 + move(x,...  18.3 us
    pallas_call x2, Pallas kernels, forward_terms(): pl.pallas_call(functools.partial(forward_kernel, chained), grid_spec=pltp...  17 us
    pallas_call x1, Pallas kernels, gate_up_grads(): pl.pallas_call(gate_up_kernel, grid_spec=pltpu.PrefetchScalarGridSpec(num...  13.5 us
    ppermute x8, starting transfers between devices, dp_hop(): lax.ppermute(value, 'dp', [(x * 2 + c, move(x, c)[0] % SIDE * 2 + move(x,...  10.7 us
    pallas_call x1, Pallas kernels, down_grads(): pl.pallas_call(down_kernel, grid_spec=pltpu.PrefetchScalarGridSpec(num_sc...  9.01 us
  transfers between devices with their start and end apart: 24, of which 10 were waited for; matrix products, arithmetic and copies ran while one was open for 6% of the time, Pallas kernels for 40%

profile of v3, /device:TPU:0, one launch (start us, length us, event | category | flops | bytes accessed | tf_op | source)
XLA Modules:
  0.0 167.4 jit_solution(14352288019949953337)
XLA Ops:
  0.6 1.9 %pack.1 = bf16[272,1024]{1,0:T(8,128)(2,1)} custom-call(bf16[256,1024]{1,0:T(8,128)(2,1)} %tokens.1, s32[8,256]{1,0:T(8,128)} %bitcast.61, f32[8,256]{1,0:T(8,128)} %bitcast.62), custom_call_target="tpu_custom_call" | custom-call | bytes 1100000 | tf_op jit(solution)/shard_map/pack/pallas_call | solution.py:69
  2.5 2.0 %collective-permute-start = (bf16[272,1024]{1,0:T(8,128)(2,1)}, bf16[272,1024]{1,0:T(8,128)(2,1)S(1)}, u32[]{:S(2)}, u32[]{:S(2)}) collective-permute-start(bf16[272,1024]{1,0:T(8,128)(2,1)} %pack.1), channel_id=1, source_target_pairs={{0,4},{1,5},{2,6},{3,7},{4,8},{5,9},{6,10},{7,11},{8,12},{9,13},{1... | collective-permute-start | bytes 1671176 | tf_op jit(solution)/shard_map/ppermute | solution.py:42
  4.5 2.1 %collective-permute-start.1 = (bf16[272,1024]{1,0:T(8,128)(2,1)}, bf16[272,1024]{1,0:T(8,128)(2,1)S(1)}, u32[]{:S(2)}, u32[]{:S(2)}) collective-permute-start(bf16[272,1024]{1,0:T(8,128)(2,1)} %pack.1), channel_id=1, source_target_pairs={{0,12},{1,13},{2,14},{3,15},{4,0},{5,1},{6,2},{7,3},{8,4},{9,5},{1... | collective-permute-start | bytes 1671176 | tf_op jit(solution)/shard_map/ppermute | solution.py:42
  6.7 1.9 %collective-permute-start.2 = (bf16[272,1024]{1,0:T(8,128)(2,1)}, bf16[272,1024]{1,0:T(8,128)(2,1)S(1)}, u32[]{:S(2)}, u32[]{:S(2)}) collective-permute-start(bf16[272,1024]{1,0:T(8,128)(2,1)} %pack.1), channel_id=1, source_target_pairs={{0,8},{1,9},{2,10},{3,11},{4,12},{5,13},{6,14},{7,15},{8,0},{9,1},... | collective-permute-start | bytes 1671176 | tf_op jit(solution)/shard_map/ppermute | solution.py:42
  9.9 8.6 %forward_terms.2 = (bf16[2,1024,1280]{2,1,0:T(8,128)(2,1)}, bf16[2,512,1280]{2,1,0:T(8,128)(2,1)}, f32[2,1280,1024]{2,1,0:T(8,128)}) custom-call(s32[16]{0:T(128)} %select_n.79.perm, bf16[2,16,80,1024]{3,2,1,0:T(8,128)(2,1)} %bitcast.45, bf16[2,16,80,1024]{3,2,1,0:T(8,128)(2,1)} %bitcast.46, bf16[2,16,80,1024]{3,2,1,0:T(8,128)(2,1)} %bitcast.47, ...), custom_call_target="tpu_custom_call" | custom-call | flops 2700000000 | bytes 15000000 | tf_op jit(solution)/shard_map/forward_terms/pallas_call | solution.py:111
  18.4 1.6 collective-permute-done.1
  20.0 1.8 %collective-permute-done.2 = bf16[272,1024]{1,0:T(8,128)(2,1)S(1)} collective-permute-done((bf16[272,1024]{1,0:T(8,128)(2,1)}, bf16[272,1024]{1,0:T(8,128)(2,1)S(1)}, u32[]{:S(2)}, u32[]{:S(2)}) %collective-permute-start.2) | collective-permute-done | bytes 557088 | tf_op jit(solution)/shard_map/ppermute | solution.py:42
  23.9 1.6 collective-permute-start.3
  25.5 1.7 collective-permute-start.4
  27.2 8.4 %forward_terms.3 = (bf16[2,1024,1280]{2,1,0:T(8,128)(2,1)}, bf16[2,512,1280]{2,1,0:T(8,128)(2,1)}, f32[2,1280,1024]{2,1,0:T(8,128)}) custom-call(s32[16]{0:T(128)} %select_n.79.perm, bf16[2,16,80,1024]{3,2,1,0:T(8,128)(2,1)} %bitcast.53, bf16[2,16,80,1024]{3,2,1,0:T(8,128)(2,1)} %bitcast.54, ...), custom_call_target="tpu_custom_call", output_to_operand_aliasing={{0}: (11, {}), {1}: (12, {}), {2}: (13, {})} | custom-call | flops 2700000000 | bytes 15000000 | tf_op jit(solution)/shard_map/forward_terms/pallas_call | solution.py:111
  35.6 8.0 %groups_0.1 = (bf16[2,1280,1024]{2,1,0:T(8,128)(2,1)}, bf16[2,1280,1024]{2,1,0:T(8,128)(2,1)}, bf16[512,1024]{1,0:T(8,128)(2,1)}, bf16[512,1024]{1,0:T(8,128)(2,1)}) custom-call(s32[1]{0:T(128)} %bitcast.eid, bf16[1088,1024]{1,0:T(8,128)(2,1)} %copy-done.1, f32[2,1280,1024]{2,1,0:T(8,128)} %get-tuple-element.60.refs_1_.refs_2_, ...), custom_call_target="tpu_custom_call" | custom-call | flops 2900000000 | bytes 15000000 | tf_op jit(solution)/shard_map/groups_0/pallas_call | solution.py:238
  43.6 9.1 %collective-permute-done.3.refs_0_ = bf16[1088,1024]{1,0:T(8,128)(2,1)} collective-permute-done((bf16[1088,1024]{1,0:T(8,128)(2,1)S(1)}, bf16[1088,1024]{1,0:T(8,128)(2,1)}, u32[]{:S(2)}, u32[]{:S(2)}) %collective-permute-start.3) | collective-permute-done | bytes 2228256 | tf_op jit(solution)/shard_map/ppermute | solution.py:42
  54.4 1.6 collective-permute-start.5
  57.4 1.9 %collective-permute-start.6 = (bf16[544,1024]{1,0:T(8,128)(2,1)S(1)}, bf16[544,1024]{1,0:T(8,128)(2,1)S(1)}, u32[]{:S(2)}, u32[]{:S(2)}) collective-permute-start(bf16[544,1024]{1,0:T(8,128)(2,1)S(1)} %slice.98), channel_id=1, source_target_pairs={{0,3},{1,0},{2,1},{3,2},{4,7},{5,4},{6,5},{7,6},{8,11},{9,8},{10,9... | collective-permute-start | bytes 3342344 | tf_op jit(solution)/shard_map/ppermute | solution.py:42
  59.3 11.5 %groups_12.1 = (bf16[2,1280,1024]{2,1,0:T(8,128)(2,1)}, bf16[2,1280,1024]{2,1,0:T(8,128)(2,1)}, bf16[512,1024]{1,0:T(8,128)(2,1)}, bf16[512,1024]{1,0:T(8,128)(2...) custom-call(s32[1]{0:T(128)} %bitcast.eid, ...), custom_call_target="tpu_custom_call", output_to_operand_aliasing={{0}: (7, {}), {1}: (8, {})} | custom-call | flops 5800000000 | bytes 24000000 | tf_op jit(solution)/shard_map/groups_12/pallas_call | solution.py:238
  70.8 1.7 %collective-permute-start.10 = (bf16[512,1024]{1,0:T(8,128)(2,1)}, bf16[512,1024]{1,0:T(8,128)(2,1)S(1)}, u32[]{:S(2)}, u32[]{:S(2)}) collective-permute-start(bf16[512,1024]{1,0:T(8,128)(2,1)} %get-tuple-element.73), channel_id=1, source_target_pairs={{0,3},{1,0},{2,1},{3,2},{4,7},{5,4},{6,5},{7,6},{8,11},{9,8},{10,9... | collective-permute-start | bytes 3145736 | tf_op jit(solution)/shard_map/ppermute | solution.py:42
  74.2 8.0 %groups_3.1 = (bf16[2,1280,1024]{2,1,0:T(8,128)(2,1)}, bf16[2,1280,1024]{2,1,0:T(8,128)(2,1)}, bf16[512,1024]{1,0:T(8,128)(2,1)}, bf16[512,1024]{1,0:T(8,128)(2,1)}) custom-call(s32[1]{0:T(128)} %bitcast.eid, bf16[544,1024]{1,0:T(8,128)(2,1)} %copy-done.4, bf16[544,1024]{1,0:T(8,128)(2,1)} %copy-done.5, ...), custom_call_target="tpu_custom_call", output_to_operand_aliasing={{0}: (7, {}), {1}: (8, {})} | custom-call | flops 2900000000 | bytes 15000000 | tf_op jit(solution)/shard_map/groups_3/pallas_call | solution.py:238
  83.4 2.1 %collective-permute-start.8 = (bf16[512,1024]{1,0:T(8,128)(2,1)}, bf16[512,1024]{1,0:T(8,128)(2,1)S(1)}, u32[]{:S(2)}, u32[]{:S(2)}) collective-permute-start(bf16[512,1024]{1,0:T(8,128)(2,1)} %get-tuple-element.71), channel_id=1, source_target_pairs={{0,3},{1,0},{2,1},{3,2},{4,7},{5,4},{6,5},{7,6},{8,11},{9,8},{10,9... | collective-permute-start | bytes 3145736 | tf_op jit(solution)/shard_map/ppermute | solution.py:42
  86.8 13.5 %gate_up_grads.1 = (bf16[4,2,2,128,512]{4,3,2,1,0:T(8,128)(2,1)}, bf16[4,2,2,128,512]{4,3,2,1,0:T(8,128)(2,1)}, bf16[2,1024,512]{2,1,0:T(8,128)(2,1)}, bf16[2,1024,512]{2,1,0:T(8,128)(2,1)}) custom-call(s32[5]{0:T(128)} %pad_add_fusion.spot, bf16[2,1024,1280]{2,1,0:T(8,128)(2,1)} %get-tuple-element.74.xt, bf16[2,1280,1024]{2,1,0:T(8,128)(2,1)} %get-tuple-element.75.gab, ...), custom_call_target="tpu_custom_call" | custom-call | flops 5400000000 | bytes 22000000 | tf_op jit(solution)/shard_map/gate_up_grads/pallas_call | solution.py:291
  100.7 1.7 %collective-permute-start.12 = (bf16[512,1024]{1,0:T(8,128)(2,1)S(1)}, bf16[512,1024]{1,0:T(8,128)(2,1)}, u32[]{:S(2)}, u32[]{:S(2)}) collective-permute-start(bf16[512,1024]{1,0:T(8,128)(2,1)S(1)} %add_convert_fusion), channel_id=1, source_target_pairs={{0,3},{1,0},{2,1},{3,2},{4,7},{5,4},{6,5},{7,6},{8,11},{9,8},{10,9... | collective-permute-start | bytes 3145736 | tf_op jit(solution)/shard_map/ppermute | solution.py:42
  103.3 9.0 %down_grads.1 = (bf16[4,2,512,128]{3,2,1,0:T(8,128)(2,1)}, bf16[4,2,512,128]{3,2,1,0:T(8,128)(2,1)}, bf16[2,512,1024]{2,1,0:T(8,128)(2,1)}) custom-call(s32[5]{0:T(128)} %pad_add_fusion.spot, bf16[2,512,1280]{2,1,0:T(8,128)(2,1)} %get-tuple-element.80.ht, bf16[2,1280,1024]{2,1,0:T(8,128)(2,1)} %get-tuple-element.81.cot, bf16[2,512,1024]{2,1,0:T(8,128)(2,1)} %bitcast.65), custom_call_target="tpu_custom_call" | custom-call | flops 2700000000 | bytes 14000000 | tf_op jit(solution)/shard_map/down_grads/pallas_call | solution.py:330
  112.3 3.4 %collective-permute-done.12 = bf16[512,1024]{1,0:T(8,128)(2,1)} collective-permute-done((bf16[512,1024]{1,0:T(8,128)(2,1)S(1)}, bf16[512,1024]{1,0:T(8,128)(2,1)}, u32[]{:S(2)}, u32[]{:S(2)}) %collective-permute-start.12) | collective-permute-done | bytes 1048608 | tf_op jit(solution)/shard_map/ppermute | solution.py:42
  115.7 3.2 %collective-permute-done.11 = bf16[512,1024]{1,0:T(8,128)(2,1)S(1)} collective-permute-done((bf16[512,1024]{1,0:T(8,128)(2,1)S(1)}, bf16[512,1024]{1,0:T(8,128)(2,1)S(1)}, u32[]{:S(2)}, u32[]{:S(2)}) %collective-permute-start.11) | collective-permute-done | bytes 1048608 | tf_op jit(solution)/shard_map/ppermute | solution.py:42
  120.2 1.9 %collective-permute-start.14 = (bf16[256,1024]{1,0:T(8,128)(2,1)S(1)}, bf16[256,1024]{1,0:T(8,128)(2,1)S(1)}, u32[]{:S(2)}, u32[]{:S(2)}) collective-permute-start(bf16[256,1024]{1,0:T(8,128)(2,1)S(1)} %add_convert_fusion.7), channel_id=1, source_target_pairs={{0,12},{1,13},{2,14},{3,15},{4,0},{5,1},{6,2},{7,3},{8,4},{9,5},{1... | collective-permute-start | bytes 1572872 | tf_op jit(solution)/shard_map/ppermute | solution.py:42
  122.0 2.1 %add_convert_fusion.8 = (bf16[256,1024]{1,0:T(8,128)(2,1)S(1)}, bf16[256,1024]{1,0:T(8,128)(2,1)S(1)}) fusion(bf16[512,1024]{1,0:T(8,128)(2,1)} %collective-permute-done.12, bf16[512,1024]{1,0:T(8,128)(2,1)} %collective-permute-done.9, bf16[512,1024]{1,0:T(8,128)(2,1)S(1)} %copy-done.12), kind=kLoop, calls=%fused_computation.14 | loop fusion | flops 3145728 | bytes 4194304 | tf_op jit(solution)/shard_map/convert_element_type | solution.py:418
  126.3 2.8 %collective-permute-start.21 = (bf16[2,512,128]{2,1,0:T(8,128)(2,1)S(1)}, bf16[2,512,128]{2,1,0:T(8,128)(2,1)S(1)}, u32[]{:S(2)}, u32[]{:S(2)}) collective-permute-start(bf16[2,512,128]{2,1,0:T(8,128)(2,1)S(1)} %get-tuple-element.104), channel_id=1, source_target_pairs={{0,96},{16,112},{32,0},{48,16},{64,32},{80,48},{96,64},{112,80},{1... | collective-permute-start | bytes 786440 | tf_op jit(solution)/shard_map/ppermute | solution.py:46
  129.6 2.8 %collective-permute-start.23 = (bf16[2,512,128]{2,1,0:T(8,128)(2,1)S(1)}, bf16[2,512,128]{2,1,0:T(8,128)(2,1)S(1)}, u32[]{:S(2)}, u32[]{:S(2)}) collective-permute-start(bf16[2,512,128]{2,1,0:T(8,128)(2,1)S(1)} %get-tuple-element.105), channel_id=1, source_target_pairs={{0,64},{16,80},{32,96},{48,112},{64,0},{80,16},{96,32},{112,48},{1... | collective-permute-start | bytes 786440 | tf_op jit(solution)/shard_map/ppermute | solution.py:46
  132.5 7.8 %collective-permute-done.13 = bf16[256,1024]{1,0:T(8,128)(2,1)S(1)} collective-permute-done((bf16[256,1024]{1,0:T(8,128)(2,1)S(1)}, bf16[256,1024]{1,0:T(8,128)(2,1)S(1)}, u32[]{:S(2)}, u32[]{:S(2)}) %collective-permute-start.13) | collective-permute-done | bytes 524320 | tf_op jit(solution)/shard_map/ppermute | solution.py:42
  140.3 2.8 %collective-permute-start.17 = (bf16[2,2,128,512]{3,2,1,0:T(8,128)(2,1)S(1)}, bf16[2,2,128,512]{3,2,1,0:T(8,128)(2,1)S(1)}, u32[]{:S(2)}, u32[]{:S(2)}) collective-permute-start(bf16[2,2,128,512]{3,2,1,0:T(8,128)(2,1)S(1)} %get-tuple-element.99), channel_id=1, source_target_pairs={{0,96},{16,112},{32,0},{48,16},{64,32},{80,48},{96,64},{112,80},{1... | collective-permute-start | bytes 1572872 | tf_op jit(solution)/shard_map/ppermute | solution.py:46
  143.0 2.3 %collective-permute-start.19 = (bf16[2,2,128,512]{3,2,1,0:T(8,128)(2,1)S(1)}, bf16[2,2,128,512]{3,2,1,0:T(8,128)(2,1)S(1)}, u32[]{:S(2)}, u32[]{:S(2)}) collective-permute-start(bf16[2,2,128,512]{3,2,1,0:T(8,128)(2,1)S(1)} %get-tuple-element.100), channel_id=1, source_target_pairs={{0,64},{16,80},{32,96},{48,112},{64,0},{80,16},{96,32},{112,48},{1... | collective-permute-start | bytes 1572872 | tf_op jit(solution)/shard_map/ppermute | solution.py:46
  147.7 14.9 %collective-permute-done.17 = bf16[2,2,128,512]{3,2,1,0:T(8,128)(2,1)S(1)} collective-permute-done((bf16[2,2,128,512]{3,2,1,0:T(8,128)(2,1)S(1)}, bf16[2,2,128,512]{3,2,1,0:T(8,128)(2,1)S(1)}, u32[]{:S(2)}, u32[]{:S(2)}) %collective-permute-start.17) | collective-permute-done | bytes 524320 | tf_op jit(solution)/shard_map/ppermute | solution.py:46
  162.7 3.4 %collective-permute-done.18 = bf16[2,2,128,512]{3,2,1,0:T(8,128)(2,1)S(1)} collective-permute-done((bf16[2,2,128,512]{3,2,1,0:T(8,128)(2,1)S(1)}, bf16[2,2,128,512]{3,2,1,0:T(8,128)(2,1)S(1)}, u32[]{:S(2)}, u32[]{:S(2)}) %collective-permute-start.18) | collective-permute-done | bytes 524320 | tf_op jit(solution)/shard_map/ppermute | solution.py:46
  (72 shorter events, 19.4 us)
Async XLA Ops:
  2.5 15.9 %collective-permute-start = (bf16[272,1024]{1,0:T(8,128)(2,1)}, bf16[272,1024]{1,0:T(8,128)(2,1)S(1)}, u32[]{:S(2)}, u32[]{:S(2)}) collective-permute-start(bf16[272,1024]{1,0:T(8,128)(2,1)} %pack.1), channel_id=1, source_target_pairs={{0,4},{1,5},{2,6},{3,7},{4,8},{5,9},{6,10},{7,11},{8,12},{9,13},{1... | collective-permute-start | bytes 1671176 | tf_op jit(solution)/shard_map/ppermute | solution.py:42
  4.5 15.5 %collective-permute-start.1 = (bf16[272,1024]{1,0:T(8,128)(2,1)}, bf16[272,1024]{1,0:T(8,128)(2,1)S(1)}, u32[]{:S(2)}, u32[]{:S(2)}) collective-permute-start(bf16[272,1024]{1,0:T(8,128)(2,1)} %pack.1), channel_id=1, source_target_pairs={{0,12},{1,13},{2,14},{3,15},{4,0},{5,1},{6,2},{7,3},{8,4},{9,5},{1... | collective-permute-start | bytes 1671176 | tf_op jit(solution)/shard_map/ppermute | solution.py:42
  6.7 15.1 %collective-permute-start.2 = (bf16[272,1024]{1,0:T(8,128)(2,1)}, bf16[272,1024]{1,0:T(8,128)(2,1)S(1)}, u32[]{:S(2)}, u32[]{:S(2)}) collective-permute-start(bf16[272,1024]{1,0:T(8,128)(2,1)} %pack.1), channel_id=1, source_target_pairs={{0,8},{1,9},{2,10},{3,11},{4,12},{5,13},{6,14},{7,15},{8,0},{9,1},... | collective-permute-start | bytes 1671176 | tf_op jit(solution)/shard_map/ppermute | solution.py:42
  9.9 12.8 %copy-start.2 = (bf16[272,1024]{1,0:T(8,128)(2,1)S(1)}, bf16[272,1024]{1,0:T(8,128)(2,1)}, u32[]{:S(2)}) copy-start(bf16[272,1024]{1,0:T(8,128)(2,1)} %pack.1) | copy-start | bytes 1671172
  23.9 11.7 %copy-start.1 = (bf16[1088,1024]{1,0:T(8,128)(2,1)}, bf16[1088,1024]{1,0:T(8,128)(2,1)S(1)}, u32[]{:S(2)}) copy-start(bf16[1088,1024]{1,0:T(8,128)(2,1)S(1)} %pad_maximum_fusion.refs_0_) | copy-start | bytes 6684676
  23.9 28.8 %collective-permute-start.3 = (bf16[1088,1024]{1,0:T(8,128)(2,1)S(1)}, bf16[1088,1024]{1,0:T(8,128)(2,1)}, u32[]{:S(2)}, u32[]{:S(2)}) collective-permute-start(bf16[1088,1024]{1,0:T(8,128)(2,1)S(1)} %pad_maximum_fusion.refs_0_), channel_id=1, source_target_pairs={{0,1},{1,2},{2,3},{3,0},{4,5},{5,6},{6,7},{7,4},{8,9},{9,10},{10,1... | collective-permute-start | bytes 6684680 | tf_op jit(solution)/shard_map/ppermute | solution.py:42
  25.5 27.5 %collective-permute-start.4 = (bf16[1088,1024]{1,0:T(8,128)(2,1)S(1)}, bf16[1088,1024]{1,0:T(8,128)(2,1)}, u32[]{:S(2)}, u32[]{:S(2)}) collective-permute-start(bf16[1088,1024]{1,0:T(8,128)(2,1)S(1)} %pad_maximum_fusion.refs_0_), channel_id=1, source_target_pairs={{0,3},{1,0},{2,1},{3,2},{4,7},{5,4},{6,5},{7,6},{8,11},{9,8},{10,9... | collective-permute-start | bytes 6684680 | tf_op jit(solution)/shard_map/ppermute | solution.py:42
  54.4 18.5 %collective-permute-start.5 = (bf16[544,1024]{1,0:T(8,128)(2,1)S(1)}, bf16[544,1024]{1,0:T(8,128)(2,1)S(1)}, u32[]{:S(2)}, u32[]{:S(2)}) collective-permute-start(bf16[544,1024]{1,0:T(8,128)(2,1)S(1)} %slice.97), channel_id=1, source_target_pairs={{0,1},{1,2},{2,3},{3,0},{4,5},{5,6},{6,7},{7,4},{8,9},{9,10},{10,1... | collective-permute-start | bytes 3342344 | tf_op jit(solution)/shard_map/ppermute | solution.py:42
  57.4 15.8 %collective-permute-start.6 = (bf16[544,1024]{1,0:T(8,128)(2,1)S(1)}, bf16[544,1024]{1,0:T(8,128)(2,1)S(1)}, u32[]{:S(2)}, u32[]{:S(2)}) collective-permute-start(bf16[544,1024]{1,0:T(8,128)(2,1)S(1)} %slice.98), channel_id=1, source_target_pairs={{0,3},{1,0},{2,1},{3,2},{4,7},{5,4},{6,5},{7,6},{8,11},{9,8},{10,9... | collective-permute-start | bytes 3342344 | tf_op jit(solution)/shard_map/ppermute | solution.py:42
  70.8 29.5 %collective-permute-start.10 = (bf16[512,1024]{1,0:T(8,128)(2,1)}, bf16[512,1024]{1,0:T(8,128)(2,1)S(1)}, u32[]{:S(2)}, u32[]{:S(2)}) collective-permute-start(bf16[512,1024]{1,0:T(8,128)(2,1)} %get-tuple-element.73), channel_id=1, source_target_pairs={{0,3},{1,0},{2,1},{3,2},{4,7},{5,4},{6,5},{7,6},{8,11},{9,8},{10,9... | collective-permute-start | bytes 3145736 | tf_op jit(solution)/shard_map/ppermute | solution.py:42
  72.5 27.8 %collective-permute-start.9 = (bf16[512,1024]{1,0:T(8,128)(2,1)}, bf16[512,1024]{1,0:T(8,128)(2,1)}, u32[]{:S(2)}, u32[]{:S(2)}) collective-permute-start(bf16[512,1024]{1,0:T(8,128)(2,1)} %get-tuple-element.72), channel_id=1, source_target_pairs={{0,1},{1,2},{2,3},{3,0},{4,5},{5,6},{6,7},{7,4},{8,9},{9,10},{10,1... | collective-permute-start | bytes 3145736 | tf_op jit(solution)/shard_map/ppermute | solution.py:42
  74.2 11.3 %copy-start = (s32[4]{0:T(128)S(1)}, s32[4]{0:T(128)}, u32[]{:S(2)}) copy-start(s32[4]{0:T(128)} %constant.88.clone) | copy-start | bytes 52
  82.2 18.1 %collective-permute-start.7 = (bf16[512,1024]{1,0:T(8,128)(2,1)}, bf16[512,1024]{1,0:T(8,128)(2,1)S(1)}, u32[]{:S(2)}, u32[]{:S(2)}) collective-permute-start(bf16[512,1024]{1,0:T(8,128)(2,1)} %get-tuple-element.70), channel_id=1, source_target_pairs={{0,1},{1,2},{2,3},{3,0},{4,5},{5,6},{6,7},{7,4},{8,9},{9,10},{10,1... | collective-permute-start | bytes 3145736 | tf_op jit(solution)/shard_map/ppermute | solution.py:42
  83.4 16.9 %collective-permute-start.8 = (bf16[512,1024]{1,0:T(8,128)(2,1)}, bf16[512,1024]{1,0:T(8,128)(2,1)S(1)}, u32[]{:S(2)}, u32[]{:S(2)}) collective-permute-start(bf16[512,1024]{1,0:T(8,128)(2,1)} %get-tuple-element.71), channel_id=1, source_target_pairs={{0,3},{1,0},{2,1},{3,2},{4,7},{5,4},{6,5},{7,6},{8,11},{9,8},{10,9... | collective-permute-start | bytes 3145736 | tf_op jit(solution)/shard_map/ppermute | solution.py:42
  86.8 13.6 %copy-start.7 = (bf16[512,1024]{1,0:T(8,128)(2,1)S(1)}, bf16[512,1024]{1,0:T(8,128)(2,1)}, u32[]{:S(2)}) copy-start(bf16[512,1024]{1,0:T(8,128)(2,1)} %get-tuple-element.78) | copy-start | bytes 3145732
  100.7 15.0 %collective-permute-start.12 = (bf16[512,1024]{1,0:T(8,128)(2,1)S(1)}, bf16[512,1024]{1,0:T(8,128)(2,1)}, u32[]{:S(2)}, u32[]{:S(2)}) collective-permute-start(bf16[512,1024]{1,0:T(8,128)(2,1)S(1)} %add_convert_fusion), channel_id=1, source_target_pairs={{0,3},{1,0},{2,1},{3,2},{4,7},{5,4},{6,5},{7,6},{8,11},{9,8},{10,9... | collective-permute-start | bytes 3145736 | tf_op jit(solution)/shard_map/ppermute | solution.py:42
  102.9 16.1 %collective-permute-start.11 = (bf16[512,1024]{1,0:T(8,128)(2,1)S(1)}, bf16[512,1024]{1,0:T(8,128)(2,1)S(1)}, u32[]{:S(2)}, u32[]{:S(2)}) collective-permute-start(bf16[512,1024]{1,0:T(8,128)(2,1)S(1)} %add_convert_fusion.1), channel_id=1, source_target_pairs={{0,1},{1,2},{2,3},{3,0},{4,5},{5,6},{6,7},{7,4},{8,9},{9,10},{10,1... | collective-permute-start | bytes 3145736 | tf_op jit(solution)/shard_map/ppermute | solution.py:42
  103.3 25.8 %collective-permute-start.16 = (bf16[4,2,2,128,512]{4,3,2,1,0:T(8,128)(2,1)}, bf16[4,2,2,128,512]{4,3,2,1,0:T(8,128)(2,1)S(1)}, u32[]{:S(2)}, u32[]{:S(2)}) collective-permute-start(bf16[4,2,2,128,512]{4,3,2,1,0:T(8,128)(2,1)} %get-tuple-element.89), channel_id=1, source_target_pairs={{0,16},{16,0},{32,48},{48,32},{64,80},{80,64},{96,112},{112,96},{1... | collective-permute-start | bytes 6291464 | tf_op jit(solution)/shard_map/ppermute | solution.py:46
  103.3 16.6 %copy-start.8 = (bf16[512,1024]{1,0:T(8,128)(2,1)S(1)}, bf16[512,1024]{1,0:T(8,128)(2,1)}, u32[]{:S(2)}) copy-start(bf16[512,1024]{1,0:T(8,128)(2,1)} %get-tuple-element.61) | copy-start | bytes 3145732
  112.3 9.7 %copy-start.12 = (bf16[512,1024]{1,0:T(8,128)(2,1)S(1)}, bf16[512,1024]{1,0:T(8,128)(2,1)}, u32[]{:S(2)}) copy-start(bf16[512,1024]{1,0:T(8,128)(2,1)} %get-tuple-element.85) | copy-start | bytes 3145732
  118.9 7.1 %collective-permute-start.20 = (bf16[4,2,512,128]{3,2,1,0:T(8,128)(2,1)}, bf16[4,2,512,128]{3,2,1,0:T(8,128)(2,1)S(1)}, u32[]{:S(2)}, u32[]{:S(2)}) collective-permute-start(bf16[4,2,512,128]{3,2,1,0:T(8,128)(2,1)} %get-tuple-element.91), channel_id=1, source_target_pairs={{0,16},{16,0},{32,48},{48,32},{64,80},{80,64},{96,112},{112,96},{1... | collective-permute-start | bytes 3145736 | tf_op jit(solution)/shard_map/ppermute | solution.py:46
  120.2 5.9 %copy-start.9 = (bf16[4,2,512,128]{3,2,1,0:T(8,128)(2,1)S(1)}, bf16[4,2,512,128]{3,2,1,0:T(8,128)(2,1)}, u32[]{:S(2)}) copy-start(bf16[4,2,512,128]{3,2,1,0:T(8,128)(2,1)} %get-tuple-element.90) | copy-start | bytes 3145732
  120.2 9.4 %collective-permute-start.14 = (bf16[256,1024]{1,0:T(8,128)(2,1)S(1)}, bf16[256,1024]{1,0:T(8,128)(2,1)S(1)}, u32[]{:S(2)}, u32[]{:S(2)}) collective-permute-start(bf16[256,1024]{1,0:T(8,128)(2,1)S(1)} %add_convert_fusion.7), channel_id=1, source_target_pairs={{0,12},{1,13},{2,14},{3,15},{4,0},{5,1},{6,2},{7,3},{8,4},{9,5},{1... | collective-permute-start | bytes 1572872 | tf_op jit(solution)/shard_map/ppermute | solution.py:42
  124.2 16.1 %collective-permute-start.13 = (bf16[256,1024]{1,0:T(8,128)(2,1)S(1)}, bf16[256,1024]{1,0:T(8,128)(2,1)S(1)}, u32[]{:S(2)}, u32[]{:S(2)}) collective-permute-start(bf16[256,1024]{1,0:T(8,128)(2,1)S(1)} %get-tuple-element.102), channel_id=1, source_target_pairs={{0,4},{1,5},{2,6},{3,7},{4,8},{5,9},{6,10},{7,11},{8,12},{9,13},{1... | collective-permute-start | bytes 1572872 | tf_op jit(solution)/shard_map/ppermute | solution.py:42
  124.5 18.5 %collective-permute-start.15 = (bf16[256,1024]{1,0:T(8,128)(2,1)S(1)}, bf16[256,1024]{1,0:T(8,128)(2,1)S(1)}, u32[]{:S(2)}, u32[]{:S(2)}) collective-permute-start(bf16[256,1024]{1,0:T(8,128)(2,1)S(1)} %get-tuple-element.103), channel_id=1, source_target_pairs={{0,8},{1,9},{2,10},{3,11},{4,12},{5,13},{6,14},{7,15},{8,0},{9,1},... | collective-permute-start | bytes 1572872 | tf_op jit(solution)/shard_map/ppermute | solution.py:42
  126.3 16.8 %collective-permute-start.21 = (bf16[2,512,128]{2,1,0:T(8,128)(2,1)S(1)}, bf16[2,512,128]{2,1,0:T(8,128)(2,1)S(1)}, u32[]{:S(2)}, u32[]{:S(2)}) collective-permute-start(bf16[2,512,128]{2,1,0:T(8,128)(2,1)S(1)} %get-tuple-element.104), channel_id=1, source_target_pairs={{0,96},{16,112},{32,0},{48,16},{64,32},{80,48},{96,64},{112,80},{1... | collective-permute-start | bytes 786440 | tf_op jit(solution)/shard_map/ppermute | solution.py:46
  129.1 17.6 %collective-permute-start.22 = (bf16[2,512,128]{2,1,0:T(8,128)(2,1)S(1)}, bf16[2,512,128]{2,1,0:T(8,128)(2,1)S(1)}, u32[]{:S(2)}, u32[]{:S(2)}) collective-permute-start(bf16[2,512,128]{2,1,0:T(8,128)(2,1)S(1)} %get-tuple-element.106), channel_id=1, source_target_pairs={{0,32},{16,48},{32,64},{48,80},{64,96},{80,112},{96,0},{112,16},{1... | collective-permute-start | bytes 786440 | tf_op jit(solution)/shard_map/ppermute | solution.py:46
  129.1 16.2 %copy-start.11 = (bf16[512,1024]{1,0:T(8,128)(2,1)S(1)}, bf16[512,1024]{1,0:T(8,128)(2,1)}, u32[]{:S(2)}) copy-start(bf16[512,1024]{1,0:T(8,128)(2,1)} %copy-done.10) | copy-start | bytes 3145732
  129.6 17.1 %collective-permute-start.23 = (bf16[2,512,128]{2,1,0:T(8,128)(2,1)S(1)}, bf16[2,512,128]{2,1,0:T(8,128)(2,1)S(1)}, u32[]{:S(2)}, u32[]{:S(2)}) collective-permute-start(bf16[2,512,128]{2,1,0:T(8,128)(2,1)S(1)} %get-tuple-element.105), channel_id=1, source_target_pairs={{0,64},{16,80},{32,96},{48,112},{64,0},{80,16},{96,32},{112,48},{1... | collective-permute-start | bytes 786440 | tf_op jit(solution)/shard_map/ppermute | solution.py:46
  140.3 22.4 %collective-permute-start.17 = (bf16[2,2,128,512]{3,2,1,0:T(8,128)(2,1)S(1)}, bf16[2,2,128,512]{3,2,1,0:T(8,128)(2,1)S(1)}, u32[]{:S(2)}, u32[]{:S(2)}) collective-permute-start(bf16[2,2,128,512]{3,2,1,0:T(8,128)(2,1)S(1)} %get-tuple-element.99), channel_id=1, source_target_pairs={{0,96},{16,112},{32,0},{48,16},{64,32},{80,48},{96,64},{112,80},{1... | collective-permute-start | bytes 1572872 | tf_op jit(solution)/shard_map/ppermute | solution.py:46
  143.0 23.0 %collective-permute-start.18 = (bf16[2,2,128,512]{3,2,1,0:T(8,128)(2,1)S(1)}, bf16[2,2,128,512]{3,2,1,0:T(8,128)(2,1)S(1)}, u32[]{:S(2)}, u32[]{:S(2)}) collective-permute-start(bf16[2,2,128,512]{3,2,1,0:T(8,128)(2,1)S(1)} %get-tuple-element.101), channel_id=1, source_target_pairs={{0,32},{16,48},{32,64},{48,80},{64,96},{80,112},{96,0},{112,16},{1... | collective-permute-start | bytes 1572872 | tf_op jit(solution)/shard_map/ppermute | solution.py:46
  143.0 23.0 %collective-permute-start.19 = (bf16[2,2,128,512]{3,2,1,0:T(8,128)(2,1)S(1)}, bf16[2,2,128,512]{3,2,1,0:T(8,128)(2,1)S(1)}, u32[]{:S(2)}, u32[]{:S(2)}) collective-permute-start(bf16[2,2,128,512]{3,2,1,0:T(8,128)(2,1)S(1)} %get-tuple-element.100), channel_id=1, source_target_pairs={{0,64},{16,80},{32,96},{48,112},{64,0},{80,16},{96,32},{112,48},{1... | collective-permute-start | bytes 1572872 | tf_op jit(solution)/shard_map/ppermute | solution.py:46
  (6 other events, 11.0 us)

commit v4 on v3

v4 whole, which is shorter than its diff:
```python
import functools

import jax
import jax.numpy as jnp
from jax import lax
from jax.experimental import pallas as pl
from jax.experimental.pallas import tpu as pltpu
from jax.sharding import PartitionSpec as P

loss_unscale = 0.0625
epsilon = 1e-05

SIDE = 4
OFFSETS = (0, -1, 1, 2)
CAP = 80
TOK = 256
PACK = TOK + 16
D = 1024
HID = 512
BF = jnp.bfloat16
F32 = jnp.float32
VMEM_LIMIT = 56 * 2**20


def expert_index(core, first, second):
    return jnp.where(core == 0, first * SIDE + second, second * SIDE + first)


def pairs(axis, step):
    out = []
    for dp in range(8):
        core = dp % 2
        for z in range(SIDE):
            for y in range(SIDE):
                along_z = (axis == 0) == (core == 0)
                z2, y2 = ((z + step) % SIDE, y) if along_z else (z, (y + step) % SIDE)
                out.append((dp * 16 + z * SIDE + y, dp * 16 + z2 * SIDE + y2))
    return out


def hop(value, axis, step):
    return lax.ppermute(value, ("dp", "expert"), pairs(axis, step))


def dp_hop(value, move):
    return lax.ppermute(
        value, "dp", [(x * 2 + c, move(x, c)[0] % SIDE * 2 + move(x, c)[1]) for x in range(SIDE) for c in range(2)]
    )


def nt(left, right):
    return lax.dot_general(left, right, (((1,), (1,)), ((), ())), preferred_element_type=F32)


def pack_kernel(tokens, routes, probs, out):
    out[:TOK, :] = tokens[...]
    weights = probs[...]
    high = weights.astype(BF)
    left = weights - high.astype(F32)
    middle = left.astype(BF)
    low = (left - middle.astype(F32)).astype(BF)
    out[TOK : TOK + 8, :] = jnp.concatenate(
        [routes[...].astype(F32).astype(BF), high, middle, low], axis=1
    )
    out[TOK + 8 :, :] = jnp.zeros((8, D), BF)


def pack(tokens, routes, probs):
    return pl.pallas_call(
        pack_kernel,
        out_shape=jax.ShapeDtypeStruct((PACK, D), BF),
        cost_estimate=pl.CostEstimate(flops=0, bytes_accessed=1_100_000, transcendentals=0),
        name="pack",
    )(tokens, routes.T, probs.T)


def forward_kernel(chained, perm, *refs):
    xs, (wg, wu), refs = refs[:8], refs[8:10], refs[10 + (3 if chained else 0) :]
    xt, ht, m12, rows = refs
    for i in range(8):
        rows[i * CAP : (i + 1) * CAP, :] = xs[i][0, 0]
    half = 4 * CAP
    pre = []
    for h in range(2):
        saved = rows[h * half : (h + 1) * half, :]
        pre.append(
            (
                jnp.dot(saved, wg[0], preferred_element_type=F32),
                jnp.dot(saved, wu[0], preferred_element_type=F32),
            )
        )
    xt[0] = rows[...].T
    hidden = []
    for h, (gate, up) in enumerate(pre):
        logistic = jax.nn.sigmoid(gate)
        act = gate * logistic
        m12[0, h * half : (h + 1) * half, :HID] = up * (logistic * (1.0 + gate * (1.0 - logistic)))
        m12[0, h * half : (h + 1) * half, HID:] = act
        hidden.append((act * up).astype(BF))
    ht[0] = jnp.concatenate(hidden, axis=0).T


def forward_terms(e, perm, x, wg, wu, carried):
    blocks = x.reshape(2, 16, CAP, D)
    chained = carried is not None

    def block_at(i):
        return pl.BlockSpec((1, 1, CAP, D), lambda h, p: (e, p[8 * h + i], 0, 0))

    half = 8 * CAP
    return pl.pallas_call(
        functools.partial(forward_kernel, chained),
        grid_spec=pltpu.PrefetchScalarGridSpec(
            num_scalar_prefetch=1,
            grid=(2,),
            in_specs=[block_at(i) for i in range(8)]
            + [pl.BlockSpec((1, D, HID), lambda h, p: (e, 0, 0))] * 2
            + [pl.BlockSpec(memory_space=pl.ANY)] * (3 if chained else 0),
            out_specs=[
                pl.BlockSpec((1, D, half), lambda h, p: (e, 0, h)),
                pl.BlockSpec((1, HID, half), lambda h, p: (e, 0, h)),
                pl.BlockSpec((1, half, 2 * HID), lambda h, p: (e, h, 0)),
            ],
            scratch_shapes=[pltpu.VMEM((half, D), BF)],
        ),
        out_shape=[
            jax.ShapeDtypeStruct((2, D, 16 * CAP), BF),
            jax.ShapeDtypeStruct((2, HID, 16 * CAP), BF),
            jax.ShapeDtypeStruct((2, 16 * CAP, 2 * HID), F32),
        ],
        input_output_aliases={11 + i: i for i in range(3)} if chained else {},
        compiler_params=pltpu.CompilerParams(vmem_limit_bytes=VMEM_LIMIT),
        cost_estimate=pl.CostEstimate(flops=2_700_000_000, bytes_accessed=15_000_000, transcendentals=655_360),
        name="forward_terms",
    )(perm, *([blocks] * 8), wg, wu, *(carried or ()))


def dispatch_kernel(targets, eids, *refs):
    blocks, (cots, hots) = refs[:4], (refs[4 : 4 + len(targets)], refs[4 + len(targets) :])
    before = (
        lax.broadcasted_iota(jnp.int32, (TOK, TOK), 0) < lax.broadcasted_iota(jnp.int32, (TOK, TOK), 1)
    ).astype(BF)
    slot = lax.broadcasted_iota(jnp.int32, (CAP, TOK), 0).astype(F32)
    named, weights = [], []
    for i in range(4):
        meta = blocks[i][TOK:, :].astype(F32)[:8]
        routes = meta[:, :TOK]
        probs = meta[:, TOK : 2 * TOK] + meta[:, 2 * TOK : 3 * TOK] + meta[:, 3 * TOK :]
        for target in targets:
            for e in range(2):
                hit = routes == (eids[target] + e).astype(F32)
                named.append(jnp.sum(jnp.where(hit, 1.0, 0.0), axis=0, keepdims=True))
                weights.append(jnp.sum(jnp.where(hit, probs, 0.0), axis=0, keepdims=True))
    mask = jnp.concatenate(named, axis=0)
    rank = jnp.dot(mask.astype(BF), before, preferred_element_type=F32)
    key = jnp.where(mask > 0.5, rank, -1.0)
    per = 2 * len(targets)
    for i in range(4):
        halves, scales = [], []
        for k in range(per):
            hit = slot == key[per * i + k : per * i + k + 1, :]
            halves.append(jnp.where(hit, 1.0, 0.0).astype(BF))
            scales.append(jnp.sum(jnp.where(hit, weights[per * i + k], 0.0), axis=1, keepdims=True))
        chosen = jnp.concatenate(halves, axis=0)
        taken = jnp.dot(chosen, blocks[i][:TOK, :], preferred_element_type=F32)
        scaled = (taken * jnp.concatenate(scales, axis=0)).astype(BF)
        for k in range(per):
            cots[k // 2][k % 2, i * CAP : (i + 1) * CAP, :] = scaled[k * CAP : (k + 1) * CAP]
            hots[k // 2][i, k % 2 * CAP : (k % 2 + 1) * CAP, :] = halves[k]


def dispatch(targets, eids, blocks):
    whole = pl.BlockSpec(memory_space=pltpu.VMEM)
    count = len(targets)
    out = pl.pallas_call(
        functools.partial(dispatch_kernel, targets),
        in_specs=[pl.BlockSpec(memory_space=pltpu.SMEM)] + [whole] * 4,
        out_specs=[whole] * (2 * count),
        out_shape=[jax.ShapeDtypeStruct((2, 4 * CAP, D), BF)] * count
        + [jax.ShapeDtypeStruct((4, 2 * CAP, TOK), BF)] * count,
        compiler_params=pltpu.CompilerParams(vmem_limit_bytes=VMEM_LIMIT),
        cost_estimate=pl.CostEstimate(flops=400_000_000 * count, bytes_accessed=6_000_000, transcendentals=0),
        name="dispatch_" + "".join(str(t) for t in targets),
    )(eids, *blocks)
    return out[:count], out[count:]


def groups_kernel(groups, chained, *refs):
    count = len(groups)
    arrived, m12, wd, wg, wu = refs[:count], *refs[count : count + 4]
    refs = refs[count + 4 + (2 if chained else 0) :]
    cot, gab, outs, refs = refs[0], refs[1], refs[2 : 2 + count], refs[2 + count :]
    m12_v, wd_v, wg_v, wu_v, cot_v, gab_v, rows_v, sem_in, sem_out = refs
    loads, stores, cot_loads, factor_loads = [], [], [], []

    def load(source, target):
        loads.append(pltpu.make_async_copy(source, target, sem_in.at[len(loads)]))
        loads[-1].start()
        return loads[-1]

    def store(source, target):
        stores.append(pltpu.make_async_copy(source, target, sem_out.at[len(stores)]))
        stores[-1].start()

    down_loads, weight_loads = [], []
    for n, group in enumerate(groups):
        cot_loads.append([load(arrived[n].at[e], cot_v.at[n, e]) for e in range(2)])
        if n == 0:
            down_loads = [load(wd.at[e], wd_v.at[e]) for e in range(2)]
        factor_loads.append(
            [load(m12.at[e, pl.ds(group * 4 * CAP, 4 * CAP)], m12_v.at[n, e]) for e in range(2)]
        )
        if n == 0:
            weight_loads = [[load(wg.at[e], wg_v.at[e]), load(wu.at[e], wu_v.at[e])] for e in range(2)]
    for n, group in enumerate(groups):
        place = pl.ds(group * 4 * CAP, 4 * CAP)
        for e in range(2):
            cot_loads[n][e].wait()
            store(cot_v.at[n, e], cot.at[e, place])
            if n == 0:
                down_loads[e].wait()
            grad_hidden = nt(cot_v[n, e], wd_v[e])
            factor_loads[n][e].wait()
            gab_v[n, e, :, :HID] = (grad_hidden * m12_v[n, e, :, :HID]).astype(BF)
            gab_v[n, e, :, HID:] = (grad_hidden * m12_v[n, e, :, HID:]).astype(BF)
            store(gab_v.at[n, e], gab.at[e, place])
        for e in range(2):
            if n == 0:
                for item in weight_loads[e]:
                    item.wait()
            rows_v[n, e] = (nt(gab_v[n, e, :, :HID], wg_v[e]) + nt(gab_v[n, e, :, HID:], wu_v[e])).astype(BF)
            store(rows_v.at[n, e], outs[n].at[e])
    for item in stores:
        item.wait()


def groups_pass(groups, arrived, m12, wd, wg, wu, carried):
    chained = carried is not None
    count = len(groups)
    anywhere = pl.BlockSpec(memory_space=pl.ANY)
    slots = jax.ShapeDtypeStruct((2, 16 * CAP, D), BF)
    args = [*arrived, m12, wd, wg, wu] + (list(carried) if chained else [])
    out = pl.pallas_call(
        functools.partial(groups_kernel, groups, chained),
        in_specs=[anywhere] * len(args),
        out_specs=[anywhere] * (2 + count),
        out_shape=[slots, slots] + [jax.ShapeDtypeStruct((2, 4 * CAP, D), BF)] * count,
        scratch_shapes=[
            pltpu.VMEM((count, 2, 4 * CAP, 2 * HID), F32),
            pltpu.VMEM((2, HID, D), BF),
            pltpu.VMEM((2, D, HID), BF),
            pltpu.VMEM((2, D, HID), BF),
            pltpu.VMEM((count, 2, 4 * CAP, D), BF),
            pltpu.VMEM((count, 2, 4 * CAP, 2 * HID), BF),
            pltpu.VMEM((count, 2, 4 * CAP, D), BF),
            pltpu.SemaphoreType.DMA((6 + 4 * count,)),
            pltpu.SemaphoreType.DMA((6 * count,)),
        ],
        input_output_aliases={count + 4: 0, count + 5: 1} if chained else {},
        compiler_params=pltpu.CompilerParams(vmem_limit_bytes=VMEM_LIMIT),
        cost_estimate=pl.CostEstimate(
            flops=2_100_000_000 * count, bytes_accessed=6_000_000 + 9_000_000 * count, transcendentals=0
        ),
        name="groups_" + "".join(str(g) for g in groups),
    )(*args)
    return out[0], out[1], out[2:]


def combine_kernel(*refs):
    rows, hots, outs, (rows_v, hots_v, sem_rows, sem_hots) = refs[:4], refs[4:8], refs[8:12], refs[12:]
    loads = []
    for i in range(4):
        mine = []
        for k in range(4):
            mine.append(
                pltpu.make_async_copy(
                    hots[k].at[i], hots_v.at[i, pl.ds(k * 2 * CAP, 2 * CAP)], sem_hots.at[4 * i + k]
                )
            )
            for e in range(2):
                mine.append(
                    pltpu.make_async_copy(
                        rows[k].at[e, pl.ds(i * CAP, CAP)],
                        rows_v.at[i, pl.ds((2 * k + e) * CAP, CAP)],
                        sem_rows.at[8 * i + 2 * k + e],
                    )
                )
        for item in mine:
            item.start()
        loads.append(mine)
    for i in range(4):
        for item in loads[i]:
            item.wait()
        outs[i][...] = lax.dot_general(
            hots_v[i], rows_v[i], (((0,), (0,)), ((), ())), preferred_element_type=F32
        ).astype(BF)


def combine(rows, hots):
    anywhere = pl.BlockSpec(memory_space=pl.ANY)
    return pl.pallas_call(
        combine_kernel,
        in_specs=[anywhere] * 8,
        out_specs=[pl.BlockSpec(memory_space=pltpu.VMEM)] * 4,
        out_shape=[jax.ShapeDtypeStruct((TOK, D), BF)] * 4,
        scratch_shapes=[
            pltpu.VMEM((4, 8 * CAP, D), BF),
            pltpu.VMEM((4, 8 * CAP, TOK), BF),
            pltpu.SemaphoreType.DMA((32,)),
            pltpu.SemaphoreType.DMA((16,)),
        ],
        compiler_params=pltpu.CompilerParams(vmem_limit_bytes=VMEM_LIMIT),
        cost_estimate=pl.CostEstimate(flops=1_400_000_000, bytes_accessed=9_000_000, transcendentals=0),
        name="combine",
    )(*rows, *hots)


def compress(local_grad, residual):
    carried = local_grad * loss_unscale + residual.astype(F32)
    magnitude = jnp.mean(jnp.abs(carried), axis=-1, keepdims=True) + epsilon
    compressed = (magnitude * jnp.tanh(carried * (1.0 / magnitude))).astype(BF)
    return compressed, (carried - compressed.astype(F32)).astype(BF)


def gate_up_kernel(spot, xt, gab, res_gate, res_up, keep, give_gate, give_up, left_gate, left_up, held):
    core = spot[8]
    half = pl.program_id(1)
    grads = [jnp.dot(xt[0, u * 256 : (u + 1) * 256], gab[0], preferred_element_type=F32) for u in range(2)]
    for u in range(2):
        rows = slice(u * 256, (u + 1) * 256)
        kept_at, given_at = spot[2 * half + u], spot[SIDE + 2 * half + u]
        for m, (res, left) in enumerate(((res_gate, left_gate), (res_up, left_up))):
            held[u, m], left[0, rows] = compress(grads[u][:, m * HID : (m + 1) * HID], res[0, rows])
            keep[kept_at, m, 0] = held[u, m, pl.ds(pl.multiple_of(core * 128, 128), 128)]
            give = (give_gate, give_up)[m]
            give[given_at, 0] = held[u, m, pl.ds(pl.multiple_of((1 - core) * 128, 128), 128)]


def gate_up_grads(spot, xt, gab, res_gate, res_up):
    tile = pl.BlockSpec((1, HID, HID), lambda e, t, s: (e, t, 0))
    res_shape = jax.ShapeDtypeStruct((2, D, HID), BF)
    keep_shape = jax.ShapeDtypeStruct((SIDE, 2, 2, 128, HID), BF)
    give_shape = jax.ShapeDtypeStruct((SIDE, 2, 128, HID), BF)
    return pl.pallas_call(
        gate_up_kernel,
        grid_spec=pltpu.PrefetchScalarGridSpec(
            num_scalar_prefetch=1,
            grid=(2, 2),
            in_specs=[
                pl.BlockSpec((1, 512, 16 * CAP), lambda e, t, s: (e, t, 0)),
                pl.BlockSpec((1, 16 * CAP, 2 * HID), lambda e, t, s: (e, 0, 0)),
                tile,
                tile,
            ],
            out_specs=[pl.BlockSpec((SIDE, 2, 1, 128, HID), lambda e, t, s: (0, 0, e, 0, 0))]
            + [pl.BlockSpec((SIDE, 1, 128, HID), lambda e, t, s: (0, e, 0, 0))] * 2
            + [tile, tile],
            scratch_shapes=[pltpu.VMEM((2, 2, 256, HID), BF)],
        ),
        out_shape=[keep_shape, give_shape, give_shape, res_shape, res_shape],
        compiler_params=pltpu.CompilerParams(vmem_limit_bytes=VMEM_LIMIT),
        cost_estimate=pl.CostEstimate(flops=5_400_000_000, bytes_accessed=22_000_000, transcendentals=2_000_000),
        name="gate_up_grads",
    )(spot, xt, gab, res_gate, res_up)


def down_kernel(spot, ht, cot, res, keep, give, left):
    core = spot[8]
    grads = [jnp.dot(ht[0, u * 256 : (u + 1) * 256], cot[0], preferred_element_type=F32) for u in range(2)]
    for u in range(2):
        rows = slice(u * 256, (u + 1) * 256)
        compressed, left[0, rows] = compress(grads[u], res[0, rows])
        for own in range(2):

            @pl.when(core == own)
            def _():
                for x in range(SIDE):
                    keep[spot[x], 0, rows] = compressed[:, (2 * x + own) * 128 : (2 * x + own + 1) * 128]
                    give[spot[SIDE + x], 0, rows] = compressed[:, (2 * x + 1 - own) * 128 : (2 * x + 2 - own) * 128]


def down_grads(spot, ht, cot, res):
    tile = pl.BlockSpec((1, HID, D), lambda e, s: (e, 0, 0))
    blocks = jax.ShapeDtypeStruct((SIDE, 2, HID, 128), BF)
    return pl.pallas_call(
        down_kernel,
        grid_spec=pltpu.PrefetchScalarGridSpec(
            num_scalar_prefetch=1,
            grid=(2,),
            in_specs=[
                pl.BlockSpec((1, HID, 16 * CAP), lambda e, s: (e, 0, 0)),
                pl.BlockSpec((1, 16 * CAP, D), lambda e, s: (e, 0, 0)),
                tile,
            ],
            out_specs=[pl.BlockSpec((SIDE, 1, HID, 128), lambda e, s: (0, e, 0, 0))] * 2 + [tile],
        ),
        out_shape=[blocks, blocks, jax.ShapeDtypeStruct((2, HID, D), BF)],
        compiler_params=pltpu.CompilerParams(vmem_limit_bytes=VMEM_LIMIT),
        cost_estimate=pl.CostEstimate(flops=2_700_000_000, bytes_accessed=14_000_000, transcendentals=1_000_000),
        name="down_grads",
    )(spot, ht, cot, res)


def total(*terms):
    out = terms[0].astype(F32)
    for term in terms[1:]:
        out = out + term.astype(F32)
    return out


def add(*terms):
    return total(*terms).astype(BF)


def partner(stage, x, core):
    return x ^ (1 if stage == core else 3)


def mean_over_dp(keep, got, beside):
    first = dp_hop(add(keep[2:], got[2:]), lambda x, c: (partner(0, x, c), c))
    first, _ = lax.optimization_barrier((first, beside))
    second = dp_hop(add(keep[1], got[1], first[1]), lambda x, c: (partner(1, x, c), c))
    return total(keep[0], got[0], first[0], second) / 8.0


def on_device(x_saved, d_out, routes, probs, w_gate, w_up, w_down, res_gate, res_up, res_down):
    place = lax.axis_index("expert")
    replica = lax.axis_index("dp")
    x, core = replica // 2, replica % 2
    first = jnp.where(core == 0, place // SIDE, place % SIDE)
    second = jnp.where(core == 0, place % SIDE, place // SIDE)
    offsets = jnp.array(OFFSETS, jnp.int32)
    perm = expert_index(
        core, ((first + offsets) % SIDE)[None, :], ((second + offsets) % SIDE)[:, None]
    ).reshape(-1).astype(jnp.int32)
    apart = jnp.arange(SIDE, dtype=jnp.int32) ^ x
    orders = [apart_at[apart] for apart_at in (jnp.array([0, 2, 3, 1]), jnp.array([0, 1, 3, 2]))]
    spot = jnp.concatenate(
        [jnp.where(core == 0, orders[0], orders[1]), jnp.where(core == 0, orders[1], orders[0]), core[None]]
    ).astype(jnp.int32)
    eids = (expert_index(core, first, (second + offsets) % SIDE) * 2).astype(jnp.int32)

    own = pack(d_out, routes, probs)
    near = (hop(own, 0, 1), hop(own, 0, -1), hop(own, 0, 2))
    terms = forward_terms(0, perm, x_saved[0], w_gate, w_up, None)
    near, terms = lax.optimization_barrier((near, terms))
    (to_minus, to_plus), (hot1, hot2) = dispatch((1, 2), eids, (own, *near))
    group1, group2 = hop(to_plus, 1, 1), hop(to_minus, 1, -1)
    (group0, to_far), (hot0, hot3) = dispatch((0, 3), eids, (own, *near))
    group3 = hop(to_far, 1, 2)
    xt, ht, m12 = forward_terms(1, perm, x_saved[0], w_gate, w_up, terms)

    run = functools.partial(groups_pass, m12=m12, wd=w_down, wg=w_gate, wu=w_up)
    cot, gab, (rows0,) = run((0,), [group0], carried=None)
    group1, group2, cot = lax.optimization_barrier((group1, group2, cot))
    cot, gab, (rows1, rows2) = run((1, 2), [group1, group2], carried=(cot, gab))
    cot, gab, (rows3,) = run((3,), [group3], carried=(cot, gab))
    rows = (rows0, hop(rows2, 1, 1), hop(rows1, 1, -1), hop(rows3, 1, 2))

    keep, give_gate, give_up, left_gate, left_up = gate_up_grads(spot, xt, gab, res_gate[0], res_up[0])
    got_gate, got_up = (dp_hop(g, lambda x, c: (x, 1 - c)) for g in (give_gate, give_up))
    near_rows, ht, left_gate = lax.optimization_barrier((rows[1:3], ht, left_gate))
    keep_down, give_down, left_down = down_grads(spot, ht, cot, res_down[0])
    rows = (rows[0], *near_rows, rows[3])
    rows, got_gate, got_up, give_down = lax.optimization_barrier((rows, got_gate, got_up, give_down))
    got_down = dp_hop(give_down, lambda x, c: (x, 1 - c))
    mine, before, behind, across = combine(rows, (hot0, hot1, hot2, hot3))
    mean = mean_over_dp(keep, jnp.stack([got_gate, got_up], axis=1), mine)
    mean_down = mean_over_dp(keep_down, got_down, mine)
    terms = (mine, hop(behind, 0, 1), hop(before, 0, -1), hop(across, 0, 2))
    terms, mean, mean_down = lax.optimization_barrier((terms, mean, mean_down))
    d_tokens = add(*terms)
    return (d_tokens, mean[0], mean[1], mean_down, left_gate[None], left_up[None], left_down[None])


def solution(mesh):
    in_specs = (
        P("dp", "expert", None, None),
        P(("dp", "expert"), None),
        P(("dp", "expert"), None),
        P(("dp", "expert"), None),
        P("expert", None, None),
        P("expert", None, None),
        P("expert", None, None),
        P("dp", "expert", None, None),
        P("dp", "expert", None, None),
        P("dp", "expert", None, None),
    )
    out_specs = (
        P(("dp", "expert"), None),
        P("expert", "dp", None),
        P("expert", "dp", None),
        P("expert", None, "dp"),
        P("dp", "expert", None, None),
        P("dp", "expert", None, None),
        P("dp", "expert", None, None),
    )
    return jax.shard_map(
        on_device, mesh=mesh, in_specs=in_specs, out_specs=out_specs, check_vma=False
    )
```

time: 168 us -> 156 us (0.929)
  waiting for transfers between devices: 45.9 us -> 27.1 us
  Pallas kernels: 68.8 us -> 78.6 us
  other arithmetic: 9.2 us -> 6.13 us
    ppermute x16 -> x12, waiting for transfers between devices: 27.5 us -> 6.7 us  [hop(): return lax.ppermute(value, ('dp', 'expert'), pairs(axis, step))]
    pallas_call x3 -> x6, Pallas kernels: 27.4 us -> 37.3 us  [the longest x3 23 us: groups_pass(): pl.pallas_call(functools.partial(groups_kernel, groups, chained), in_spec...]
    ppermute x16 -> x12, starting transfers between devices: 24.1 us -> 28.5 us  [hop(): return lax.ppermute(value, ('dp', 'expert'), pairs(axis, step))]
    ppermute x8 -> x7, starting transfers between devices: 10.7 us -> 6.66 us  [dp_hop(): lax.ppermute(value, 'dp', [(x * 2 + c, move(x, c)[0] % SIDE * 2 + move(x,...]
    slice x2 -> x0, local copies, waits for them, and re-layouts: 2.64 us -> none  [on_device(): group3 = (hop(group1[:2 * PACK], 1, 1), hop(group2[2 * PACK:], 1, -1))]
    convert_element_type x2 -> x0, other arithmetic: 2.4 us -> none  [the longest x1 2.14 us: on_device(): column(2).astype(BF)]
    ppermute x8 -> x7, waiting for transfers between devices: 18.3 us -> 20.4 us  [dp_hop(): lax.ppermute(value, 'dp', [(x * 2 + c, move(x, c)[0] % SIDE * 2 + move(x,...]
    unnamed x28 -> x32, local copies, waits for them, and re-layouts: 2.91 us -> 3.57 us
  transfers between devices with their start and end apart: 24 -> 19, of which waited for: 10 -> 5; matrix products, arithmetic and copies ran while one was open for 6% -> 4% of each run, Pallas kernels for 40% -> 47%
where the time goes in v4:
time: 156 us; the launch traced here: 155 us
  Pallas kernels  78.6 us (50%)
  starting transfers between devices  35.1 us (22%)
  waiting for transfers between devices  27.1 us (17%)
  local copies, waits for them, and re-layouts  7.13 us (5%)
  other arithmetic  6.13 us (4%)
    ppermute x12, starting transfers between devices, hop(): return lax.ppermute(value, ('dp', 'expert'), pairs(axis, step))  28.5 us
    pallas_call x3, Pallas kernels, groups_pass(): pl.pallas_call(functools.partial(groups_kernel, groups, chained), in_spec...  23 us
    ppermute x7, waiting for transfers between devices, dp_hop(): lax.ppermute(value, 'dp', [(x * 2 + c, move(x, c)[0] % SIDE * 2 + move(x,...  20.4 us
    pallas_call x2, Pallas kernels, forward_terms(): pl.pallas_call(functools.partial(forward_kernel, chained), grid_spec=pltp...  16.7 us
    pallas_call x1, Pallas kernels, gate_up_grads(): pl.pallas_call(gate_up_kernel, grid_spec=pltpu.PrefetchScalarGridSpec(num...  13.4 us
    pallas_call x1, Pallas kernels, down_grads(): pl.pallas_call(down_kernel, grid_spec=pltpu.PrefetchScalarGridSpec(num_sc...  9.28 us
    pallas_call x2, Pallas kernels, dispatch(): pl.pallas_call(functools.partial(dispatch_kernel, targets), in_specs=[pl....  8.52 us
    ppermute x12, waiting for transfers between devices, hop(): return lax.ppermute(value, ('dp', 'expert'), pairs(axis, step))  6.7 us
  transfers between devices with their start and end apart: 19, of which 5 were waited for; matrix products, arithmetic and copies ran while one was open for 4% of the time, Pallas kernels for 47%

profile of v4, /device:TPU:0, one launch (start us, length us, event | category | flops | bytes accessed | tf_op | source)
XLA Modules:
  0.0 155.0 jit_solution(4988658276797203307)
XLA Ops:
  0.6 2.0 %pack.1.refs_0_ = bf16[272,1024]{1,0:T(8,128)(2,1)} custom-call(bf16[256,1024]{1,0:T(8,128)(2,1)} %tokens.1, s32[8,256]{1,0:T(8,128)} %bitcast.59, f32[8,256]{1,0:T(8,128)} %bitcast.60), custom_call_target="tpu_custom_call" | custom-call | bytes 1100000 | tf_op jit(solution)/shard_map/pack/pallas_call | solution.py:69
  2.6 4.0 %collective-permute-start.2 = (bf16[272,1024]{1,0:T(8,128)(2,1)}, bf16[272,1024]{1,0:T(8,128)(2,1)S(1)}, u32[]{:S(2)}, u32[]{:S(2)}) collective-permute-start(bf16[272,1024]{1,0:T(8,128)(2,1)} %pack.1.refs_0_), channel_id=1, source_target_pairs={{0,8},{1,9},{2,10},{3,11},{4,12},{5,13},{6,14},{7,15},{8,0},{9,1},... | collective-permute-start | bytes 1671176 | tf_op jit(solution)/shard_map/ppermute | solution.py:42
  7.3 1.3 collective-permute-start
  9.9 1.3 gather_fusion.1
  12.4 8.4 %forward_terms.2 = (bf16[2,1024,1280]{2,1,0:T(8,128)(2,1)}, bf16[2,512,1280]{2,1,0:T(8,128)(2,1)}, f32[2,1280,1024]{2,1,0:T(8,128)}) custom-call(s32[16]{0:T(128)} %select_n.89.perm, bf16[2,16,80,1024]{3,2,1,0:T(8,128)(2,1)} %bitcast.37, bf16[2,16,80,1024]{3,2,1,0:T(8,128)(2,1)} %bitcast.38, bf16[2,16,80,1024]{3,2,1,0:T(8,128)(2,1)} %bitcast.39, ...), custom_call_target="tpu_custom_call" | custom-call | flops 2700000000 | bytes 15000000 | tf_op jit(solution)/shard_map/forward_terms/pallas_call | solution.py:111
  22.3 4.2 %dispatch_12.1 = (bf16[2,320,1024]{2,1,0:T(8,128)(2,1)}, bf16[2,320,1024]{2,1,0:T(8,128)(2,1)}, bf16[4,160,256]{2,1,0:T(8,128)(2,1)}, bf16[4,160,256]{2,1,0:T(8,128)(2,1)}) custom-call(s32[4]{0:T(128)} %get-tuple-element.145.eids, bf16[272,1024]{1,0:T(8,128)(2,1)} %pack.1.refs_0_, bf16[272,1024]{1,0:T(8,128)(2,1)} %copy-done.12, ...), custom_call_target="tpu_custom_call" | custom-call | flops 800000000 | bytes 6000000 | tf_op jit(solution)/shard_map/dispatch_12/pallas_call | solution.py:175
  26.6 1.6 %collective-permute-start.3 = (bf16[2,320,1024]{2,1,0:T(8,128)(2,1)}, bf16[2,320,1024]{2,1,0:T(8,128)(2,1)S(1)}, u32[]{:S(2)}, u32[]{:S(2)}) collective-permute-start(bf16[2,320,1024]{2,1,0:T(8,128)(2,1)} %get-tuple-element.83), channel_id=1, source_target_pairs={{0,1},{1,2},{2,3},{3,0},{4,5},{5,6},{6,7},{7,4},{8,9},{9,10},{10,1... | collective-permute-start | bytes 3932168 | tf_op jit(solution)/shard_map/ppermute | solution.py:42
  28.1 1.7 %collective-permute-start.4 = (bf16[2,320,1024]{2,1,0:T(8,128)(2,1)}, bf16[2,320,1024]{2,1,0:T(8,128)(2,1)S(1)}, u32[]{:S(2)}, u32[]{:S(2)}) collective-permute-start(bf16[2,320,1024]{2,1,0:T(8,128)(2,1)} %get-tuple-element.84), channel_id=1, source_target_pairs={{0,3},{1,0},{2,1},{3,2},{4,7},{5,4},{6,5},{7,6},{8,11},{9,8},{10,9... | collective-permute-start | bytes 3932168 | tf_op jit(solution)/shard_map/ppermute | solution.py:42
  29.8 4.3 %dispatch_03.1 = (bf16[2,320,1024]{2,1,0:T(8,128)(2,1)}, bf16[2,320,1024]{2,1,0:T(8,128)(2,1)}, bf16[4,160,256]{2,1,0:T(8,128)(2,1)}, bf16[4,160,256]{2,1,0:T(8,128)(2,1)}) custom-call(s32[4]{0:T(128)} %get-tuple-element.145.eids, bf16[272,1024]{1,0:T(8,128)(2,1)} %pack.1.refs_0_, bf16[272,1024]{1,0:T(8,128)(2,1)} %copy-done.12, ...), custom_call_target="tpu_custom_call" | custom-call | flops 800000000 | bytes 6000000 | tf_op jit(solution)/shard_map/dispatch_03/pallas_call | solution.py:175
  34.1 2.0 %collective-permute-start.7 = (bf16[2,320,1024]{2,1,0:T(8,128)(2,1)}, bf16[2,320,1024]{2,1,0:T(8,128)(2,1)S(1)}, u32[]{:S(2)}, u32[]{:S(2)}) collective-permute-start(bf16[2,320,1024]{2,1,0:T(8,128)(2,1)} %get-tuple-element.94), channel_id=1, source_target_pairs={{0,2},{1,3},{2,0},{3,1},{4,6},{5,7},{6,4},{7,5},{8,10},{9,11},{10,... | collective-permute-start | bytes 3932168 | tf_op jit(solution)/shard_map/ppermute | solution.py:42
  36.6 8.4 %forward_terms.3 = (bf16[2,1024,1280]{2,1,0:T(8,128)(2,1)}, bf16[2,512,1280]{2,1,0:T(8,128)(2,1)}, f32[2,1280,1024]{2,1,0:T(8,128)}) custom-call(s32[16]{0:T(128)} %select_n.89.perm, bf16[2,16,80,1024]{3,2,1,0:T(8,128)(2,1)} %bitcast.45, bf16[2,16,80,1024]{3,2,1,0:T(8,128)(2,1)} %bitcast.46, ...), custom_call_target="tpu_custom_call", output_to_operand_aliasing={{0}: (11, {}), {1}: (12, {}), {2}: (13, {})} | custom-call | flops 2700000000 | bytes 15000000 | tf_op jit(solution)/shard_map/forward_terms/pallas_call | solution.py:111
  45.0 6.7 %groups_0.1 = (bf16[2,1280,1024]{2,1,0:T(8,128)(2,1)}, bf16[2,1280,1024]{2,1,0:T(8,128)(2,1)}, bf16[2,320,1024]{2,1,0:T(8,128)(2,1)}) custom-call(bf16[2,320,1024]{2,1,0:T(8,128)(2,1)} %get-tuple-element.77.refs_0_, f32[2,1280,1024]{2,1,0:T(8,128)} %get-tuple-element.81.refs_1_.refs_2_, bf16[2,512,1024]{2,1,0:T(8,128)(2,1)} %refs_2_.3, ...), custom_call_target="tpu_custom_call" | custom-call | flops 2100000000 | bytes 15000000 | tf_op jit(solution)/shard_map/groups_0/pallas_call | solution.py:243
  53.2 9.6 %groups_12.1 = (bf16[2,1280,1024]{2,1,0:T(8,128)(2,1)}, bf16[2,1280,1024]{2,1,0:T(8,128)(2,1)}, bf16[2,320,1024]{2,1,0:T(8,128)(2,1)}, bf16[2,320,1024]{2,1,0:T(8,128)(2,1)}) custom-call(bf16[2,320,1024]{2,1,0:T(8,128)(2,1)} %copy-done.3, bf16[2,320,1024]{2,1,0:T(8,128)(2,1)} %copy-done.4, ...), custom_call_target="tpu_custom_call", output_to_operand_aliasing={{0}: (6, {}), {1}: (7, {})} | custom-call | flops 4200000000 | bytes 24000000 | tf_op jit(solution)/shard_map/groups_12/pallas_call | solution.py:243
  63.6 10.1 %collective-permute-start.6 = (bf16[2,320,1024]{2,1,0:T(8,128)(2,1)}, bf16[2,320,1024]{2,1,0:T(8,128)(2,1)S(1)}, u32[]{:S(2)}, u32[]{:S(2)}) collective-permute-start(bf16[2,320,1024]{2,1,0:T(8,128)(2,1)} %get-tuple-element.91), channel_id=1, source_target_pairs={{0,3},{1,0},{2,1},{3,2},{4,7},{5,4},{6,5},{7,6},{8,11},{9,8},{10,9... | collective-permute-start | bytes 3932168 | tf_op jit(solution)/shard_map/ppermute | solution.py:42
  73.7 1.1 copy-done.2
  74.8 6.7 %groups_3.1 = (bf16[2,1280,1024]{2,1,0:T(8,128)(2,1)}, bf16[2,1280,1024]{2,1,0:T(8,128)(2,1)}, bf16[2,320,1024]{2,1,0:T(8,128)(2,1)}) custom-call(bf16[2,320,1024]{2,1,0:T(8,128)(2,1)} %copy-done.2, f32[2,1280,1024]{2,1,0:T(8,128)} %get-tuple-element.81.refs_1_.refs_2_, bf16[2,512,1024]{2,1,0:T(8,128)(2,1)} %refs_2_.3, ...), custom_call_target="tpu_custom_call", output_to_operand_aliasing={{0}: (5, {}), {1}: (6, {})} | custom-call | flops 2100000000 | bytes 15000000 | tf_op jit(solution)/shard_map/groups_3/pallas_call | solution.py:243
  81.5 1.7 %collective-permute-start.8 = (bf16[2,320,1024]{2,1,0:T(8,128)(2,1)}, bf16[2,320,1024]{2,1,0:T(8,128)(2,1)S(1)}, u32[]{:S(2)}, u32[]{:S(2)}) collective-permute-start(bf16[2,320,1024]{2,1,0:T(8,128)(2,1)} %get-tuple-element.101), channel_id=1, source_target_pairs={{0,2},{1,3},{2,0},{3,1},{4,6},{5,7},{6,4},{7,5},{8,10},{9,11},{10,... | collective-permute-start | bytes 3932168 | tf_op jit(solution)/shard_map/ppermute | solution.py:42
  83.2 13.4 %gate_up_grads.1 = (bf16[4,2,2,128,512]{4,3,2,1,0:T(8,128)(2,1)}, bf16[4,2,128,512]{3,2,1,0:T(8,128)(2,1)}, bf16[4,2,128,512]{3,2,1,0:T(8,128)(2,1)}, bf16[2,1024,512]{2,1,0:T(8,128)(2,1)}, bf16[2,1024,512]{2,1,0:T(8,128)(2,1)}) custom-call(s32[9]{0:T(128)} %pad_add_fusion.spot, bf16[2,1024,1280]{2,1,0:T(8,128)(2,1)} %get-tuple-element.93.xt, ...), custom_call_target="tpu_custom_call" | custom-call | flops 5400000000 | bytes 22000000 | tf_op jit(solution)/shard_map/gate_up_grads/pallas_call | solution.py:344
  97.1 6.1 %collective-permute-done.6.refs_2_ = bf16[2,320,1024]{2,1,0:T(8,128)(2,1)S(1)} collective-permute-done((bf16[2,320,1024]{2,1,0:T(8,128)(2,1)}, bf16[2,320,1024]{2,1,0:T(8,128)(2,1)S(1)}, u32[]{:S(2)}, u32[]{:S(2)}) %collective-permute-start.6) | collective-permute-done | bytes 1310752 | tf_op jit(solution)/shard_map/ppermute | solution.py:42
  103.2 9.3 %down_grads.1 = (bf16[4,2,512,128]{3,2,1,0:T(8,128)(2,1)}, bf16[4,2,512,128]{3,2,1,0:T(8,128)(2,1)}, bf16[2,512,1024]{2,1,0:T(8,128)(2,1)}) custom-call(s32[9]{0:T(128)} %pad_add_fusion.spot, bf16[2,512,1280]{2,1,0:T(8,128)(2,1)} %get-tuple-element.104.ht, bf16[2,1280,1024]{2,1,0:T(8,128)(2,1)} %get-tuple-element.105.cot, bf16[2,512,1024]{2,1,0:T(8,128)(2,1)} %bitcast.63), custom_call_target="tpu_custom_call" | custom-call | flops 2700000000 | bytes 14000000 | tf_op jit(solution)/shard_map/down_grads/pallas_call | solution.py:385
  112.5 1.5 add_convert_fusion
  114.0 1.5 collective-permute-start.14
  115.5 5.8 %combine.1 = (bf16[256,1024]{1,0:T(8,128)(2,1)}, bf16[256,1024]{1,0:T(8,128)(2,1)}, bf16[256,1024]{1,0:T(8,128)(2,1)}, bf16[256,1024]{1,0:T(8,128)(2,1)}) custom-call(bf16[2,320,1024]{2,1,0:T(8,128)(2,1)} %get-tuple-element.107.refs_0_, bf16[2,320,1024]{2,1,0:T(8,128)(2,1)} %copy-done.5, bf16[2,320,1024]{2,1,0:T(8,128)(2,1)} %copy-done.6, ...), custom_call_target="tpu_custom_call" | custom-call | flops 1400000000 | bytes 9000000 | tf_op jit(solution)/shard_map/combine/pallas_call | solution.py:301
  121.3 7.7 %collective-permute-done.14 = bf16[2,2,2,128,512]{4,3,2,1,0:T(8,128)(2,1)S(1)} collective-permute-done((bf16[2,2,2,128,512]{4,3,2,1,0:T(8,128)(2,1)}, bf16[2,2,2,128,512]{4,3,2,1,0:T(8,128)(2,1)S(1)}, u32[]{:S(2)}, u32[]{:S(2)}) %collective-permute-start.14) | collective-permute-done | bytes 1048608 | tf_op jit(solution)/shard_map/ppermute | solution.py:46
  129.2 1.6 %collective-permute-start.17 = (bf16[2,2,512,128]{3,2,1,0:T(8,128)(2,1)S(1)}, bf16[2,2,512,128]{3,2,1,0:T(8,128)(2,1)S(1)}, u32[]{:S(2)}, u32[]{:S(2)}) collective-permute-start(bf16[2,2,512,128]{3,2,1,0:T(8,128)(2,1)S(1)} %add_convert_fusion.2), channel_id=1, source_target_pairs={{0,32},{16,112},{32,0},{48,80},{64,96},{80,48},{96,64},{112,16},{1... | collective-permute-start | bytes 1572872 | tf_op jit(solution)/shard_map/ppermute | solution.py:46
  131.0 2.2 %collective-permute-start.15 = (bf16[2,2,128,512]{3,2,1,0:T(8,128)(2,1)S(1)}, bf16[2,2,128,512]{3,2,1,0:T(8,128)(2,1)S(1)}, u32[]{:S(2)}, u32[]{:S(2)}) collective-permute-start(bf16[2,2,128,512]{3,2,1,0:T(8,128)(2,1)S(1)} %fusion.3), channel_id=1, source_target_pairs={{0,96},{16,48},{32,64},{48,16},{64,32},{80,112},{96,0},{112,80},{1... | collective-permute-start | bytes 1572872 | tf_op jit(solution)/shard_map/ppermute | solution.py:46
  133.2 2.2 %collective-permute-start.11 = (bf16[256,1024]{1,0:T(8,128)(2,1)S(1)}, bf16[256,1024]{1,0:T(8,128)(2,1)S(1)}, u32[]{:S(2)}, u32[]{:S(2)}) collective-permute-start(bf16[256,1024]{1,0:T(8,128)(2,1)S(1)} %copy-done.15), channel_id=1, source_target_pairs={{0,4},{1,5},{2,6},{3,7},{4,8},{5,9},{6,10},{7,11},{8,12},{9,13},{1... | collective-permute-start | bytes 1572872 | tf_op jit(solution)/shard_map/ppermute | solution.py:42
  135.4 1.1 collective-permute-start.12
  136.4 1.5 collective-permute-start.13
  137.9 6.1 %collective-permute-done.17 = bf16[2,2,512,128]{3,2,1,0:T(8,128)(2,1)S(1)} collective-permute-done((bf16[2,2,512,128]{3,2,1,0:T(8,128)(2,1)S(1)}, bf16[2,2,512,128]{3,2,1,0:T(8,128)(2,1)S(1)}, u32[]{:S(2)}, u32[]{:S(2)}) %collective-permute-start.17) | collective-permute-done | bytes 524320 | tf_op jit(solution)/shard_map/ppermute | solution.py:46
  145.4 6.5 %collective-permute-done.18 = bf16[2,512,128]{2,1,0:T(8,128)(2,1)S(1)} collective-permute-done((bf16[2,512,128]{2,1,0:T(8,128)(2,1)S(1)}, bf16[2,512,128]{2,1,0:T(8,128)(2,1)S(1)}, u32[]{:S(2)}, u32[]{:S(2)}) %collective-permute-start.18) | collective-permute-done | bytes 262176 | tf_op jit(solution)/shard_map/ppermute | solution.py:46
  153.8 1.1 add_convert_fusion.1
  (66 shorter events, 11.7 us)
Async XLA Ops:
  0.6 10.6 %copy-start = (s32[4]{0:T(128)S(1)}, s32[4]{0:T(128)}, u32[]{:S(2)}) copy-start(s32[4]{0:T(128)} %constant.89.clone) | copy-start | bytes 52
  2.6 18.1 %collective-permute-start.2 = (bf16[272,1024]{1,0:T(8,128)(2,1)}, bf16[272,1024]{1,0:T(8,128)(2,1)S(1)}, u32[]{:S(2)}, u32[]{:S(2)}) collective-permute-start(bf16[272,1024]{1,0:T(8,128)(2,1)} %pack.1.refs_0_), channel_id=1, source_target_pairs={{0,8},{1,9},{2,10},{3,11},{4,12},{5,13},{6,14},{7,15},{8,0},{9,1},... | collective-permute-start | bytes 1671176 | tf_op jit(solution)/shard_map/ppermute | solution.py:42
  6.6 14.7 %collective-permute-start.1 = (bf16[272,1024]{1,0:T(8,128)(2,1)}, bf16[272,1024]{1,0:T(8,128)(2,1)S(1)}, u32[]{:S(2)}, u32[]{:S(2)}) collective-permute-start(bf16[272,1024]{1,0:T(8,128)(2,1)} %pack.1.refs_0_), channel_id=1, source_target_pairs={{0,12},{1,13},{2,14},{3,15},{4,0},{5,1},{6,2},{7,3},{8,4},{9,5},{1... | collective-permute-start | bytes 1671176 | tf_op jit(solution)/shard_map/ppermute | solution.py:42
  7.3 14.0 %collective-permute-start = (bf16[272,1024]{1,0:T(8,128)(2,1)}, bf16[272,1024]{1,0:T(8,128)(2,1)S(1)}, u32[]{:S(2)}, u32[]{:S(2)}) collective-permute-start(bf16[272,1024]{1,0:T(8,128)(2,1)} %pack.1.refs_0_), channel_id=1, source_target_pairs={{0,4},{1,5},{2,6},{3,7},{4,8},{5,9},{6,10},{7,11},{8,12},{9,13},{1... | collective-permute-start | bytes 1671176 | tf_op jit(solution)/shard_map/ppermute | solution.py:42
  26.6 25.2 %collective-permute-start.3 = (bf16[2,320,1024]{2,1,0:T(8,128)(2,1)}, bf16[2,320,1024]{2,1,0:T(8,128)(2,1)S(1)}, u32[]{:S(2)}, u32[]{:S(2)}) collective-permute-start(bf16[2,320,1024]{2,1,0:T(8,128)(2,1)} %get-tuple-element.83), channel_id=1, source_target_pairs={{0,1},{1,2},{2,3},{3,0},{4,5},{5,6},{6,7},{7,4},{8,9},{9,10},{10,1... | collective-permute-start | bytes 3932168 | tf_op jit(solution)/shard_map/ppermute | solution.py:42
  28.1 23.6 %collective-permute-start.4 = (bf16[2,320,1024]{2,1,0:T(8,128)(2,1)}, bf16[2,320,1024]{2,1,0:T(8,128)(2,1)S(1)}, u32[]{:S(2)}, u32[]{:S(2)}) collective-permute-start(bf16[2,320,1024]{2,1,0:T(8,128)(2,1)} %get-tuple-element.84), channel_id=1, source_target_pairs={{0,3},{1,0},{2,1},{3,2},{4,7},{5,4},{6,5},{7,6},{8,11},{9,8},{10,9... | collective-permute-start | bytes 3932168 | tf_op jit(solution)/shard_map/ppermute | solution.py:42
  34.1 39.6 %collective-permute-start.7 = (bf16[2,320,1024]{2,1,0:T(8,128)(2,1)}, bf16[2,320,1024]{2,1,0:T(8,128)(2,1)S(1)}, u32[]{:S(2)}, u32[]{:S(2)}) collective-permute-start(bf16[2,320,1024]{2,1,0:T(8,128)(2,1)} %get-tuple-element.94), channel_id=1, source_target_pairs={{0,2},{1,3},{2,0},{3,1},{4,6},{5,7},{6,4},{7,5},{8,10},{9,11},{10,... | collective-permute-start | bytes 3932168 | tf_op jit(solution)/shard_map/ppermute | solution.py:42
  51.7 1.1 copy-start.3
  51.7 1.5 copy-start.4
  62.8 34.2 %collective-permute-start.5 = (bf16[2,320,1024]{2,1,0:T(8,128)(2,1)}, bf16[2,320,1024]{2,1,0:T(8,128)(2,1)S(1)}, u32[]{:S(2)}, u32[]{:S(2)}) collective-permute-start(bf16[2,320,1024]{2,1,0:T(8,128)(2,1)} %get-tuple-element.90), channel_id=1, source_target_pairs={{0,1},{1,2},{2,3},{3,0},{4,5},{5,6},{6,7},{7,4},{8,9},{9,10},{10,1... | collective-permute-start | bytes 3932168 | tf_op jit(solution)/shard_map/ppermute | solution.py:42
  63.6 39.6 %collective-permute-start.6 = (bf16[2,320,1024]{2,1,0:T(8,128)(2,1)}, bf16[2,320,1024]{2,1,0:T(8,128)(2,1)S(1)}, u32[]{:S(2)}, u32[]{:S(2)}) collective-permute-start(bf16[2,320,1024]{2,1,0:T(8,128)(2,1)} %get-tuple-element.91), channel_id=1, source_target_pairs={{0,3},{1,0},{2,1},{3,2},{4,7},{5,4},{6,5},{7,6},{8,11},{9,8},{10,9... | collective-permute-start | bytes 3932168 | tf_op jit(solution)/shard_map/ppermute | solution.py:42
  73.7 1.1 copy-start.2
  81.5 31.0 %collective-permute-start.8 = (bf16[2,320,1024]{2,1,0:T(8,128)(2,1)}, bf16[2,320,1024]{2,1,0:T(8,128)(2,1)S(1)}, u32[]{:S(2)}, u32[]{:S(2)}) collective-permute-start(bf16[2,320,1024]{2,1,0:T(8,128)(2,1)} %get-tuple-element.101), channel_id=1, source_target_pairs={{0,2},{1,3},{2,0},{3,1},{4,6},{5,7},{6,4},{7,5},{8,10},{9,11},{10,... | collective-permute-start | bytes 3932168 | tf_op jit(solution)/shard_map/ppermute | solution.py:42
  96.5 15.9 %collective-permute-start.9 = (bf16[4,2,128,512]{3,2,1,0:T(8,128)(2,1)}, bf16[4,2,128,512]{3,2,1,0:T(8,128)(2,1)S(1)}, u32[]{:S(2)}, u32[]{:S(2)}) collective-permute-start(bf16[4,2,128,512]{3,2,1,0:T(8,128)(2,1)} %get-tuple-element.102), channel_id=1, source_target_pairs={{0,16},{16,0},{32,48},{48,32},{64,80},{80,64},{96,112},{112,96},{1... | collective-permute-start | bytes 3145736 | tf_op jit(solution)/shard_map/ppermute | solution.py:46
  96.6 15.9 %collective-permute-start.10 = (bf16[4,2,128,512]{3,2,1,0:T(8,128)(2,1)}, bf16[4,2,128,512]{3,2,1,0:T(8,128)(2,1)S(1)}, u32[]{:S(2)}, u32[]{:S(2)}) collective-permute-start(bf16[4,2,128,512]{3,2,1,0:T(8,128)(2,1)} %get-tuple-element.103), channel_id=1, source_target_pairs={{0,16},{16,0},{32,48},{48,32},{64,80},{80,64},{96,112},{112,96},{1... | collective-permute-start | bytes 3145736 | tf_op jit(solution)/shard_map/ppermute | solution.py:46
  97.1 15.4 %copy-start.5 = (bf16[2,320,1024]{2,1,0:T(8,128)(2,1)}, bf16[2,320,1024]{2,1,0:T(8,128)(2,1)S(1)}, u32[]{:S(2)}) copy-start(bf16[2,320,1024]{2,1,0:T(8,128)(2,1)S(1)} %collective-permute-done.5.refs_1_) | copy-start | bytes 3932164
  103.2 9.3 %copy-start.6 = (bf16[2,320,1024]{2,1,0:T(8,128)(2,1)}, bf16[2,320,1024]{2,1,0:T(8,128)(2,1)S(1)}, u32[]{:S(2)}) copy-start(bf16[2,320,1024]{2,1,0:T(8,128)(2,1)S(1)} %collective-permute-done.6.refs_2_) | copy-start | bytes 3932164
  103.2 9.3 %copy-start.1 = (bf16[4,2,2,128,512]{4,3,2,1,0:T(8,128)(2,1)S(1)}, bf16[4,2,2,128,512]{4,3,2,1,0:T(8,128)(2,1)}, u32[]{:S(2)}) copy-start(bf16[4,2,2,128,512]{4,3,2,1,0:T(8,128)(2,1)} %get-tuple-element.119) | copy-start | bytes 6291460
  112.5 1.5 copy-start.7
  114.0 15.0 %collective-permute-start.14 = (bf16[2,2,2,128,512]{4,3,2,1,0:T(8,128)(2,1)}, bf16[2,2,2,128,512]{4,3,2,1,0:T(8,128)(2,1)S(1)}, u32[]{:S(2)}, u32[]{:S(2)}) collective-permute-start(bf16[2,2,2,128,512]{4,3,2,1,0:T(8,128)(2,1)} %add_convert_fusion), channel_id=1, source_target_pairs={{0,32},{16,112},{32,0},{48,80},{64,96},{80,48},{96,64},{112,16},{1... | collective-permute-start | bytes 3145736 | tf_op jit(solution)/shard_map/ppermute | solution.py:46
  115.5 13.5 %collective-permute-start.16 = (bf16[4,2,512,128]{3,2,1,0:T(8,128)(2,1)}, bf16[4,2,512,128]{3,2,1,0:T(8,128)(2,1)S(1)}, u32[]{:S(2)}, u32[]{:S(2)}) collective-permute-start(bf16[4,2,512,128]{3,2,1,0:T(8,128)(2,1)} %get-tuple-element.124), channel_id=1, source_target_pairs={{0,16},{16,0},{32,48},{48,32},{64,80},{80,64},{96,112},{112,96},{1... | collective-permute-start | bytes 3145736 | tf_op jit(solution)/shard_map/ppermute | solution.py:46
  115.5 13.5 %copy-start.8 = (bf16[4,2,512,128]{3,2,1,0:T(8,128)(2,1)S(1)}, bf16[4,2,512,128]{3,2,1,0:T(8,128)(2,1)}, u32[]{:S(2)}) copy-start(bf16[4,2,512,128]{3,2,1,0:T(8,128)(2,1)} %get-tuple-element.123) | copy-start | bytes 3145732
  129.2 4.0 %copy-start.15 = (bf16[256,1024]{1,0:T(8,128)(2,1)S(1)}, bf16[256,1024]{1,0:T(8,128)(2,1)}, u32[]{:S(2)}) copy-start(bf16[256,1024]{1,0:T(8,128)(2,1)} %get-tuple-element.116) | copy-start | bytes 1572868
  129.2 6.2 %copy-start.14 = (bf16[256,1024]{1,0:T(8,128)(2,1)S(1)}, bf16[256,1024]{1,0:T(8,128)(2,1)}, u32[]{:S(2)}) copy-start(bf16[256,1024]{1,0:T(8,128)(2,1)} %get-tuple-element.117) | copy-start | bytes 1572868
  129.2 7.2 %copy-start.13 = (bf16[256,1024]{1,0:T(8,128)(2,1)S(1)}, bf16[256,1024]{1,0:T(8,128)(2,1)}, u32[]{:S(2)}) copy-start(bf16[256,1024]{1,0:T(8,128)(2,1)} %get-tuple-element.118) | copy-start | bytes 1572868
  129.2 14.9 %collective-permute-start.17 = (bf16[2,2,512,128]{3,2,1,0:T(8,128)(2,1)S(1)}, bf16[2,2,512,128]{3,2,1,0:T(8,128)(2,1)S(1)}, u32[]{:S(2)}, u32[]{:S(2)}) collective-permute-start(bf16[2,2,512,128]{3,2,1,0:T(8,128)(2,1)S(1)} %add_convert_fusion.2), channel_id=1, source_target_pairs={{0,32},{16,112},{32,0},{48,80},{64,96},{80,48},{96,64},{112,16},{1... | collective-permute-start | bytes 1572872 | tf_op jit(solution)/shard_map/ppermute | solution.py:46
  131.0 14.0 %collective-permute-start.15 = (bf16[2,2,128,512]{3,2,1,0:T(8,128)(2,1)S(1)}, bf16[2,2,128,512]{3,2,1,0:T(8,128)(2,1)S(1)}, u32[]{:S(2)}, u32[]{:S(2)}) collective-permute-start(bf16[2,2,128,512]{3,2,1,0:T(8,128)(2,1)S(1)} %fusion.3), channel_id=1, source_target_pairs={{0,96},{16,48},{32,64},{48,16},{64,32},{80,112},{96,0},{112,80},{1... | collective-permute-start | bytes 1572872 | tf_op jit(solution)/shard_map/ppermute | solution.py:46
  133.2 19.6 %collective-permute-start.11 = (bf16[256,1024]{1,0:T(8,128)(2,1)S(1)}, bf16[256,1024]{1,0:T(8,128)(2,1)S(1)}, u32[]{:S(2)}, u32[]{:S(2)}) collective-permute-start(bf16[256,1024]{1,0:T(8,128)(2,1)S(1)} %copy-done.15), channel_id=1, source_target_pairs={{0,4},{1,5},{2,6},{3,7},{4,8},{5,9},{6,10},{7,11},{8,12},{9,13},{1... | collective-permute-start | bytes 1572872 | tf_op jit(solution)/shard_map/ppermute | solution.py:42
  135.4 17.4 %collective-permute-start.12 = (bf16[256,1024]{1,0:T(8,128)(2,1)S(1)}, bf16[256,1024]{1,0:T(8,128)(2,1)S(1)}, u32[]{:S(2)}, u32[]{:S(2)}) collective-permute-start(bf16[256,1024]{1,0:T(8,128)(2,1)S(1)} %copy-done.14), channel_id=1, source_target_pairs={{0,12},{1,13},{2,14},{3,15},{4,0},{5,1},{6,2},{7,3},{8,4},{9,5},{1... | collective-permute-start | bytes 1572872 | tf_op jit(solution)/shard_map/ppermute | solution.py:42
  136.4 16.4 %collective-permute-start.13 = (bf16[256,1024]{1,0:T(8,128)(2,1)S(1)}, bf16[256,1024]{1,0:T(8,128)(2,1)S(1)}, u32[]{:S(2)}, u32[]{:S(2)}) collective-permute-start(bf16[256,1024]{1,0:T(8,128)(2,1)S(1)} %copy-done.13), channel_id=1, source_target_pairs={{0,8},{1,9},{2,10},{3,11},{4,12},{5,13},{6,14},{7,15},{8,0},{9,1},... | collective-permute-start | bytes 1572872 | tf_op jit(solution)/shard_map/ppermute | solution.py:42
  144.2 7.7 %collective-permute-start.18 = (bf16[2,512,128]{2,1,0:T(8,128)(2,1)S(1)}, bf16[2,512,128]{2,1,0:T(8,128)(2,1)S(1)}, u32[]{:S(2)}, u32[]{:S(2)}) collective-permute-start(bf16[2,512,128]{2,1,0:T(8,128)(2,1)S(1)} %fusion.5), channel_id=1, source_target_pairs={{0,96},{16,48},{32,64},{48,16},{64,32},{80,112},{96,0},{112,80},{1... | collective-permute-start | bytes 786440 | tf_op jit(solution)/shard_map/ppermute | solution.py:46
  145.3 8.5 %copy-start.9 = (bf16[256,1024]{1,0:T(8,128)(2,1)S(1)}, bf16[256,1024]{1,0:T(8,128)(2,1)}, u32[]{:S(2)}) copy-start(bf16[256,1024]{1,0:T(8,128)(2,1)} %get-tuple-element.126) | copy-start | bytes 1572868
  (3 other events, 2.6 us)

commit v5 on v4

--- a/solution.py
+++ b/solution.py
@@ -22,8 +22,21 @@
 VMEM_LIMIT = 56 * 2**20
 
 
-def expert_index(core, first, second):
+def place_of(here):
+    core = here[0] & 1
+    z, y = here[1] // SIDE, here[1] & (SIDE - 1)
+    return here[0] // 2, core, jnp.where(core == 0, z, y), jnp.where(core == 0, y, z)
+
+
+def expert_at(here, first_off, second_off):
+    _, core, first, second = place_of(here)
+    first, second = (first + first_off + SIDE) & (SIDE - 1), (second + second_off + SIDE) & (SIDE - 1)
     return jnp.where(core == 0, first * SIDE + second, second * SIDE + first)
+
+
+def block_place(owner, x, core):
+    apart = owner ^ x
+    return jnp.where(apart == 0, 0, jnp.where(apart == 1, 2 - core, jnp.where(apart == 2, 3, 1 + core)))
 
 
 def pairs(axis, step):
@@ -74,7 +87,7 @@
     )(tokens, routes.T, probs.T)
 
 
-def forward_kernel(chained, perm, *refs):
+def forward_kernel(chained, here, *refs):
     xs, (wg, wu), refs = refs[:8], refs[8:10], refs[10 + (3 if chained else 0) :]
     xt, ht, m12, rows = refs
     for i in range(8):
@@ -100,12 +113,15 @@
     ht[0] = jnp.concatenate(hidden, axis=0).T
 
 
-def forward_terms(e, perm, x, wg, wu, carried):
+def forward_terms(e, here, x, wg, wu, carried):
     blocks = x.reshape(2, 16, CAP, D)
     chained = carried is not None
 
     def block_at(i):
-        return pl.BlockSpec((1, 1, CAP, D), lambda h, p: (e, p[8 * h + i], 0, 0))
+        def at(h, here):
+            return e, expert_at(here, OFFSETS[i % 4], h if i < 4 else 3 * h - 1), 0, 0
+
+        return pl.BlockSpec((1, 1, CAP, D), at)
 
     half = 8 * CAP
     return pl.pallas_call(
@@ -132,64 +148,77 @@
         compiler_params=pltpu.CompilerParams(vmem_limit_bytes=VMEM_LIMIT),
         cost_estimate=pl.CostEstimate(flops=2_700_000_000, bytes_accessed=15_000_000, transcendentals=655_360),
         name="forward_terms",
-    )(perm, *([blocks] * 8), wg, wu, *(carried or ()))
-
-
-def dispatch_kernel(targets, eids, *refs):
-    blocks, (cots, hots) = refs[:4], (refs[4 : 4 + len(targets)], refs[4 + len(targets) :])
+    )(here, *([blocks] * 8), wg, wu, *(carried or ()))
+
+
+def dispatch_kernel(targets, layout, here, *refs):
+    blocks, outs, hots = refs[:4], refs[4 : 4 + len(layout)], refs[4 + len(layout) :]
     before = (
         lax.broadcasted_iota(jnp.int32, (TOK, TOK), 0) < lax.broadcasted_iota(jnp.int32, (TOK, TOK), 1)
     ).astype(BF)
     slot = lax.broadcasted_iota(jnp.int32, (CAP, TOK), 0).astype(F32)
+    names = [(2 * expert_at(here, 0, OFFSETS[t]) + e).astype(F32) for t in targets for e in range(2)]
     named, weights = [], []
     for i in range(4):
         meta = blocks[i][TOK:, :].astype(F32)[:8]
         routes = meta[:, :TOK]
         probs = meta[:, TOK : 2 * TOK] + meta[:, 2 * TOK : 3 * TOK] + meta[:, 3 * TOK :]
-        for target in targets:
-            for e in range(2):
-                hit = routes == (eids[target] + e).astype(F32)
-                named.append(jnp.sum(jnp.where(hit, 1.0, 0.0), axis=0, keepdims=True))
-                weights.append(jnp.sum(jnp.where(hit, probs, 0.0), axis=0, keepdims=True))
+        for name in names:
+            hit = routes == name
+            named.append(jnp.sum(jnp.where(hit, 1.0, 0.0), axis=0, keepdims=True))
+            weights.append(jnp.sum(jnp.where(hit, probs, 0.0), axis=0, keepdims=True))
     mask = jnp.concatenate(named, axis=0)
     rank = jnp.dot(mask.astype(BF), before, preferred_element_type=F32)
     key = jnp.where(mask > 0.5, rank, -1.0)
-    per = 2 * len(targets)
+    per = len(names)
     for i in range(4):
         halves, scales = [], []
         for k in range(per):
             hit = slot == key[per * i + k : per * i + k + 1, :]
             halves.append(jnp.where(hit, 1.0, 0.0).astype(BF))
             scales.append(jnp.sum(jnp.where(hit, weights[per * i + k], 0.0), axis=1, keepdims=True))
+            hots[k // 2][i, k % 2 * CAP : (k % 2 + 1) * CAP, :] = halves[k]
         chosen = jnp.concatenate(halves, axis=0)
         taken = jnp.dot(chosen, blocks[i][:TOK, :], preferred_element_type=F32)
         scaled = (taken * jnp.concatenate(scales, axis=0)).astype(BF)
-        for k in range(per):
-            cots[k // 2][k % 2, i * CAP : (i + 1) * CAP, :] = scaled[k * CAP : (k + 1) * CAP]
-            hots[k // 2][i, k % 2 * CAP : (k % 2 + 1) * CAP, :] = halves[k]
-
-
-def dispatch(targets, eids, blocks):
+        for out, held in zip(outs, layout):
+            for n, (target, e) in enumerate(held):
+                k = 2 * targets.index(target) + e
+                out[n, i * CAP : (i + 1) * CAP, :] = scaled[k * CAP : (k + 1) * CAP]
+
+
+def dispatch(targets, layout, here, blocks):
     whole = pl.BlockSpec(memory_space=pltpu.VMEM)
-    count = len(targets)
     out = pl.pallas_call(
-        functools.partial(dispatch_kernel, targets),
+        functools.partial(dispatch_kernel, targets, layout),
         in_specs=[pl.BlockSpec(memory_space=pltpu.SMEM)] + [whole] * 4,
-        out_specs=[whole] * (2 * count),
-        out_shape=[jax.ShapeDtypeStruct((2, 4 * CAP, D), BF)] * count
-        + [jax.ShapeDtypeStruct((4, 2 * CAP, TOK), BF)] * count,
+        out_specs=[whole] * (len(layout) + len(targets)),
+        out_shape=[jax.ShapeDtypeStruct((len(held), 4 * CAP, D), BF) for held in layout]
+        + [jax.ShapeDtypeStruct((4, 2 * CAP, TOK), BF)] * len(targets),
         compiler_params=pltpu.CompilerParams(vmem_limit_bytes=VMEM_LIMIT),
-        cost_estimate=pl.CostEstimate(flops=400_000_000 * count, bytes_accessed=6_000_000, transcendentals=0),
+        cost_estimate=pl.CostEstimate(
+            flops=400_000_000 * len(targets), bytes_accessed=6_000_000, transcendentals=0
+        ),
         name="dispatch_" + "".join(str(t) for t in targets),
-    )(eids, *blocks)
-    return out[:count], out[count:]
-
-
-def groups_kernel(groups, chained, *refs):
+    )(here, *blocks)
+    return out[: len(layout)], out[len(layout) :]
+
+
+def halves_of(refs, split):
+    out = []
+    for two in split:
+        out.append([refs[0], refs[1]] if two else [refs[0].at[0], refs[0].at[1]])
+        refs = refs[2 if two else 1 :]
+    return out
+
+
+def groups_kernel(groups, split, chained, *refs):
     count = len(groups)
-    arrived, m12, wd, wg, wu = refs[:count], *refs[count : count + 4]
-    refs = refs[count + 4 + (2 if chained else 0) :]
-    cot, gab, outs, refs = refs[0], refs[1], refs[2 : 2 + count], refs[2 + count :]
+    lent = count + sum(split)
+    arrived = halves_of(refs[:lent], split)
+    m12, wd, wg, wu = refs[lent : lent + 4]
+    refs = refs[lent + 4 + (2 if chained else 0) :]
+    cot, gab, outs, refs = refs[0], refs[1], halves_of(refs[2 : 2 + lent], split), refs[2 + lent :]
     m12_v, wd_v, wg_v, wu_v, cot_v, gab_v, rows_v, sem_in, sem_out = refs
     loads, stores, cot_loads, factor_loads = [], [], [], []
 
@@ -204,7 +233,7 @@
 
     down_loads, weight_loads = [], []
     for n, group in enumerate(groups):
-        cot_loads.append([load(arrived[n].at[e], cot_v.at[n, e]) for e in range(2)])
+        cot_loads.append([load(arrived[n][e], cot_v.at[n, e]) for e in range(2)])
         if n == 0:
             down_loads = [load(wd.at[e], wd_v.at[e]) for e in range(2)]
         factor_loads.append(
@@ -229,7 +258,7 @@
                 for item in weight_loads[e]:
                     item.wait()
             rows_v[n, e] = (nt(gab_v[n, e, :, :HID], wg_v[e]) + nt(gab_v[n, e, :, HID:], wu_v[e])).astype(BF)
-            store(rows_v.at[n, e], outs[n].at[e])
+            store(rows_v.at[n, e], outs[n][e])
     for item in stores:
         item.wait()
 
@@ -239,12 +268,19 @@
     count = len(groups)
     anywhere = pl.BlockSpec(memory_space=pl.ANY)
     slots = jax.ShapeDtypeStruct((2, 16 * CAP, D), BF)
-    args = [*arrived, m12, wd, wg, wu] + (list(carried) if chained else [])
+    split = [isinstance(a, tuple) for a in arrived]
+    lent = count + sum(split)
+    args = [a for two, a in zip(split, arrived) for a in (a if two else (a,))]
+    args += [m12, wd, wg, wu] + (list(carried) if chained else [])
+    row_shapes = []
+    for two in split:
+        shape = (4 * CAP, D) if two else (2, 4 * CAP, D)
+        row_shapes += [jax.ShapeDtypeStruct(shape, BF)] * (2 if two else 1)
     out = pl.pallas_call(
-        functools.partial(groups_kernel, groups, chained),
+        functools.partial(groups_kernel, groups, split, chained),
         in_specs=[anywhere] * len(args),
-        out_specs=[anywhere] * (2 + count),
-        out_shape=[slots, slots] + [jax.ShapeDtypeStruct((2, 4 * CAP, D), BF)] * count,
+        out_specs=[anywhere] * (2 + lent),
+        out_shape=[slots, slots] + row_shapes,
         scratch_shapes=[
             pltpu.VMEM((count, 2, 4 * CAP, 2 * HID), F32),
             pltpu.VMEM((2, HID, D), BF),
@@ -256,7 +292,7 @@
             pltpu.SemaphoreType.DMA((6 + 4 * count,)),
             pltpu.SemaphoreType.DMA((6 * count,)),
         ],
-        input_output_aliases={count + 4: 0, count + 5: 1} if chained else {},
+        input_output_aliases={lent + 4: 0, lent + 5: 1} if chained else {},
         compiler_params=pltpu.CompilerParams(vmem_limit_bytes=VMEM_LIMIT),
         cost_estimate=pl.CostEstimate(
             flops=2_100_000_000 * count, bytes_accessed=6_000_000 + 9_000_000 * count, transcendentals=0
@@ -267,7 +303,8 @@
 
 
 def combine_kernel(*refs):
-    rows, hots, outs, (rows_v, hots_v, sem_rows, sem_hots) = refs[:4], refs[4:8], refs[8:12], refs[12:]
+    rows, hots, outs, (rows_v, hots_v, sem_rows, sem_hots) = refs[:5], refs[5:9], refs[9:13], refs[13:]
+    rows = halves_of(rows, (False, False, False, True))
     loads = []
     for i in range(4):
         mine = []
@@ -280,7 +317,7 @@
             for e in range(2):
                 mine.append(
                     pltpu.make_async_copy(
-                        rows[k].at[e, pl.ds(i * CAP, CAP)],
+                        rows[k][e].at[pl.ds(i * CAP, CAP)],
                         rows_v.at[i, pl.ds((2 * k + e) * CAP, CAP)],
                         sem_rows.at[8 * i + 2 * k + e],
                     )
@@ -300,7 +337,7 @@
     anywhere = pl.BlockSpec(memory_space=pl.ANY)
     return pl.pallas_call(
         combine_kernel,
-        in_specs=[anywhere] * 8,
+        in_specs=[anywhere] * 9,
         out_specs=[pl.BlockSpec(memory_space=pltpu.VMEM)] * 4,
         out_shape=[jax.ShapeDtypeStruct((TOK, D), BF)] * 4,
         scratch_shapes=[
@@ -322,13 +359,14 @@
     return compressed, (carried - compressed.astype(F32)).astype(BF)
 
 
-def gate_up_kernel(spot, xt, gab, res_gate, res_up, keep, give_gate, give_up, left_gate, left_up, held):
-    core = spot[8]
+def gate_up_kernel(here, xt, gab, res_gate, res_up, keep, give_gate, give_up, left_gate, left_up, held):
+    x, core, _, _ = place_of(here)
     half = pl.program_id(1)
     grads = [jnp.dot(xt[0, u * 256 : (u + 1) * 256], gab[0], preferred_element_type=F32) for u in range(2)]
     for u in range(2):
         rows = slice(u * 256, (u + 1) * 256)
-        kept_at, given_at = spot[2 * half + u], spot[SIDE + 2 * half + u]
+        kept_at = block_place(2 * half + u, x, core)
+        given_at = block_place(2 * half + u, x, 1 - core)
         for m, (res, left) in enumerate(((res_gate, left_gate), (res_up, left_up))):
             held[u, m], left[0, rows] = compress(grads[u][:, m * HID : (m + 1) * HID], res[0, rows])
             keep[kept_at, m, 0] = held[u, m, pl.ds(pl.multiple_of(core * 128, 128), 128)]
@@ -336,7 +374,7 @@
             give[given_at, 0] = held[u, m, pl.ds(pl.multiple_of((1 - core) * 128, 128), 128)]
 
 
-def gate_up_grads(spot, xt, gab, res_gate, res_up):
+def gate_up_grads(here, xt, gab, res_gate, res_up):
     tile = pl.BlockSpec((1, HID, HID), lambda e, t, s: (e, t, 0))
     res_shape = jax.ShapeDtypeStruct((2, D, HID), BF)
     keep_shape = jax.ShapeDtypeStruct((SIDE, 2, 2, 128, HID), BF)
@@ -361,11 +399,11 @@
         compiler_params=pltpu.CompilerParams(vmem_limit_bytes=VMEM_LIMIT),
         cost_estimate=pl.CostEstimate(flops=5_400_000_000, bytes_accessed=22_000_000, transcendentals=2_000_000),
         name="gate_up_grads",
-    )(spot, xt, gab, res_gate, res_up)
-
-
-def down_kernel(spot, ht, cot, res, keep, give, left):
-    core = spot[8]
+    )(here, xt, gab, res_gate, res_up)
+
+
+def down_kernel(here, ht, cot, res, keep, give, left):
+    x, core, _, _ = place_of(here)
     grads = [jnp.dot(ht[0, u * 256 : (u + 1) * 256], cot[0], preferred_element_type=F32) for u in range(2)]
     for u in range(2):
         rows = slice(u * 256, (u + 1) * 256)
@@ -374,12 +412,14 @@
 
             @pl.when(core == own)
             def _():
-                for x in range(SIDE):
-                    keep[spot[x], 0, rows] = compressed[:, (2 * x + own) * 128 : (2 * x + own + 1) * 128]
-                    give[spot[SIDE + x], 0, rows] = compressed[:, (2 * x + 1 - own) * 128 : (2 * x + 2 - own) * 128]
-
-
-def down_grads(spot, ht, cot, res):
+                for owner in range(SIDE):
+                    at = 2 * owner + own
+                    keep[block_place(owner, x, own), 0, rows] = compressed[:, at * 128 : (at + 1) * 128]
+                    at = 2 * owner + 1 - own
+                    give[block_place(owner, x, 1 - own), 0, rows] = compressed[:, at * 128 : (at + 1) * 128]
+
+
+def down_grads(here, ht, cot, res):
     tile = pl.BlockSpec((1, HID, D), lambda e, s: (e, 0, 0))
     blocks = jax.ShapeDtypeStruct((SIDE, 2, HID, 128), BF)
     return pl.pallas_call(
@@ -398,7 +438,7 @@
         compiler_params=pltpu.CompilerParams(vmem_limit_bytes=VMEM_LIMIT),
         cost_estimate=pl.CostEstimate(flops=2_700_000_000, bytes_accessed=14_000_000, transcendentals=1_000_000),
         name="down_grads",
-    )(spot, ht, cot, res)
+    )(here, ht, cot, res)
 
 
 def total(*terms):
@@ -424,50 +464,41 @@
 
 
 def on_device(x_saved, d_out, routes, probs, w_gate, w_up, w_down, res_gate, res_up, res_down):
-    place = lax.axis_index("expert")
-    replica = lax.axis_index("dp")
-    x, core = replica // 2, replica % 2
-    first = jnp.where(core == 0, place // SIDE, place % SIDE)
-    second = jnp.where(core == 0, place % SIDE, place // SIDE)
-    offsets = jnp.array(OFFSETS, jnp.int32)
-    perm = expert_index(
-        core, ((first + offsets) % SIDE)[None, :], ((second + offsets) % SIDE)[:, None]
-    ).reshape(-1).astype(jnp.int32)
-    apart = jnp.arange(SIDE, dtype=jnp.int32) ^ x
-    orders = [apart_at[apart] for apart_at in (jnp.array([0, 2, 3, 1]), jnp.array([0, 1, 3, 2]))]
-    spot = jnp.concatenate(
-        [jnp.where(core == 0, orders[0], orders[1]), jnp.where(core == 0, orders[1], orders[0]), core[None]]
-    ).astype(jnp.int32)
-    eids = (expert_index(core, first, (second + offsets) % SIDE) * 2).astype(jnp.int32)
+    here = jnp.stack([lax.axis_index("dp"), lax.axis_index("expert")]).astype(jnp.int32)
 
     own = pack(d_out, routes, probs)
     near = (hop(own, 0, 1), hop(own, 0, -1), hop(own, 0, 2))
-    terms = forward_terms(0, perm, x_saved[0], w_gate, w_up, None)
+    terms = forward_terms(0, here, x_saved[0], w_gate, w_up, None)
     near, terms = lax.optimization_barrier((near, terms))
-    (to_minus, to_plus), (hot1, hot2) = dispatch((1, 2), eids, (own, *near))
+    layout = (((2, 0), (2, 1), (3, 0)), ((1, 0), (1, 1), (3, 1)))
+    (to_plus, to_minus), (hot1, hot2, hot3) = dispatch((1, 2, 3), layout, here, (own, *near))
     group1, group2 = hop(to_plus, 1, 1), hop(to_minus, 1, -1)
-    (group0, to_far), (hot0, hot3) = dispatch((0, 3), eids, (own, *near))
-    group3 = hop(to_far, 1, 2)
-    xt, ht, m12 = forward_terms(1, perm, x_saved[0], w_gate, w_up, terms)
+    (group0,), (hot0,) = dispatch((0,), (((0, 0), (0, 1)),), here, (own, *near))
+    xt, ht, m12 = forward_terms(1, here, x_saved[0], w_gate, w_up, terms)
 
     run = functools.partial(groups_pass, m12=m12, wd=w_down, wg=w_gate, wu=w_up)
     cot, gab, (rows0,) = run((0,), [group0], carried=None)
     group1, group2, cot = lax.optimization_barrier((group1, group2, cot))
+    group3 = (hop(group1[2], 1, 1), hop(group2[2], 1, -1))
     cot, gab, (rows1, rows2) = run((1, 2), [group1, group2], carried=(cot, gab))
-    cot, gab, (rows3,) = run((3,), [group3], carried=(cot, gab))
-    rows = (rows0, hop(rows2, 1, 1), hop(rows1, 1, -1), hop(rows3, 1, 2))
-
-    keep, give_gate, give_up, left_gate, left_up = gate_up_grads(spot, xt, gab, res_gate[0], res_up[0])
+    near_rows = (hop(rows2[:2], 1, 1), hop(rows1[:2], 1, -1))
+    cot, gab, (rows3a, rows3b) = run((3,), [group3], carried=(cot, gab))
+    half_way = (hop(rows3a, 1, 1), hop(rows3b, 1, -1))
+
+    keep, give_gate, give_up, left_gate, left_up = gate_up_grads(here, xt, gab, res_gate[0], res_up[0])
     got_gate, got_up = (dp_hop(g, lambda x, c: (x, 1 - c)) for g in (give_gate, give_up))
-    near_rows, ht, left_gate = lax.optimization_barrier((rows[1:3], ht, left_gate))
-    keep_down, give_down, left_down = down_grads(spot, ht, cot, res_down[0])
-    rows = (rows[0], *near_rows, rows[3])
-    rows, got_gate, got_up, give_down = lax.optimization_barrier((rows, got_gate, got_up, give_down))
+    near_rows, half_way, ht, left_gate = lax.optimization_barrier((near_rows, half_way, ht, left_gate))
+    far_rows = (hop(half_way[0], 1, 1), hop(half_way[1], 1, -1))
+    keep_down, give_down, left_down = down_grads(here, ht, cot, res_down[0])
+    near_rows, far_rows, got_gate, got_up, give_down = lax.optimization_barrier(
+        (near_rows, far_rows, got_gate, got_up, give_down)
+    )
     got_down = dp_hop(give_down, lambda x, c: (x, 1 - c))
-    mine, before, behind, across = combine(rows, (hot0, hot1, hot2, hot3))
+
+    mine, before, behind, across = combine((rows0, *near_rows, *far_rows), (hot0, hot1, hot2, hot3))
+    terms = (mine, hop(behind, 0, 1), hop(before, 0, -1), hop(across, 0, 2))
     mean = mean_over_dp(keep, jnp.stack([got_gate, got_up], axis=1), mine)
-    mean_down = mean_over_dp(keep_down, got_down, mine)
-    terms = (mine, hop(behind, 0, 1), hop(before, 0, -1), hop(across, 0, 2))
+    mean_down = mean_over_dp(keep_down, got_down, terms)
     terms, mean, mean_down = lax.optimization_barrier((terms, mean, mean_down))
     d_tokens = add(*terms)
     return (d_tokens, mean[0], mean[1], mean_down, left_gate[None], left_up[None], left_down[None])

time: 156 us -> 153 us (0.981)
  local copies, waits for them, and re-layouts: 7.13 us -> 5.02 us
    ppermute x7, waiting for transfers between devices: 20.4 us -> 11.6 us  [dp_hop(): lax.ppermute(value, 'dp', [(x * 2 + c, move(x, c)[0] % SIDE * 2 + move(x,...]
    ppermute x12 -> x16, waiting for transfers between devices: 6.7 us -> 14.3 us  [hop(): return lax.ppermute(value, ('dp', 'expert'), pairs(axis, step))]
    ppermute x7, starting transfers between devices: 6.66 us -> 9.89 us  [dp_hop(): lax.ppermute(value, 'dp', [(x * 2 + c, move(x, c)[0] % SIDE * 2 + move(x,...]
    ppermute x12 -> x16, starting transfers between devices: 28.5 us -> 26.1 us  [hop(): return lax.ppermute(value, ('dp', 'expert'), pairs(axis, step))]
    squeeze x0 -> x2, local copies, waits for them, and re-layouts: none -> 2.1 us  [on_device(): group3 = (hop(group1[2], 1, 1), hop(group2[2], 1, -1))]
    gather x2 -> x0, local copies, waits for them, and re-layouts: 1.93 us -> none  [on_device(): apart_at[apart]]
    unnamed x32 -> x26, local copies, waits for them, and re-layouts: 3.57 us -> 1.89 us
  transfers between devices with their start and end apart: 19 -> 23, of which waited for: 5 -> 9; matrix products, arithmetic and copies ran while one was open for 4% -> 1% of each run, Pallas kernels for 47% -> 47%
where the time goes in v5:
time: 153 us; the launch traced here: 151 us
  Pallas kernels  78.7 us (51%)
  starting transfers between devices  36 us (24%)
  waiting for transfers between devices  26 us (17%)
  local copies, waits for them, and re-layouts  5.02 us (3%)
  other arithmetic  4.67 us (3%)
    ppermute x16, starting transfers between devices, hop(): return lax.ppermute(value, ('dp', 'expert'), pairs(axis, step))  26.1 us
    pallas_call x3, Pallas kernels, groups_pass(): pl.pallas_call(functools.partial(groups_kernel, groups, split, chained),...  23.3 us
    pallas_call x2, Pallas kernels, forward_terms(): pl.pallas_call(functools.partial(forward_kernel, chained), grid_spec=pltp...  16.8 us
    ppermute x16, waiting for transfers between devices, hop(): return lax.ppermute(value, ('dp', 'expert'), pairs(axis, step))  14.3 us
    pallas_call x1, Pallas kernels, gate_up_grads(): pl.pallas_call(gate_up_kernel, grid_spec=pltpu.PrefetchScalarGridSpec(num...  13.4 us
    ppermute x7, waiting for transfers between devices, dp_hop(): lax.ppermute(value, 'dp', [(x * 2 + c, move(x, c)[0] % SIDE * 2 + move(x,...  11.6 us
    ppermute x7, starting transfers between devices, dp_hop(): lax.ppermute(value, 'dp', [(x * 2 + c, move(x, c)[0] % SIDE * 2 + move(x,...  9.89 us
    pallas_call x1, Pallas kernels, down_grads(): pl.pallas_call(down_kernel, grid_spec=pltpu.PrefetchScalarGridSpec(num_sc...  9.01 us
  transfers between devices with their start and end apart: 23, of which 9 were waited for; matrix products, arithmetic and copies ran while one was open for 1% of the time, Pallas kernels for 47%

profile of v5, /device:TPU:0, one launch (start us, length us, event | category | flops | bytes accessed | tf_op | source)
XLA Modules:
  0.0 151.2 jit_solution(2764296806993284735)
XLA Ops:
  0.6 1.9 %pack.1.refs_0_ = bf16[272,1024]{1,0:T(8,128)(2,1)} custom-call(bf16[256,1024]{1,0:T(8,128)(2,1)} %tokens.1, s32[8,256]{1,0:T(8,128)} %bitcast.62, f32[8,256]{1,0:T(8,128)} %bitcast.63), custom_call_target="tpu_custom_call" | custom-call | bytes 1100000 | tf_op jit(solution)/shard_map/pack/pallas_call | solution.py:82
  2.6 2.0 %collective-permute-start = (bf16[272,1024]{1,0:T(8,128)(2,1)}, bf16[272,1024]{1,0:T(8,128)(2,1)S(1)}, u32[]{:S(2)}, u32[]{:S(2)}) collective-permute-start(bf16[272,1024]{1,0:T(8,128)(2,1)} %pack.1.refs_0_), channel_id=1, source_target_pairs={{0,4},{1,5},{2,6},{3,7},{4,8},{5,9},{6,10},{7,11},{8,12},{9,13},{1... | collective-permute-start | bytes 1671176 | tf_op jit(solution)/shard_map/ppermute | solution.py:55
  4.6 2.1 %collective-permute-start.1 = (bf16[272,1024]{1,0:T(8,128)(2,1)}, bf16[272,1024]{1,0:T(8,128)(2,1)S(1)}, u32[]{:S(2)}, u32[]{:S(2)}) collective-permute-start(bf16[272,1024]{1,0:T(8,128)(2,1)} %pack.1.refs_0_), channel_id=1, source_target_pairs={{0,12},{1,13},{2,14},{3,15},{4,0},{5,1},{6,2},{7,3},{8,4},{9,5},{1... | collective-permute-start | bytes 1671176 | tf_op jit(solution)/shard_map/ppermute | solution.py:55
  6.7 1.9 %collective-permute-start.2 = (bf16[272,1024]{1,0:T(8,128)(2,1)}, bf16[272,1024]{1,0:T(8,128)(2,1)S(1)}, u32[]{:S(2)}, u32[]{:S(2)}) collective-permute-start(bf16[272,1024]{1,0:T(8,128)(2,1)} %pack.1.refs_0_), channel_id=1, source_target_pairs={{0,8},{1,9},{2,10},{3,11},{4,12},{5,13},{6,14},{7,15},{8,0},{9,1},... | collective-permute-start | bytes 1671176 | tf_op jit(solution)/shard_map/ppermute | solution.py:55
  9.1 8.4 %forward_terms.2 = (bf16[2,1024,1280]{2,1,0:T(8,128)(2,1)}, bf16[2,512,1280]{2,1,0:T(8,128)(2,1)}, f32[2,1280,1024]{2,1,0:T(8,128)}) custom-call(s32[2]{0:T(128)} %pad_add_fusion.here, bf16[2,16,80,1024]{3,2,1,0:T(8,128)(2,1)} %bitcast.40, bf16[2,16,80,1024]{3,2,1,0:T(8,128)(2,1)} %bitcast.41, bf16[2,16,80,1024]{3,2,1,0:T(8,128)(2,1)} %bitcast.42, ...), custom_call_target="tpu_custom_call" | custom-call | flops 2700000000 | bytes 15000000 | tf_op jit(solution)/shard_map/forward_terms/pallas_call | solution.py:127
  17.5 2.5 %collective-permute-done.1.refs_2_ = bf16[272,1024]{1,0:T(8,128)(2,1)S(1)} collective-permute-done((bf16[272,1024]{1,0:T(8,128)(2,1)}, bf16[272,1024]{1,0:T(8,128)(2,1)S(1)}, u32[]{:S(2)}, u32[]{:S(2)}) %collective-permute-start.1) | collective-permute-done | bytes 557088 | tf_op jit(solution)/shard_map/ppermute | solution.py:55
  20.1 1.8 %collective-permute-done.2.refs_3_ = bf16[272,1024]{1,0:T(8,128)(2,1)S(1)} collective-permute-done((bf16[272,1024]{1,0:T(8,128)(2,1)}, bf16[272,1024]{1,0:T(8,128)(2,1)S(1)}, u32[]{:S(2)}, u32[]{:S(2)}) %collective-permute-start.2) | collective-permute-done | bytes 557088 | tf_op jit(solution)/shard_map/ppermute | solution.py:55
  22.7 5.2 %dispatch_123.1 = (bf16[3,320,1024]{2,1,0:T(8,128)(2,1)}, bf16[3,320,1024]{2,1,0:T(8,128)(2,1)}, bf16[4,160,256]{2,1,0:T(8,128)(2,1)}, bf16[4,160,256]{2,1,0:T(8,128)(2,1)}, bf16[4,160,256]{2,1,0:T(8,128)(2,1)}) custom-call(s32[2]{0:T(128)} %pad_add_fusion.here, bf16[272,1024]{1,0:T(8,128)(2,1)} %pack.1.refs_0_, bf16[272,1024]{1,0:T(8,128)(2,1)} %copy-done.9, ...), custom_call_target="tpu_custom_call" | custom-call | flops 1200000000 | bytes 6000000 | tf_op jit(solution)/shard_map/dispatch_123/pallas_call | solution.py:192
  27.8 1.6 %collective-permute-start.3 = (bf16[3,320,1024]{2,1,0:T(8,128)(2,1)}, bf16[3,320,1024]{2,1,0:T(8,128)(2,1)S(1)}, u32[]{:S(2)}, u32[]{:S(2)}) collective-permute-start(bf16[3,320,1024]{2,1,0:T(8,128)(2,1)} %get-tuple-element.85), channel_id=1, source_target_pairs={{0,1},{1,2},{2,3},{3,0},{4,5},{5,6},{6,7},{7,4},{8,9},{9,10},{10,1... | collective-permute-start | bytes 5898248 | tf_op jit(solution)/shard_map/ppermute | solution.py:55
  29.4 1.7 %collective-permute-start.4 = (bf16[3,320,1024]{2,1,0:T(8,128)(2,1)}, bf16[3,320,1024]{2,1,0:T(8,128)(2,1)S(1)}, u32[]{:S(2)}, u32[]{:S(2)}) collective-permute-start(bf16[3,320,1024]{2,1,0:T(8,128)(2,1)} %get-tuple-element.86), channel_id=1, source_target_pairs={{0,3},{1,0},{2,1},{3,2},{4,7},{5,4},{6,5},{7,6},{8,11},{9,8},{10,9... | collective-permute-start | bytes 5898248 | tf_op jit(solution)/shard_map/ppermute | solution.py:55
  31.1 3.4 %dispatch_0.1 = (bf16[2,320,1024]{2,1,0:T(8,128)(2,1)}, bf16[4,160,256]{2,1,0:T(8,128)(2,1)}) custom-call(s32[2]{0:T(128)} %pad_add_fusion.here, bf16[272,1024]{1,0:T(8,128)(2,1)} %pack.1.refs_0_, bf16[272,1024]{1,0:T(8,128)(2,1)} %copy-done.9, bf16[272,1024]{1,0:T(8,128)(2,1)} %copy-done.10, bf16[272,1024]{1,0:T(8,128)(2,1)} %copy-done.11), custom_call_target="tpu_custom_call" | custom-call | flops 400000000 | bytes 6000000 | tf_op jit(solution)/shard_map/dispatch_0/pallas_call | solution.py:192
  34.4 8.4 %forward_terms.3 = (bf16[2,1024,1280]{2,1,0:T(8,128)(2,1)}, bf16[2,512,1280]{2,1,0:T(8,128)(2,1)}, f32[2,1280,1024]{2,1,0:T(8,128)}) custom-call(s32[2]{0:T(128)} %pad_add_fusion.here, bf16[2,16,80,1024]{3,2,1,0:T(8,128)(2,1)} %bitcast.48, bf16[2,16,80,1024]{3,2,1,0:T(8,128)(2,1)} %bitcast.49, ...), custom_call_target="tpu_custom_call", output_to_operand_aliasing={{0}: (11, {}), {1}: (12, {}), {2}: (13, {})} | custom-call | flops 2700000000 | bytes 15000000 | tf_op jit(solution)/shard_map/forward_terms/pallas_call | solution.py:127
  42.9 6.7 %groups_0.1 = (bf16[2,1280,1024]{2,1,0:T(8,128)(2,1)}, bf16[2,1280,1024]{2,1,0:T(8,128)(2,1)}, bf16[2,320,1024]{2,1,0:T(8,128)(2,1)}) custom-call(bf16[2,320,1024]{2,1,0:T(8,128)(2,1)} %get-tuple-element.79.refs_0_, f32[2,1280,1024]{2,1,0:T(8,128)} %get-tuple-element.83.refs_1_.refs_2_, bf16[2,512,1024]{2,1,0:T(8,128)(2,1)} %refs_3_.5, ...), custom_call_target="tpu_custom_call" | custom-call | flops 2100000000 | bytes 15000000 | tf_op jit(solution)/shard_map/groups_0/pallas_call | solution.py:279
  49.6 4.3 %collective-permute-done.3.refs_0_ = bf16[3,320,1024]{2,1,0:T(8,128)(2,1)S(1)} collective-permute-done((bf16[3,320,1024]{2,1,0:T(8,128)(2,1)}, bf16[3,320,1024]{2,1,0:T(8,128)(2,1)S(1)}, u32[]{:S(2)}, u32[]{:S(2)}) %collective-permute-start.3) | collective-permute-done | bytes 1966112 | tf_op jit(solution)/shard_map/ppermute | solution.py:55
  57.6 1.9 %collective-permute-start.8 = (bf16[320,1024]{1,0:T(8,128)(2,1)}, bf16[320,1024]{1,0:T(8,128)(2,1)S(1)}, u32[]{:S(2)}, u32[]{:S(2)}) collective-permute-start(bf16[320,1024]{1,0:T(8,128)(2,1)} %slice_bitcast_fusion), channel_id=1, source_target_pairs={{0,3},{1,0},{2,1},{3,2},{4,7},{5,4},{6,5},{7,6},{8,11},{9,8},{10,9... | collective-permute-start | bytes 1966088 | tf_op jit(solution)/shard_map/ppermute | solution.py:55
  59.6 9.8 %groups_12.1 = (bf16[2,1280,1024]{2,1,0:T(8,128)(2,1)}, bf16[2,1280,1024]{2,1,0:T(8,128)(2,1)}, bf16[2,320,1024]{2,1,0:T(8,128)(2,1)}, bf16[2,320,1024]{2,1,0:T(8,128)(2,1)}) custom-call(bf16[3,320,1024]{2,1,0:T(8,128)(2,1)} %copy-done, bf16[3,320,1024]{2,1,0:T(8,128)(2,1)} %copy-done.1, ...), custom_call_target="tpu_custom_call", output_to_operand_aliasing={{0}: (6, {}), {1}: (7, {})} | custom-call | flops 4200000000 | bytes 24000000 | tf_op jit(solution)/shard_map/groups_12/pallas_call | solution.py:279
  69.5 3.1 %collective-permute-start.6 = (bf16[2,320,1024]{2,1,0:T(8,128)(2,1)}, bf16[2,320,1024]{2,1,0:T(8,128)(2,1)S(1)}, u32[]{:S(2)}, u32[]{:S(2)}) collective-permute-start(bf16[2,320,1024]{2,1,0:T(8,128)(2,1)} %get-tuple-element.93), channel_id=1, source_target_pairs={{0,3},{1,0},{2,1},{3,2},{4,7},{5,4},{6,5},{7,6},{8,11},{9,8},{10,9... | collective-permute-start | bytes 3932168 | tf_op jit(solution)/shard_map/ppermute | solution.py:55
  73.7 6.8 %groups_3.1 = (bf16[2,1280,1024]{2,1,0:T(8,128)(2,1)}, bf16[2,1280,1024]{2,1,0:T(8,128)(2,1)}, bf16[320,1024]{1,0:T(8,128)(2,1)}, bf16[320,1024]{1,0:T(8,128)(2,1)}) custom-call(bf16[320,1024]{1,0:T(8,128)(2,1)} %copy-done.6, bf16[320,1024]{1,0:T(8,128)(2,1)} %copy-done.7, ...), custom_call_target="tpu_custom_call", output_to_operand_aliasing={{0}: (6, {}), {1}: (7, {})} | custom-call | flops 2100000000 | bytes 15000000 | tf_op jit(solution)/shard_map/groups_3/pallas_call | solution.py:279
  80.6 3.2 %collective-permute-start.10 = (bf16[320,1024]{1,0:T(8,128)(2,1)}, bf16[320,1024]{1,0:T(8,128)(2,1)}, u32[]{:S(2)}, u32[]{:S(2)}) collective-permute-start(bf16[320,1024]{1,0:T(8,128)(2,1)} %get-tuple-element.97), channel_id=1, source_target_pairs={{0,3},{1,0},{2,1},{3,2},{4,7},{5,4},{6,5},{7,6},{8,11},{9,8},{10,9... | collective-permute-start | bytes 1966088 | tf_op jit(solution)/shard_map/ppermute | solution.py:55
  83.8 13.4 %gate_up_grads.1 = (bf16[4,2,2,128,512]{4,3,2,1,0:T(8,128)(2,1)}, bf16[4,2,128,512]{3,2,1,0:T(8,128)(2,1)}, bf16[4,2,128,512]{3,2,1,0:T(8,128)(2,1)}, bf16[2,1024,512]{2,1,0:T(8,128)(2,1)}, bf16[2,1024,512]{2,1,0:T(8,128)(2,1)}) custom-call(s32[2]{0:T(128)} %pad_add_fusion.here, bf16[2,1024,1280]{2,1,0:T(8,128)(2,1)} %get-tuple-element.99.xt, ...), custom_call_target="tpu_custom_call" | custom-call | flops 5400000000 | bytes 22000000 | tf_op jit(solution)/shard_map/gate_up_grads/pallas_call | solution.py:382
  97.8 3.2 %collective-permute-start.12 = (bf16[320,1024]{1,0:T(8,128)(2,1)}, bf16[320,1024]{1,0:T(8,128)(2,1)}, u32[]{:S(2)}, u32[]{:S(2)}) collective-permute-start(bf16[320,1024]{1,0:T(8,128)(2,1)} %collective-permute-done.10), channel_id=1, source_target_pairs={{0,3},{1,0},{2,1},{3,2},{4,7},{5,4},{6,5},{7,6},{8,11},{9,8},{10,9... | collective-permute-start | bytes 1966088 | tf_op jit(solution)/shard_map/ppermute | solution.py:55
  101.0 9.0 %down_grads.1 = (bf16[4,2,512,128]{3,2,1,0:T(8,128)(2,1)}, bf16[4,2,512,128]{3,2,1,0:T(8,128)(2,1)}, bf16[2,512,1024]{2,1,0:T(8,128)(2,1)}) custom-call(s32[2]{0:T(128)} %pad_add_fusion.here, bf16[2,512,1280]{2,1,0:T(8,128)(2,1)} %get-tuple-element.108.ht, bf16[2,1280,1024]{2,1,0:T(8,128)(2,1)} %get-tuple-element.109.cot, bf16[2,512,1024]{2,1,0:T(8,128)(2,1)} %bitcast.66), custom_call_target="tpu_custom_call" | custom-call | flops 2700000000 | bytes 14000000 | tf_op jit(solution)/shard_map/down_grads/pallas_call | solution.py:425
  111.4 1.5 collective-permute-start.18
  113.4 5.8 %combine.1 = (bf16[256,1024]{1,0:T(8,128)(2,1)}, bf16[256,1024]{1,0:T(8,128)(2,1)}, bf16[256,1024]{1,0:T(8,128)(2,1)}, bf16[256,1024]{1,0:T(8,128)(2,1)}) custom-call(bf16[2,320,1024]{2,1,0:T(8,128)(2,1)} %get-tuple-element.84.refs_0_, bf16[2,320,1024]{2,1,0:T(8,128)(2,1)} %copy-done.3, bf16[2,320,1024]{2,1,0:T(8,128)(2,1)} %copy-done.4, ...), custom_call_target="tpu_custom_call" | custom-call | flops 1400000000 | bytes 9000000 | tf_op jit(solution)/shard_map/combine/pallas_call | solution.py:338
  120.1 2.3 %collective-permute-start.16 = (bf16[256,1024]{1,0:T(8,128)(2,1)}, bf16[256,1024]{1,0:T(8,128)(2,1)S(1)}, u32[]{:S(2)}, u32[]{:S(2)}) collective-permute-start(bf16[256,1024]{1,0:T(8,128)(2,1)} %get-tuple-element.121), channel_id=1, source_target_pairs={{0,12},{1,13},{2,14},{3,15},{4,0},{5,1},{6,2},{7,3},{8,4},{9,5},{1... | collective-permute-start | bytes 1572872 | tf_op jit(solution)/shard_map/ppermute | solution.py:55
  122.9 3.5 %collective-permute-done.18 = bf16[2,2,2,128,512]{4,3,2,1,0:T(8,128)(2,1)S(1)} collective-permute-done((bf16[2,2,2,128,512]{4,3,2,1,0:T(8,128)(2,1)}, bf16[2,2,2,128,512]{4,3,2,1,0:T(8,128)(2,1)S(1)}, u32[]{:S(2)}, u32[]{:S(2)}) %collective-permute-start.18) | collective-permute-done | bytes 1048608 | tf_op jit(solution)/shard_map/ppermute | solution.py:59
  126.5 1.6 %collective-permute-start.21 = (bf16[2,2,512,128]{3,2,1,0:T(8,128)(2,1)S(1)}, bf16[2,2,512,128]{3,2,1,0:T(8,128)(2,1)S(1)}, u32[]{:S(2)}, u32[]{:S(2)}) collective-permute-start(bf16[2,2,512,128]{3,2,1,0:T(8,128)(2,1)S(1)} %add_convert_fusion.2), channel_id=1, source_target_pairs={{0,32},{16,112},{32,0},{48,80},{64,96},{80,48},{96,64},{112,16},{1... | collective-permute-start | bytes 1572872 | tf_op jit(solution)/shard_map/ppermute | solution.py:59
  128.3 2.2 %collective-permute-start.19 = (bf16[2,2,128,512]{3,2,1,0:T(8,128)(2,1)S(1)}, bf16[2,2,128,512]{3,2,1,0:T(8,128)(2,1)S(1)}, u32[]{:S(2)}, u32[]{:S(2)}) collective-permute-start(bf16[2,2,128,512]{3,2,1,0:T(8,128)(2,1)S(1)} %fusion.3), channel_id=1, source_target_pairs={{0,96},{16,48},{32,64},{48,16},{64,32},{80,112},{96,0},{112,80},{1... | collective-permute-start | bytes 1572872 | tf_op jit(solution)/shard_map/ppermute | solution.py:59
  130.5 4.6 %collective-permute-done.16 = bf16[256,1024]{1,0:T(8,128)(2,1)S(1)} collective-permute-done((bf16[256,1024]{1,0:T(8,128)(2,1)}, bf16[256,1024]{1,0:T(8,128)(2,1)S(1)}, u32[]{:S(2)}, u32[]{:S(2)}) %collective-permute-start.16) | collective-permute-done | bytes 524320 | tf_op jit(solution)/shard_map/ppermute | solution.py:55
  135.9 4.1 %collective-permute-done.21 = bf16[2,2,512,128]{3,2,1,0:T(8,128)(2,1)S(1)} collective-permute-done((bf16[2,2,512,128]{3,2,1,0:T(8,128)(2,1)S(1)}, bf16[2,2,512,128]{3,2,1,0:T(8,128)(2,1)S(1)}, u32[]{:S(2)}, u32[]{:S(2)}) %collective-permute-start.21) | collective-permute-done | bytes 524320 | tf_op jit(solution)/shard_map/ppermute | solution.py:59
  140.1 3.6 %collective-permute-start.22 = (bf16[2,512,128]{2,1,0:T(8,128)(2,1)S(1)}, bf16[2,512,128]{2,1,0:T(8,128)(2,1)S(1)}, u32[]{:S(2)}, u32[]{:S(2)}) collective-permute-start(bf16[2,512,128]{2,1,0:T(8,128)(2,1)S(1)} %fusion.5), channel_id=1, source_target_pairs={{0,96},{16,48},{32,64},{48,16},{64,32},{80,112},{96,0},{112,80},{1... | collective-permute-start | bytes 786440 | tf_op jit(solution)/shard_map/ppermute | solution.py:59
  144.1 4.1 %collective-permute-done.22 = bf16[2,512,128]{2,1,0:T(8,128)(2,1)S(1)} collective-permute-done((bf16[2,512,128]{2,1,0:T(8,128)(2,1)S(1)}, bf16[2,512,128]{2,1,0:T(8,128)(2,1)S(1)}, u32[]{:S(2)}, u32[]{:S(2)}) %collective-permute-start.22) | collective-permute-done | bytes 262176 | tf_op jit(solution)/shard_map/ppermute | solution.py:59
  (62 shorter events, 14.9 us)
Async XLA Ops:
  2.6 15.0 %collective-permute-start = (bf16[272,1024]{1,0:T(8,128)(2,1)}, bf16[272,1024]{1,0:T(8,128)(2,1)S(1)}, u32[]{:S(2)}, u32[]{:S(2)}) collective-permute-start(bf16[272,1024]{1,0:T(8,128)(2,1)} %pack.1.refs_0_), channel_id=1, source_target_pairs={{0,4},{1,5},{2,6},{3,7},{4,8},{5,9},{6,10},{7,11},{8,12},{9,13},{1... | collective-permute-start | bytes 1671176 | tf_op jit(solution)/shard_map/ppermute | solution.py:55
  4.6 15.5 %collective-permute-start.1 = (bf16[272,1024]{1,0:T(8,128)(2,1)}, bf16[272,1024]{1,0:T(8,128)(2,1)S(1)}, u32[]{:S(2)}, u32[]{:S(2)}) collective-permute-start(bf16[272,1024]{1,0:T(8,128)(2,1)} %pack.1.refs_0_), channel_id=1, source_target_pairs={{0,12},{1,13},{2,14},{3,15},{4,0},{5,1},{6,2},{7,3},{8,4},{9,5},{1... | collective-permute-start | bytes 1671176 | tf_op jit(solution)/shard_map/ppermute | solution.py:55
  6.7 15.1 %collective-permute-start.2 = (bf16[272,1024]{1,0:T(8,128)(2,1)}, bf16[272,1024]{1,0:T(8,128)(2,1)S(1)}, u32[]{:S(2)}, u32[]{:S(2)}) collective-permute-start(bf16[272,1024]{1,0:T(8,128)(2,1)} %pack.1.refs_0_), channel_id=1, source_target_pairs={{0,8},{1,9},{2,10},{3,11},{4,12},{5,13},{6,14},{7,15},{8,0},{9,1},... | collective-permute-start | bytes 1671176 | tf_op jit(solution)/shard_map/ppermute | solution.py:55
  17.5 4.3 %copy-start.9 = (bf16[272,1024]{1,0:T(8,128)(2,1)}, bf16[272,1024]{1,0:T(8,128)(2,1)S(1)}, u32[]{:S(2)}) copy-start(bf16[272,1024]{1,0:T(8,128)(2,1)S(1)} %collective-permute-done.refs_1_) | copy-start | bytes 1671172
  20.1 1.8 %copy-start.10 = (bf16[272,1024]{1,0:T(8,128)(2,1)}, bf16[272,1024]{1,0:T(8,128)(2,1)S(1)}, u32[]{:S(2)}) copy-start(bf16[272,1024]{1,0:T(8,128)(2,1)S(1)} %collective-permute-done.1.refs_2_) | copy-start | bytes 1671172
  27.8 26.1 %collective-permute-start.3 = (bf16[3,320,1024]{2,1,0:T(8,128)(2,1)}, bf16[3,320,1024]{2,1,0:T(8,128)(2,1)S(1)}, u32[]{:S(2)}, u32[]{:S(2)}) collective-permute-start(bf16[3,320,1024]{2,1,0:T(8,128)(2,1)} %get-tuple-element.85), channel_id=1, source_target_pairs={{0,1},{1,2},{2,3},{3,0},{4,5},{5,6},{6,7},{7,4},{8,9},{9,10},{10,1... | collective-permute-start | bytes 5898248 | tf_op jit(solution)/shard_map/ppermute | solution.py:55
  29.4 24.8 %collective-permute-start.4 = (bf16[3,320,1024]{2,1,0:T(8,128)(2,1)}, bf16[3,320,1024]{2,1,0:T(8,128)(2,1)S(1)}, u32[]{:S(2)}, u32[]{:S(2)}) collective-permute-start(bf16[3,320,1024]{2,1,0:T(8,128)(2,1)} %get-tuple-element.86), channel_id=1, source_target_pairs={{0,3},{1,0},{2,1},{3,2},{4,7},{5,4},{6,5},{7,6},{8,11},{9,8},{10,9... | collective-permute-start | bytes 5898248 | tf_op jit(solution)/shard_map/ppermute | solution.py:55
  53.9 5.7 %copy-start = (bf16[3,320,1024]{2,1,0:T(8,128)(2,1)}, bf16[3,320,1024]{2,1,0:T(8,128)(2,1)S(1)}, u32[]{:S(2)}) copy-start(bf16[3,320,1024]{2,1,0:T(8,128)(2,1)S(1)} %collective-permute-done.3.refs_0_) | copy-start | bytes 5898244
  54.2 5.3 %copy-start.1 = (bf16[3,320,1024]{2,1,0:T(8,128)(2,1)}, bf16[3,320,1024]{2,1,0:T(8,128)(2,1)S(1)}, u32[]{:S(2)}) copy-start(bf16[3,320,1024]{2,1,0:T(8,128)(2,1)S(1)} %collective-permute-done.4.refs_1_) | copy-start | bytes 5898244
  55.4 17.2 %collective-permute-start.7 = (bf16[320,1024]{1,0:T(8,128)(2,1)}, bf16[320,1024]{1,0:T(8,128)(2,1)S(1)}, u32[]{:S(2)}, u32[]{:S(2)}) collective-permute-start(bf16[320,1024]{1,0:T(8,128)(2,1)} %slice_bitcast_fusion.1), channel_id=1, source_target_pairs={{0,1},{1,2},{2,3},{3,0},{4,5},{5,6},{6,7},{7,4},{8,9},{9,10},{10,1... | collective-permute-start | bytes 1966088 | tf_op jit(solution)/shard_map/ppermute | solution.py:55
  57.6 15.0 %collective-permute-start.8 = (bf16[320,1024]{1,0:T(8,128)(2,1)}, bf16[320,1024]{1,0:T(8,128)(2,1)S(1)}, u32[]{:S(2)}, u32[]{:S(2)}) collective-permute-start(bf16[320,1024]{1,0:T(8,128)(2,1)} %slice_bitcast_fusion), channel_id=1, source_target_pairs={{0,3},{1,0},{2,1},{3,2},{4,7},{5,4},{6,5},{7,6},{8,11},{9,8},{10,9... | collective-permute-start | bytes 1966088 | tf_op jit(solution)/shard_map/ppermute | solution.py:55
  69.4 27.8 %collective-permute-start.5 = (bf16[2,320,1024]{2,1,0:T(8,128)(2,1)}, bf16[2,320,1024]{2,1,0:T(8,128)(2,1)S(1)}, u32[]{:S(2)}, u32[]{:S(2)}) collective-permute-start(bf16[2,320,1024]{2,1,0:T(8,128)(2,1)} %get-tuple-element.92), channel_id=1, source_target_pairs={{0,1},{1,2},{2,3},{3,0},{4,5},{5,6},{6,7},{7,4},{8,9},{9,10},{10,1... | collective-permute-start | bytes 3932168 | tf_op jit(solution)/shard_map/ppermute | solution.py:55
  69.5 28.2 %collective-permute-start.6 = (bf16[2,320,1024]{2,1,0:T(8,128)(2,1)}, bf16[2,320,1024]{2,1,0:T(8,128)(2,1)S(1)}, u32[]{:S(2)}, u32[]{:S(2)}) collective-permute-start(bf16[2,320,1024]{2,1,0:T(8,128)(2,1)} %get-tuple-element.93), channel_id=1, source_target_pairs={{0,3},{1,0},{2,1},{3,2},{4,7},{5,4},{6,5},{7,6},{8,11},{9,8},{10,9... | collective-permute-start | bytes 3932168 | tf_op jit(solution)/shard_map/ppermute | solution.py:55
  80.5 17.2 %collective-permute-start.9 = (bf16[320,1024]{1,0:T(8,128)(2,1)}, bf16[320,1024]{1,0:T(8,128)(2,1)}, u32[]{:S(2)}, u32[]{:S(2)}) collective-permute-start(bf16[320,1024]{1,0:T(8,128)(2,1)} %get-tuple-element.96), channel_id=1, source_target_pairs={{0,1},{1,2},{2,3},{3,0},{4,5},{5,6},{6,7},{7,4},{8,9},{9,10},{10,1... | collective-permute-start | bytes 1966088 | tf_op jit(solution)/shard_map/ppermute | solution.py:55
  80.6 17.1 %collective-permute-start.10 = (bf16[320,1024]{1,0:T(8,128)(2,1)}, bf16[320,1024]{1,0:T(8,128)(2,1)}, u32[]{:S(2)}, u32[]{:S(2)}) collective-permute-start(bf16[320,1024]{1,0:T(8,128)(2,1)} %get-tuple-element.97), channel_id=1, source_target_pairs={{0,3},{1,0},{2,1},{3,2},{4,7},{5,4},{6,5},{7,6},{8,11},{9,8},{10,9... | collective-permute-start | bytes 1966088 | tf_op jit(solution)/shard_map/ppermute | solution.py:55
  97.2 12.9 %collective-permute-start.13 = (bf16[4,2,128,512]{3,2,1,0:T(8,128)(2,1)}, bf16[4,2,128,512]{3,2,1,0:T(8,128)(2,1)S(1)}, u32[]{:S(2)}, u32[]{:S(2)}) collective-permute-start(bf16[4,2,128,512]{3,2,1,0:T(8,128)(2,1)} %get-tuple-element.106), channel_id=1, source_target_pairs={{0,16},{16,0},{32,48},{48,32},{64,80},{80,64},{96,112},{112,96},{1... | collective-permute-start | bytes 3145736 | tf_op jit(solution)/shard_map/ppermute | solution.py:59
  97.2 12.8 %copy-start.3 = (bf16[2,320,1024]{2,1,0:T(8,128)(2,1)}, bf16[2,320,1024]{2,1,0:T(8,128)(2,1)S(1)}, u32[]{:S(2)}) copy-start(bf16[2,320,1024]{2,1,0:T(8,128)(2,1)S(1)} %collective-permute-done.5.refs_1_) | copy-start | bytes 3932164
  97.2 12.9 %collective-permute-start.14 = (bf16[4,2,128,512]{3,2,1,0:T(8,128)(2,1)}, bf16[4,2,128,512]{3,2,1,0:T(8,128)(2,1)S(1)}, u32[]{:S(2)}, u32[]{:S(2)}) collective-permute-start(bf16[4,2,128,512]{3,2,1,0:T(8,128)(2,1)} %get-tuple-element.107), channel_id=1, source_target_pairs={{0,16},{16,0},{32,48},{48,32},{64,80},{80,64},{96,112},{112,96},{1... | collective-permute-start | bytes 3145736 | tf_op jit(solution)/shard_map/ppermute | solution.py:59
  97.7 12.3 %copy-start.4 = (bf16[2,320,1024]{2,1,0:T(8,128)(2,1)}, bf16[2,320,1024]{2,1,0:T(8,128)(2,1)S(1)}, u32[]{:S(2)}) copy-start(bf16[2,320,1024]{2,1,0:T(8,128)(2,1)S(1)} %collective-permute-done.6.refs_2_) | copy-start | bytes 3932164
  97.7 12.4 %collective-permute-start.11 = (bf16[320,1024]{1,0:T(8,128)(2,1)}, bf16[320,1024]{1,0:T(8,128)(2,1)S(1)}, u32[]{:S(2)}, u32[]{:S(2)}) collective-permute-start(bf16[320,1024]{1,0:T(8,128)(2,1)} %collective-permute-done.9), channel_id=1, source_target_pairs={{0,1},{1,2},{2,3},{3,0},{4,5},{5,6},{6,7},{7,4},{8,9},{9,10},{10,1... | collective-permute-start | bytes 1966088 | tf_op jit(solution)/shard_map/ppermute | solution.py:55
  97.8 12.3 %collective-permute-start.12 = (bf16[320,1024]{1,0:T(8,128)(2,1)}, bf16[320,1024]{1,0:T(8,128)(2,1)}, u32[]{:S(2)}, u32[]{:S(2)}) collective-permute-start(bf16[320,1024]{1,0:T(8,128)(2,1)} %collective-permute-done.10), channel_id=1, source_target_pairs={{0,3},{1,0},{2,1},{3,2},{4,7},{5,4},{6,5},{7,6},{8,11},{9,8},{10,9... | collective-permute-start | bytes 1966088 | tf_op jit(solution)/shard_map/ppermute | solution.py:55
  101.0 9.1 %copy-start.2 = (bf16[4,2,2,128,512]{4,3,2,1,0:T(8,128)(2,1)S(1)}, bf16[4,2,2,128,512]{4,3,2,1,0:T(8,128)(2,1)}, u32[]{:S(2)}) copy-start(bf16[4,2,2,128,512]{4,3,2,1,0:T(8,128)(2,1)} %get-tuple-element.123) | copy-start | bytes 6291460
  111.4 15.0 %collective-permute-start.18 = (bf16[2,2,2,128,512]{4,3,2,1,0:T(8,128)(2,1)}, bf16[2,2,2,128,512]{4,3,2,1,0:T(8,128)(2,1)S(1)}, u32[]{:S(2)}, u32[]{:S(2)}) collective-permute-start(bf16[2,2,2,128,512]{4,3,2,1,0:T(8,128)(2,1)} %add_convert_fusion), channel_id=1, source_target_pairs={{0,32},{16,112},{32,0},{48,80},{64,96},{80,48},{96,64},{112,16},{1... | collective-permute-start | bytes 3145736 | tf_op jit(solution)/shard_map/ppermute | solution.py:59
  112.9 13.5 %collective-permute-start.20 = (bf16[4,2,512,128]{3,2,1,0:T(8,128)(2,1)}, bf16[4,2,512,128]{3,2,1,0:T(8,128)(2,1)S(1)}, u32[]{:S(2)}, u32[]{:S(2)}) collective-permute-start(bf16[4,2,512,128]{3,2,1,0:T(8,128)(2,1)} %get-tuple-element.128), channel_id=1, source_target_pairs={{0,16},{16,0},{32,48},{48,32},{64,80},{80,64},{96,112},{112,96},{1... | collective-permute-start | bytes 3145736 | tf_op jit(solution)/shard_map/ppermute | solution.py:59
  113.4 13.0 %copy-start.5 = (bf16[4,2,512,128]{3,2,1,0:T(8,128)(2,1)S(1)}, bf16[4,2,512,128]{3,2,1,0:T(8,128)(2,1)}, u32[]{:S(2)}) copy-start(bf16[4,2,512,128]{3,2,1,0:T(8,128)(2,1)} %get-tuple-element.127) | copy-start | bytes 3145732
  119.2 11.4 %collective-permute-start.15 = (bf16[256,1024]{1,0:T(8,128)(2,1)}, bf16[256,1024]{1,0:T(8,128)(2,1)S(1)}, u32[]{:S(2)}, u32[]{:S(2)}) collective-permute-start(bf16[256,1024]{1,0:T(8,128)(2,1)} %get-tuple-element.120), channel_id=1, source_target_pairs={{0,4},{1,5},{2,6},{3,7},{4,8},{5,9},{6,10},{7,11},{8,12},{9,13},{1... | collective-permute-start | bytes 1572872 | tf_op jit(solution)/shard_map/ppermute | solution.py:55
  120.1 15.0 %collective-permute-start.16 = (bf16[256,1024]{1,0:T(8,128)(2,1)}, bf16[256,1024]{1,0:T(8,128)(2,1)S(1)}, u32[]{:S(2)}, u32[]{:S(2)}) collective-permute-start(bf16[256,1024]{1,0:T(8,128)(2,1)} %get-tuple-element.121), channel_id=1, source_target_pairs={{0,12},{1,13},{2,14},{3,15},{4,0},{5,1},{6,2},{7,3},{8,4},{9,5},{1... | collective-permute-start | bytes 1572872 | tf_op jit(solution)/shard_map/ppermute | solution.py:55
  122.5 13.5 %collective-permute-start.17 = (bf16[256,1024]{1,0:T(8,128)(2,1)}, bf16[256,1024]{1,0:T(8,128)(2,1)S(1)}, u32[]{:S(2)}, u32[]{:S(2)}) collective-permute-start(bf16[256,1024]{1,0:T(8,128)(2,1)} %get-tuple-element.122), channel_id=1, source_target_pairs={{0,8},{1,9},{2,10},{3,11},{4,12},{5,13},{6,14},{7,15},{8,0},{9,1},... | collective-permute-start | bytes 1572872 | tf_op jit(solution)/shard_map/ppermute | solution.py:55
  126.5 13.5 %collective-permute-start.21 = (bf16[2,2,512,128]{3,2,1,0:T(8,128)(2,1)S(1)}, bf16[2,2,512,128]{3,2,1,0:T(8,128)(2,1)S(1)}, u32[]{:S(2)}, u32[]{:S(2)}) collective-permute-start(bf16[2,2,512,128]{3,2,1,0:T(8,128)(2,1)S(1)} %add_convert_fusion.2), channel_id=1, source_target_pairs={{0,32},{16,112},{32,0},{48,80},{64,96},{80,48},{96,64},{112,16},{1... | collective-permute-start | bytes 1572872 | tf_op jit(solution)/shard_map/ppermute | solution.py:59
  128.3 15.4 %collective-permute-start.19 = (bf16[2,2,128,512]{3,2,1,0:T(8,128)(2,1)S(1)}, bf16[2,2,128,512]{3,2,1,0:T(8,128)(2,1)S(1)}, u32[]{:S(2)}, u32[]{:S(2)}) collective-permute-start(bf16[2,2,128,512]{3,2,1,0:T(8,128)(2,1)S(1)} %fusion.3), channel_id=1, source_target_pairs={{0,96},{16,48},{32,64},{48,16},{64,32},{80,112},{96,0},{112,80},{1... | collective-permute-start | bytes 1572872 | tf_op jit(solution)/shard_map/ppermute | solution.py:59
  140.1 8.0 %collective-permute-start.22 = (bf16[2,512,128]{2,1,0:T(8,128)(2,1)S(1)}, bf16[2,512,128]{2,1,0:T(8,128)(2,1)S(1)}, u32[]{:S(2)}, u32[]{:S(2)}) collective-permute-start(bf16[2,512,128]{2,1,0:T(8,128)(2,1)S(1)} %fusion.5), channel_id=1, source_target_pairs={{0,96},{16,48},{32,64},{48,16},{64,32},{80,112},{96,0},{112,80},{1... | collective-permute-start | bytes 786440 | tf_op jit(solution)/shard_map/ppermute | solution.py:59
  144.1 6.0 %copy-start.12 = (bf16[256,1024]{1,0:T(8,128)(2,1)S(1)}, bf16[256,1024]{1,0:T(8,128)(2,1)}, u32[]{:S(2)}) copy-start(bf16[256,1024]{1,0:T(8,128)(2,1)} %get-tuple-element.130) | copy-start | bytes 1572868
  (4 other events, 4.0 us)
